TPU v7x, 32 devices: a whole 2x2x4 slice. The times are simulated.
32 devices in a mesh: slab: 4 (over y, x), coil: 8 (over z, core).
Axes of the slice: x: 2, y: 2, z: 4, core: 2. Of those that a mesh axis runs over, the one named last changes fastest.
Arguments:
- kspace: bfloat16 [4, 8, 2, 512, 512], P('slab', 'coil'), may hold values from -6 to 6
- sensitivity: bfloat16 [4, 8, 2, 512, 512], P('slab', 'coil'), may hold values from -2 to 2
- sampling: int32 [4, 512, 512], P('slab'), may hold values 0 or 1
Outputs:
- estimate: float32 [4, 2, 512, 512], P('slab', None, 'coil')
All inputs are finite; a program needn't handle non-finite values. No bound on the sum of `sampling` on one device may be relied on, other than what follows from the above.
Results may differ from a plain program's by a relative error of at most 0.005.
Values sent between devices are 32-bit elements; how exact they have to be, the bound alone decides.
No kernel may reach another device: no remote copies, remote signals or barrier semaphores. Data moves between devices by JAX's collectives and lax.ppermute only.
A program may use at most 128 MiB of HBM per device.

v0:
```python
from functools import partial
import math

import jax
import jax.numpy as jnp
from jax import lax
from jax.sharding import PartitionSpec as P

STEP_SIZE = 0.25
TV_WEIGHT = 0.5
TV_SMOOTH = 0.25


def padded_2(block, sides, width):
    for axis, dim in sides:
        count = lax.axis_size(axis)
        forward = [(i, i + 1) for i in range(count - 1)]
        forward.append((count - 1, 0))
        backward = [(target, source) for source, target in forward]
        low = lax.ppermute(
            lax.slice_in_dim(block, block.shape[dim] - width, None, axis=dim), axis, forward
        )
        high = lax.ppermute(lax.slice_in_dim(block, 0, width, axis=dim), axis, backward)
        block = jnp.concatenate([low, block, high], axis=dim)
    return block


def dft_tables(length):
    indices = jnp.arange(length, dtype=jnp.int32)
    products = indices[:, None] * indices[None, :] % length
    angles = products.astype(jnp.float32) * (2.0 * math.pi / length)
    factor = 1.0 / math.sqrt(length)
    return (
        (jnp.cos(angles) * factor).astype(jnp.bfloat16),
        (-jnp.sin(angles) * factor).astype(jnp.bfloat16),
    )


def right_table(length, sign):
    cosine, sine = dft_tables(length)
    signed = sine if sign > 0 else -sine
    return jnp.stack(
        [jnp.stack([cosine, signed], axis=1), jnp.stack([-signed, cosine], axis=1)], axis=0
    )


def left_table(length, sign):
    cosine, sine = dft_tables(length)
    signed = sine if sign > 0 else -sine
    return jnp.stack(
        [jnp.stack([cosine, -signed], axis=1), jnp.stack([signed, cosine], axis=1)], axis=0
    )


def all_tables(rows, cols):
    return (left_table(rows, 1), left_table(rows, -1), right_table(cols, 1), right_table(cols, -1))


def apply_right(pair, table):
    return jnp.einsum("pyz,pzqw->qyw", pair, table, preferred_element_type=jnp.float32)


def apply_left(table, pair):
    return jnp.einsum("qypk,pkz->qyz", table, pair, preferred_element_type=jnp.float32)


def coil_adjoint(tables, resid, sens_pair):
    row_fwd, row_adj, col_fwd, col_adj = tables
    upper = apply_left(row_adj, resid).astype(jnp.bfloat16)
    back = apply_right(upper, col_adj)
    sens_real = sens_pair[0].astype(jnp.float32)
    sens_imag = sens_pair[1].astype(jnp.float32)
    return jnp.stack(
        [sens_real * back[0] + sens_imag * back[1], sens_real * back[1] - sens_imag * back[0]]
    )


def coil_zero_filled(tables, inputs):
    sens_pair, kspace_pair, sampling_slice = inputs
    measured = kspace_pair * sampling_slice.astype(jnp.bfloat16)[None]
    return coil_adjoint(tables, measured, sens_pair)


def coil_gradient(tables, inputs):
    sens_pair, kspace_pair, sampling_slice, estimate_pair = inputs
    row_fwd, row_adj, col_fwd, col_adj = tables
    sens_real = sens_pair[0].astype(jnp.float32)
    sens_imag = sens_pair[1].astype(jnp.float32)
    coil_pair = jnp.stack(
        [
            sens_real * estimate_pair[0] - sens_imag * estimate_pair[1],
            sens_real * estimate_pair[1] + sens_imag * estimate_pair[0],
        ]
    ).astype(jnp.bfloat16)
    middle = apply_right(coil_pair, col_fwd).astype(jnp.bfloat16)
    freq = apply_left(row_fwd, middle)
    weight = sampling_slice.astype(jnp.float32)[None]
    resid = (weight * (freq - kspace_pair.astype(jnp.float32))).astype(jnp.bfloat16)
    return coil_adjoint(tables, resid, sens_pair)


def coil_sum(per_coil, sensitivity, kspace, sampling, extras):
    mapped = (sensitivity, kspace, sampling) + extras
    vmap_axes = (0, 0, None) + (None,) * len(extras)

    def one_slice(inputs):
        coil_terms = jax.vmap(per_coil, in_axes=(vmap_axes,))(inputs)
        return jnp.sum(coil_terms, axis=0)

    return lax.map(one_slice, mapped)


def tv_gradient(volume, padded):
    differences = [jnp.roll(volume, -1, axis=axis_id) - volume for axis_id in (0, 2, 3)]
    squares = (
        differences[0] * differences[0]
        + differences[1] * differences[1]
        + differences[2] * differences[2]
    )
    weights = lax.rsqrt(jnp.sum(squares, axis=1, keepdims=True) + TV_SMOOTH)
    result = jnp.zeros_like(volume)
    for axis_id, change in zip((0, 2, 3), differences):
        flux_term = weights * change
        result = result + (jnp.roll(flux_term, 1, axis=axis_id) - flux_term)
    for axis_id in padded:
        result = lax.slice_in_dim(result, 1, result.shape[axis_id] - 1, axis=axis_id)
    return result


def shards(kspace, sensitivity, sampling):
    tables = all_tables(sampling.shape[1], sampling.shape[2])
    zero_term = partial(coil_zero_filled, tables)
    grad_term = partial(coil_gradient, tables)
    initial = coil_sum(zero_term, sensitivity, kspace, sampling, ())
    owned_rows = lax.psum_scatter(initial, "coil", scatter_dimension=2, tiled=True)
    estimate = lax.all_gather(owned_rows, "coil", axis=2, tiled=True)
    coil_part = coil_sum(grad_term, sensitivity, kspace, sampling, (estimate,))
    gradient = lax.psum_scatter(coil_part, "coil", scatter_dimension=2, tiled=True)
    extended = padded_2(owned_rows, (("slab", 0), ("coil", 2)), 1)
    regular = tv_gradient(extended, (0, 2))
    owned_rows = owned_rows - STEP_SIZE * (gradient + TV_WEIGHT * regular)
    return owned_rows


def solution(mesh):
    placed = (
        P("slab", "coil", None, None, None),
        P("slab", "coil", None, None, None),
        P("slab", None, None),
    )
    return jax.shard_map(
        shards, mesh=mesh, in_specs=placed, out_specs=P("slab", None, "coil", None), check_vma=False
    )
```

profile of v0, /device:TPU:0, one launch (start us, length us, event | category | flops | bytes accessed | tf_op | source)
XLA Modules:
  0.0 234.0 jit_solution(11677870541979016497)
XLA Ops:
  6.5 4.4 %multiply_convert_fusion = (bf16[512,1,512]{2,0,1:T(8,128)(2,1)S(1)}, bf16[512,1,512]{2,0,1:T(8,128)(2,1)S(1)}) fusion(), kind=kLoop, calls=%fused_computation.56 | loop fusion | flops 4980736 | bytes 1048576 | tf_op jit(solution)/shard_map/convert_element_type | solution.py:35
  10.9 4.0 %fusion.39 = bf16[512,1,512]{2,0,1:T(8,128)(2,1)S(1)} fusion(), kind=kLoop, calls=%fused_computation.86 | loop fusion | flops 5242880 | bytes 524288 | tf_op jit(solution)/shard_map/neg | solution.py:49
  16.3 1.5 copy.32
  17.8 2.2 fusion.8
  20.0 4.9 %convolution_bitcast_fusion.1 = f32[1,2,512,512]{2,3,1,0:T(8,128)S(1)} fusion(bf16[1,1,2,512,512]{4,3,2,1,0:T(8,128)(2,1)} %param.3, bf16[1,512,2,512]{3,1,2,0:T(8,128)(2,1)} %get-tuple-element.68, bf16[1,512,2,512]{3,1,2,0:T(8,128)(2,1)} %get-tuple-element.75, bf16[1,512,2,512]{3,1,2,0:T(8,128)(2,1)} %get-tuple-element.76, ...), kind=kOutput, calls=%fused_computation.23 | convolution fusion | flops 2150629376 | bytes 7864320 | tf_op jit(solution)/shard_map/while/body/eval_jaxpr/vmap(pyz,pzqw->qyw)/dot_general | solution.py:60
  25.5 2.4 %copy.34 = f32[1,2,512,512]{3,1,0,2:T(2,128)} copy(f32[1,2,512,512]{2,3,1,0:T(8,128)S(1)} %maximum_bitcast_fusion) | data formatting | bytes 4194304 | tf_op jit(solution)/shard_map/while/body/eval_jaxpr/vmap()/transpose | solution.py:107
  29.8 65.9 %all-reduce.5.cloned.1.call-done = f32[1,2,512,512]{3,1,0,2:T(2,128)} async-done(((f32[1,2,512,512]{3,1,0,2:T(2,128)}), f32[1,2,512,512]{3,1,0,2:T(2,128)}) %all-reduce.5.cloned.1.call-update) | async-done | bytes 2097168
  95.7 1.7 constant_dynamic-slice_fusion.1
  98.4 1.5 collective-permute-start
  101.4 7.2 %collective-permute-done = f32[1,2,64,512]{3,2,1,0:T(8,128)S(1)} collective-permute-done((f32[1,2,64,512]{3,2,1,0:T(8,128)S(1)}, f32[1,2,64,512]{3,2,1,0:T(8,128)S(1)}, u32[]{:S(2)}, u32[]{:S(2)}) %collective-permute-start) | collective-permute-done | bytes 262176 | tf_op jit(solution)/shard_map/ppermute | solution.py:20
  109.7 2.0 collective-permute-done.1
  111.7 14.6 %all-gather.2.cloned.1.call-done = f32[1,2,512,512]{3,1,0,2:T(2,128)} async-done(((f32[1,2,64,512]{3,1,0,2:T(2,128)}), f32[1,2,512,512]{3,1,0,2:T(2,128)}) %all-gather.2.cloned.1.call-update) | async-done | bytes 2097168 | tf_op jit(solution)/shard_map/all_gather | solution.py:136
  126.3 5.3 %fusion.46 = (f32[1,1,512,512]{3,1,0,2:T(1,128)}, f32[1,1,512,512]{3,1,0,2:T(1,128)}) fusion(f32[1,2,512,512]{3,1,0,2:T(2,128)} %all-gather.2.cloned.1.call-done), kind=kLoop, calls=%fused_computation.95 | loop fusion | bytes 4194304 | tf_op jit(solution)/shard_map/while/body/eval_jaxpr/vmap()/slice | solution.py:91
  131.6 2.3 %copy.68 = f32[1,1,512,512]{2,3,1,0:T(8,128)S(1)} copy(f32[1,1,512,512]{3,1,0,2:T(1,128)} %get-tuple-element.51) | data formatting | bytes 2097152
  134.0 3.6 %copy.69 = f32[1,1,512,512]{2,3,1,0:T(8,128)} copy(f32[1,1,512,512]{3,1,0,2:T(1,128)} %get-tuple-element.50) | data formatting | bytes 2097152
  137.6 2.4 %fusion.30 = (bf16[1,512,512]{1,2,0:T(8,128)(2,1)S(1)}, bf16[1,512,512]{1,2,0:T(8,128)(2,1)}) fusion(f32[1,1,512,512]{2,3,1,0:T(8,128)} %copy.69, f32[1,1,512,512]{2,3,1,0:T(8,128)S(1)} %copy.68, bf16[1,2,512,512]{2,3,1,0:T(8,128)(2,1)S(1)} %bitcast.105), kind=kLoop, calls=%fused_computation.67 | loop fusion | flops 2621440 | bytes 4194304 | tf_op jit(solution)/shard_map/while/body/eval_jaxpr/vmap()/stack | solution.py:89
  140.0 6.5 %fusion.4 = bf16[2,512,512,1]{2,1,0,3:T(8,128)(2,1)} fusion(bf16[1,1,2,512,512]{4,3,2,1,0:T(8,128)(2,1)} %param.3, f32[512,512]{1,0:T(8,128)} %get-tuple-element.55, bf16[1,512,512]{1,2,0:T(8,128)(2,1)} %get-tuple-element.37, bf16[1,512,512]{1,2,0:T(8,128)(2,1)S(1)} %get-tuple-element.36, bf16[1,512,2,512]{3,1,2,0:T(8,128)(2,1)} %get-tuple-element.68, ...), kind=kOutput, calls=%fused_computation.29 | convolution fusion | flops 2152726528 | bytes 8388608 | tf_op jit(solution)/shard_map/while/body/eval_jaxpr/vmap(qypk,pkz->qyz)/dot_general | solution.py:64
  146.5 5.8 %convolution_bitcast_fusion = f32[1,2,512,512]{2,3,1,0:T(8,128)} fusion(bf16[2,512,512,1]{2,1,0,3:T(8,128)(2,1)} %fusion.4, bf16[1,512,2,512]{3,1,2,0:T(8,128)(2,1)} %get-tuple-element.68, bf16[1,512,2,512]{3,1,2,0:T(8,128)(2,1)} %get-tuple-element.75, bf16[1,512,2,512]{3,1,2,0:T(8,128)(2,1)} %get-tuple-element.76, bf16[1,512,2,512]{3,1,2,0:T(8,128)(2,1)S(1)} %copy-done.3), kind=kOutput, calls=%fused_computation.22 | convolution fusion | flops 2150105088 | bytes 7340032 | tf_op jit(solution)/shard_map/while/body/eval_jaxpr/vmap(pyz,pzqw->qyw)/dot_general | solution.py:60
  152.3 1.9 fusion.19
  154.2 1.5 maximum_bitcast_fusion.1
  155.7 4.1 %copy.42 = f32[1,2,512,512]{3,1,0,2:T(2,128)} copy(f32[1,2,512,512]{2,3,1,0:T(8,128)} %maximum_bitcast_fusion.1) | data formatting | bytes 4194304 | tf_op jit(solution)/shard_map/while/body/eval_jaxpr/vmap()/transpose | solution.py:107
  160.2 3.3 %collective-permute-start.3 = (f32[3,2,1,512]{3,1,2,0:T(2,128)S(1)}, f32[3,2,1,512]{3,1,2,0:T(2,128)S(1)}, u32[]{:S(2)}, u32[]{:S(2)}) collective-permute-start(f32[3,2,1,512]{3,1,2,0:T(2,128)S(1)} %copy.47), channel_id=1, source_target_pairs={{1,0},{2,1},{3,2},{4,3},{5,4},{6,5},{7,6},{0,7},{9,8},{10,9},{11,1... | collective-permute-start | bytes 36872 | tf_op jit(solution)/shard_map/ppermute | solution.py:23
  167.7 56.8 %all-reduce.7.cloned.1.call-done = f32[1,2,512,512]{3,1,0,2:T(2,128)} async-done(((f32[1,2,512,512]{3,1,0,2:T(2,128)}), f32[1,2,512,512]{3,1,0,2:T(2,128)}) %all-reduce.7.cloned.1.call-update) | async-done | bytes 2097168
  225.5 2.0 fusion.37
  (46 shorter events, 12.0 us)
Async XLA Ops:
  6.5 8.4 %copy-start.2 = (s32[1,512,512]{2,1,0:T(8,128)S(1)}, s32[1,512,512]{2,1,0:T(8,128)}, u32[]{:S(2)}) copy-start(s32[1,512,512]{2,1,0:T(8,128)} %param.5) | copy-start | bytes 3145732
  6.5 89.1 %all-reduce.5.cloned.1.call-start = ((), (), s32[]{:S(2)}) async-start(), calls=%async_computation.1 | async-start | bytes 4194304
  27.9 0.7 copy-start.4
  28.0 98.3 %all-gather.2.cloned.1.call-start = ((), (), s32[]{:S(2)}) async-start(), calls=%async_computation | async-start | bytes 2359296 | tf_op jit(solution)/shard_map/all_gather | solution.py:136
  97.4 127.1 %all-reduce.7.cloned.1.call-start = ((), (), s32[]{:S(2)}) async-start(), calls=%async_computation.2 | async-start | bytes 4194304
  98.4 10.2 %collective-permute-start = (f32[1,2,64,512]{3,2,1,0:T(8,128)S(1)}, f32[1,2,64,512]{3,2,1,0:T(8,128)S(1)}, u32[]{:S(2)}, u32[]{:S(2)}) collective-permute-start(f32[1,2,64,512]{3,2,1,0:T(8,128)S(1)} %copy.53), channel_id=1, source_target_pairs={{0,8},{8,16},{16,24},{24,0},{1,9},{9,17},{17,25},{25,1},{2,10},{10... | collective-permute-start | bytes 786440 | tf_op jit(solution)/shard_map/ppermute | solution.py:20
  100.0 11.7 %collective-permute-start.1 = (f32[1,2,64,512]{3,2,1,0:T(8,128)S(1)}, f32[1,2,64,512]{3,2,1,0:T(8,128)S(1)}, u32[]{:S(2)}, u32[]{:S(2)}) collective-permute-start(f32[1,2,64,512]{3,2,1,0:T(8,128)S(1)} %copy.53), channel_id=1, source_target_pairs={{8,0},{16,8},{24,16},{0,24},{9,1},{17,9},{25,17},{1,25},{10,2},{18... | collective-permute-start | bytes 786440 | tf_op jit(solution)/shard_map/ppermute | solution.py:23
  140.0 6.5 %copy-start.3 = (bf16[1,512,2,512]{3,1,2,0:T(8,128)(2,1)S(1)}, bf16[1,512,2,512]{3,1,2,0:T(8,128)(2,1)}, u32[]{:S(2)}) copy-start(bf16[1,512,2,512]{3,1,2,0:T(8,128)(2,1)} %get-tuple-element.57) | copy-start | bytes 3145732
  159.9 5.1 %collective-permute-start.2 = (f32[3,2,1,512]{3,1,2,0:T(2,128)S(1)}, f32[3,2,1,512]{3,1,2,0:T(2,128)S(1)}, u32[]{:S(2)}, u32[]{:S(2)}) collective-permute-start(f32[3,2,1,512]{3,1,2,0:T(2,128)S(1)} %copy.46), channel_id=1, source_target_pairs={{0,1},{1,2},{2,3},{3,4},{4,5},{5,6},{6,7},{7,0},{8,9},{9,10},{10,1... | collective-permute-start | bytes 36872 | tf_op jit(solution)/shard_map/ppermute | solution.py:20
  160.2 4.8 %collective-permute-start.3 = (f32[3,2,1,512]{3,1,2,0:T(2,128)S(1)}, f32[3,2,1,512]{3,1,2,0:T(2,128)S(1)}, u32[]{:S(2)}, u32[]{:S(2)}) collective-permute-start(f32[3,2,1,512]{3,1,2,0:T(2,128)S(1)} %copy.47), channel_id=1, source_target_pairs={{1,0},{2,1},{3,2},{4,3},{5,4},{6,5},{7,6},{0,7},{9,8},{10,9},{11,1... | collective-permute-start | bytes 36872 | tf_op jit(solution)/shard_map/ppermute | solution.py:23
  166.6 0.9 copy-start.1
  166.6 58.9 %copy-start = (f32[1,2,64,512]{3,1,0,2:T(2,128)S(1)}, f32[1,2,64,512]{3,1,0,2:T(2,128)}, u32[]{:S(2)}) copy-start(f32[1,2,64,512]{3,1,0,2:T(2,128)} %constant_dynamic-slice_fusion.1) | copy-start | bytes 786436
Sparse Core Ops, SparseCore 0:
  28.1 67.5 all-reduce.4
  97.5 28.7 all-gather.1
  160.0 64.4 all-reduce.6
where the time goes:
time: 235 us; the launch traced here: 234 us
  waiting for transfers between devices  148 us (63%)
  local copies, waits for them, and re-layouts  26.7 us (11%)
  other arithmetic  21.3 us (9%)
  matrix products  17.3 us (7%)
  between operations  14 us (6%)
  starting transfers between devices  6.66 us (3%)
    unnamed x5, waiting for transfers between devices  123 us
    all_gather x1, waiting for transfers between devices, shards(): estimate = lax.all_gather(owned_rows, 'coil', axis=2, tiled=True)  14.6 us
    unnamed x18, local copies, waits for them, and re-layouts  13.1 us
    dot_general x2, matrix products, apply_right(): jnp.einsum('pyz,pzqw->qyw', pair, table, preferred_element_type=jnp.float32)  10.8 us
    ppermute x2, waiting for transfers between devices, padded_2(): lax.ppermute(lax.slice_in_dim(block, block.shape[dim] - width, None, axis...  8.69 us
    transpose x2, local copies, waits for them, and re-layouts, one_slice(): coil_terms = jax.vmap(per_coil, in_axes=(vmap_axes,))(inputs)  6.59 us
    dot_general x1, matrix products, apply_left(): jnp.einsum('qypk,pkz->qyz', table, pair, preferred_element_type=jnp.float32)  6.49 us
    slice x1, local copies, waits for them, and re-layouts, coil_gradient(): estimate_pair[1]  5.35 us
  transfers between devices with their start and end apart: 7, of which 6 were waited for; matrix products, arithmetic and copies ran while one was open for 2% of the time, Pallas kernels for 0%

commit v1 on v0

v1 whole, which is shorter than its diff:
```python
from functools import partial
import math

import jax
import jax.numpy as jnp
import ml_dtypes
import numpy as np
from jax import lax
from jax.experimental import pallas as pl
from jax.experimental.pallas import tpu as pltpu
from jax.sharding import PartitionSpec as P

STEP_SIZE = 0.25
TV_WEIGHT = 0.5
TV_SMOOTH = 0.25

F32 = jnp.float32
BF16 = jnp.bfloat16
VMEM = pl.BlockSpec(memory_space=pltpu.VMEM)
SMEM = pl.BlockSpec(memory_space=pltpu.SMEM)
PARAMS = pltpu.CompilerParams(vmem_limit_bytes=24 * 2**20)


def dft_table(length):
    indices = np.arange(length, dtype=np.int64)
    angles = (indices[:, None] * indices[None, :] % length) * (2.0 * math.pi / length)
    factor = 1.0 / math.sqrt(length)
    cosine = np.cos(angles) * factor
    sine = -np.sin(angles) * factor
    return np.block([[cosine, sine], [-sine, cosine]]).astype(ml_dtypes.bfloat16)


def swap(value, bit):
    count = lax.axis_size("coil")
    return lax.ppermute(value, "coil", [(i, i ^ (1 << bit)) for i in range(count)])


def halving_order(bits):
    masks = [0]
    for bit in reversed(bits):
        masks = masks + [mask | (1 << bit) for mask in masks]
    return masks


def flops(cost):
    return pl.CostEstimate(flops=cost, bytes_accessed=4 * 2**20, transcendentals=0)


def mask_kernel(kspace, sampling, out):
    weight = sampling[...].astype(F32).astype(BF16)
    out[0] = kspace[0] * weight
    out[1] = kspace[1] * weight


def adjoint_kernel(groups, size, me, table, data, sens, *refs):
    outs, (lhs, rhs) = refs[: len(groups)], refs[len(groups) :]
    length = sens.shape[1]
    device = me[0]
    starts = [pl.multiple_of(start(device), size) for group in groups for start in group]
    total = len(starts) * size
    for block, start in enumerate(starts):
        at = block * size
        lhs[at : at + size, :] = table[pl.ds(start, size), :]
        lhs[total + at : total + at + size, :] = table[pl.ds(length + start, size), :]
    upper = jnp.dot(lhs[...], data[...], preferred_element_type=F32).astype(BF16)
    real, imag = upper[:total], upper[total:]
    rhs[:total, :length] = imag
    rhs[:total, length:] = real
    rhs[total:, :length] = -real
    rhs[total:, length:] = imag
    back = jnp.dot(rhs[...], table[:, length:], preferred_element_type=F32)
    block = 0
    for group, out in zip(groups, outs):
        for place in range(len(group)):
            at, rows = block * size, pl.ds(starts[block], size)
            real, imag = back[at : at + size], back[total + at : total + at + size]
            sens_real, sens_imag = sens[0, rows, :].astype(F32), sens[1, rows, :].astype(F32)
            out[place, 0] = sens_real * real + sens_imag * imag
            out[place, 1] = sens_real * imag - sens_imag * real
            block += 1


def adjoint(groups, size, me, table, data, sens):
    length = sens.shape[1]
    total = size * sum(len(group) for group in groups)
    return pl.pallas_call(
        partial(adjoint_kernel, groups, size),
        out_shape=[jax.ShapeDtypeStruct((len(group), 2, size, length), F32) for group in groups],
        in_specs=[SMEM, VMEM, VMEM, VMEM],
        out_specs=[VMEM] * len(groups),
        scratch_shapes=[pltpu.VMEM((2 * total, 2 * length), BF16)] * 2,
        compiler_params=PARAMS,
        cost_estimate=flops(16 * total * length * length),
        name="adjoint",
    )(me, table, data.reshape(2 * length, length), sens)


def forward_kernel(chunk, masks, last, me, table, sens, *refs):
    pieces, refs = refs[: len(masks)], refs[len(masks) :]
    if last:
        before, kspace, sampling, volume, out, lhs, mid, neg = refs
    else:
        volume, out, lhs, mid, neg = refs
    length = sens.shape[1]
    size = pieces[0].shape[1]
    rows = size * len(masks)
    low = me[0] & (len(masks) - 1)
    for mask, piece in zip(masks, pieces):
        start = pl.multiple_of((low ^ mask) * size, size)
        real, imag = piece[0], piece[1]
        volume[0, pl.ds(start, size), :] = real
        volume[1, pl.ds(start, size), :] = imag
        at = pl.ds(pl.multiple_of(chunk * rows + start, size), size)
        sens_real, sens_imag = sens[0, at, :].astype(F32), sens[1, at, :].astype(F32)
        coil_real = (sens_real * real - sens_imag * imag).astype(BF16)
        coil_imag = (sens_real * imag + sens_imag * real).astype(BF16)
        top, bottom = pl.ds(start, size), pl.ds(pl.multiple_of(rows + start, size), size)
        lhs[top, :length] = -coil_imag
        lhs[top, length:] = coil_real
        lhs[bottom, :length] = coil_real
        lhs[bottom, length:] = coil_imag
    middle = jnp.dot(lhs[...], table[:, length:], preferred_element_type=F32).astype(BF16)
    mid[:, :length] = middle[:rows]
    mid[:, length:] = middle[rows:]
    neg[:, :length] = -middle[rows:]
    neg[:, length:] = middle[:rows]
    first = chunk * rows
    cosine = table[:length, first : first + rows]
    sine = table[:length, length + first : length + first + rows]
    freq = jnp.dot(cosine, mid[...], preferred_element_type=F32)
    freq += jnp.dot(sine, neg[...], preferred_element_type=F32)
    if last:
        freq += before[...]
        weight = sampling[...].astype(F32)
        out[0] = (weight * (freq[:, :length] - kspace[0].astype(F32))).astype(BF16)
        out[1] = (weight * (freq[:, length:] - kspace[1].astype(F32))).astype(BF16)
    else:
        out[...] = freq


def forward(chunk, masks, me, table, sens, pieces, rest):
    length = sens.shape[1]
    rows = pieces[0].shape[1] * len(masks)
    last = bool(rest)
    freq = jax.ShapeDtypeStruct((length, 2 * length), F32)
    resid = jax.ShapeDtypeStruct((2, length, length), BF16)
    return pl.pallas_call(
        partial(forward_kernel, chunk, masks, last),
        out_shape=[jax.ShapeDtypeStruct((2, rows, length), F32), resid if last else freq],
        in_specs=[SMEM] + [VMEM] * (2 + len(pieces) + len(rest)),
        out_specs=[VMEM] * 2,
        scratch_shapes=[pltpu.VMEM((2 * rows, 2 * length), BF16)]
        + [pltpu.VMEM((rows, 2 * length), BF16)] * 2,
        compiler_params=PARAMS,
        cost_estimate=flops(16 * rows * length * length),
        name="forward",
    )(me, table, sens, *pieces, *rest)


def extend_kernel(size, me, low, high, out):
    half = low.shape[1]
    start = me[0] * size
    for at, first, count in ((0, start - 8, 8), (8, start, size), (8 + size, start + size, 8)):
        first = (first + 2 * half) & (2 * half - 1)

        @pl.when(first < half)
        def _():
            out[:, at : at + count, :] = low[:, pl.ds(pl.multiple_of(first, 8), count), :]

        @pl.when(first >= half)
        def _():
            out[:, at : at + count, :] = high[:, pl.ds(pl.multiple_of(first - half, 8), count), :]


def tv_kernel(own, before, after, out):
    size = out.shape[1]
    length = out.shape[2]

    def parts(ref, first, count):
        return [ref[part, first : first + count, :] for part in (0, 1)]

    def next_column(values):
        return [pltpu.roll(value, length - 1, 1) for value in values]

    def minus(left, right):
        return [a - b for a, b in zip(left, right)]

    def fluxes(here, slices, rows):
        columns = minus(next_column(here), here)
        squares = TV_SMOOTH
        for change in (slices, rows, columns):
            squares = squares + (change[0] * change[0] + change[1] * change[1])
        weight = lax.rsqrt(squares)
        return [[weight * value for value in change] for change in (slices, rows, columns)]

    count = size + 1
    here = parts(own, 7, count)
    slices, rows, columns = fluxes(
        here, minus(parts(after, 7, count), here), minus(parts(own, 8, count), here)
    )
    back = parts(before, 8, size)
    center = parts(own, 8, size)
    back_slices, _, _ = fluxes(back, minus(center, back), minus(parts(before, 9, size), back))
    for part in (0, 1):
        col = columns[part][1:]
        tv = (
            (back_slices[part] - slices[part][1:])
            + (rows[part][:-1] - rows[part][1:])
            + (pltpu.roll(col, 1, 1) - col)
        )
        out[part] = center[part] - (STEP_SIZE * TV_WEIGHT) * tv


def shards(kspace, sensitivity, sampling):
    kspace, sens, sampling = kspace[0, 0], sensitivity[0, 0], sampling[0]
    length = sampling.shape[0]
    count = lax.axis_size("coil")
    slabs = lax.axis_size("slab")
    top = count.bit_length() - 2
    size = length // count
    half = count // 2
    table = jnp.asarray(dft_table(length))
    me = lax.axis_index("coil").astype(jnp.int32).reshape(1)

    measured = pl.pallas_call(
        mask_kernel,
        out_shape=jax.ShapeDtypeStruct(kspace.shape, BF16),
        in_specs=[VMEM, VMEM],
        out_specs=VMEM,
        compiler_params=PARAMS,
        name="measured",
    )(kspace, sampling)

    def chunk_start(chunk, mask):
        return lambda device: (chunk * half + ((device & (half - 1)) ^ mask)) * size

    order = halving_order(range(1, top))
    groups = []
    for chunk in (0, 1):
        groups.append([chunk_start(chunk, mask | 1) for mask in order])
        groups.append([chunk_start(chunk, mask) for mask in order])
    others, owns = [None, None], [None, None]
    (others[0],) = adjoint(groups[0:1], size, me, table, measured, sens)
    (owns[0],) = adjoint(groups[1:2], size, me, table, measured, sens)
    others[1], owns[1] = adjoint(groups[2:4], size, me, table, measured, sens)

    masks = list(range(half))
    freq, volumes = None, []
    for chunk in (0, 1):
        current = owns[chunk] + swap(others[chunk], 0)
        for bit in range(1, top):
            middle = current.shape[0] // 2
            current = current[:middle] + swap(current[middle:], bit)
        current = current[0]
        pieces = {0: current + swap(current, top)}
        for bit in reversed(range(top)):
            for mask in list(pieces):
                pieces[mask | (1 << bit)] = swap(pieces[mask], bit)
        rest = () if chunk == 0 else (freq, kspace, sampling)
        volume, freq = forward(
            chunk, masks, me, table, sens, [pieces[mask] for mask in masks], rest
        )
        volumes.append(volume)
    resid = freq

    parts = 2 if size >= 32 else 1
    part_size = size // parts

    def row_start(part, mask):
        return lambda device: (device ^ mask) * size + part * part_size

    order = halving_order(range(1, top + 1))
    gradient = []
    for part in range(parts):
        group = [row_start(part, mask | 1) for mask in order]
        (other,) = adjoint([group], part_size, me, table, resid, sens)
        group = [row_start(part, mask) for mask in order]
        (own,) = adjoint([group], part_size, me, table, resid, sens)
        current = own + swap(other, 0)
        for bit in range(1, top + 1):
            middle = current.shape[0] // 2
            current = current[:middle] + swap(current[middle:], bit)
        gradient.append(current[0])

    extended = pl.pallas_call(
        partial(extend_kernel, size),
        out_shape=jax.ShapeDtypeStruct((2, size + 16, length), F32),
        in_specs=[SMEM, VMEM, VMEM],
        out_specs=VMEM,
        compiler_params=PARAMS,
        name="extend",
    )(me, *volumes)
    ahead = [(i, (i + 1) % slabs) for i in range(slabs)]
    behind = [(target, source) for source, target in ahead]
    before = lax.ppermute(extended, "slab", ahead)
    after = lax.ppermute(extended, "slab", behind)
    base = pl.pallas_call(
        tv_kernel,
        out_shape=jax.ShapeDtypeStruct((2, size, length), F32),
        in_specs=[VMEM, VMEM, VMEM],
        out_specs=VMEM,
        compiler_params=PARAMS,
        name="total_variation",
    )(extended, before, after)
    return (base - STEP_SIZE * jnp.concatenate(gradient, axis=1))[None]


def solution(mesh):
    placed = (
        P("slab", "coil", None, None, None),
        P("slab", "coil", None, None, None),
        P("slab", None, None),
    )
    return jax.shard_map(
        shards, mesh=mesh, in_specs=placed, out_specs=P("slab", None, "coil", None), check_vma=False
    )
```

time: 235 us -> 93.3 us (0.40)
  waiting for transfers between devices: 148 us -> 58.9 us
  local copies, waits for them, and re-layouts: 26.7 us -> 2.72 us
  other arithmetic: 21.3 us -> 1.33 us
  matrix products: 17.3 us -> 0 us
  between operations: 14 us -> 0.31 us
  starting transfers between devices: 6.66 us -> 18.9 us
  Pallas kernels: 0 us -> 11 us
    unnamed x5 -> x0, waiting for transfers between devices: 123 us -> none
    ppermute x4 -> x20, waiting for transfers between devices: 10.7 us -> 58.9 us  [the longest x18 47.4 us: swap(): lax.ppermute(value, 'coil', [(i, i ^ 1 << bit) for i in range(count)])]
    dot_general x3 -> x0, matrix products: 17.3 us -> none  [the longest x2 10.8 us: apply_right(): jnp.einsum('pyz,pzqw->qyw', pair, table, preferred_element_type=jnp.float32)]
    all_gather x1 -> x0, waiting for transfers between devices: 14.6 us -> none  [shards(): estimate = lax.all_gather(owned_rows, 'coil', axis=2, tiled=True)]
    ppermute x4 -> x20, starting transfers between devices: 6.57 us -> 18.9 us  [the longest x18 16.6 us: swap(): lax.ppermute(value, 'coil', [(i, i ^ 1 << bit) for i in range(count)])]
    pallas_call x0 -> x12, Pallas kernels: none -> 11 us  [the longest x7 6.5 us: adjoint(): pl.pallas_call(partial(adjoint_kernel, groups, size), out_shape=[jax.Shap...]
    unnamed x18 -> x12, local copies, waits for them, and re-layouts: 13.1 us -> 2.62 us
    transpose x2 -> x0, local copies, waits for them, and re-layouts: 6.59 us -> none  [one_slice(): coil_terms = jax.vmap(per_coil, in_axes=(vmap_axes,))(inputs)]
  transfers between devices with their start and end apart: 7 -> 20, of which waited for: 6 -> 10; matrix products, arithmetic and copies ran while one was open for 2% -> 1% of each run, Pallas kernels for 0% -> 8%
where the time goes in v1:
time: 93.3 us; the launch traced here: 93.1 us
  waiting for transfers between devices  58.9 us (63%)
  starting transfers between devices  18.9 us (20%)
  Pallas kernels  11 us (12%)
  local copies, waits for them, and re-layouts  2.72 us (3%)
  other arithmetic  1.33 us (1%)
    ppermute x18, waiting for transfers between devices, swap(): lax.ppermute(value, 'coil', [(i, i ^ 1 << bit) for i in range(count)])  47.4 us
    ppermute x18, starting transfers between devices, swap(): lax.ppermute(value, 'coil', [(i, i ^ 1 << bit) for i in range(count)])  16.6 us
    ppermute x1, waiting for transfers between devices, shards(): before = lax.ppermute(extended, 'slab', ahead)  7.39 us
    pallas_call x7, Pallas kernels, adjoint(): pl.pallas_call(partial(adjoint_kernel, groups, size), out_shape=[jax.Shap...  6.5 us
    ppermute x1, waiting for transfers between devices, shards(): after = lax.ppermute(extended, 'slab', behind)  4.1 us
    pallas_call x2, Pallas kernels, forward(): pl.pallas_call(partial(forward_kernel, chunk, masks, last), out_shape=[ja...  3.82 us
    unnamed x12, local copies, waits for them, and re-layouts  2.62 us
    ppermute x1, starting transfers between devices, shards(): after = lax.ppermute(extended, 'slab', behind)  2.34 us
  transfers between devices with their start and end apart: 20, of which 10 were waited for; matrix products, arithmetic and copies ran while one was open for 1% of the time, Pallas kernels for 8%

profile of v1, /device:TPU:0, one launch (start us, length us, event | category | flops | bytes accessed | tf_op | source)
XLA Modules:
  0.0 93.1 jit_solution(5720930591144083576)
XLA Ops:
  0.0 1.4 %copy-done.2 = bf16[1,1,2,512,512]{4,3,2,1,0:T(8,128)(2,1)S(1)} copy-done((bf16[1,1,2,512,512]{4,3,2,1,0:T(8,128)(2,1)S(1)}, bf16[1,1,2,512,512]{4,3,2,1,0:T(8,128)(2,1)}, u32[]{:S(2)}) %copy-start.2) | copy-done | bytes 1048600
  1.4 1.2 %copy-done.4 = s32[1,512,512]{2,1,0:T(8,128)S(1)} copy-done((s32[1,512,512]{2,1,0:T(8,128)S(1)}, s32[1,512,512]{2,1,0:T(8,128)}, u32[]{:S(2)}) %copy-start.4) | copy-done | bytes 1048600
  4.1 1.4 %adjoint.9 = (f32[2,2,64,512]{3,2,1,0:T(8,128)S(1)}, f32[2,2,64,512]{3,2,1,0:T(8,128)S(1)}) custom-call(s32[1]{0:T(128)} %bitcast.me, bf16[1024,1024]{1,0:T(8,128)(2,1)S(1)} %copy-done, bf16[1024,512]{1,0:T(8,128)(2,1)S(1)} %bitcast.30, bf16[2,512,512]{2,1,0:T(8,128)(2,1)S(1)} %bitcast.17), custom_call_target="tpu_custom_call" | custom-call | flops 1073741824 | bytes 4194304 | tf_op jit(solution)/shard_map/adjoint/pallas_call | solution.py:86
  6.6 3.1 %collective-permute-start.1 = (f32[1,2,64,512]{3,2,1,0:T(8,128)S(1)}, f32[1,2,64,512]{3,2,1,0:T(8,128)S(1)}, u32[]{:S(2)}, u32[]{:S(2)}) collective-permute-start(f32[1,2,64,512]{3,2,1,0:T(8,128)S(1)} %slice.49), channel_id=1, source_target_pairs={{0,2},{1,3},{2,0},{3,1},{4,6},{5,7},{6,4},{7,5},{8,10},{9,11},{10,... | collective-permute-start | bytes 786440 | tf_op jit(solution)/shard_map/ppermute | solution.py:35
  10.4 6.4 %collective-permute-done.1 = f32[1,2,64,512]{3,2,1,0:T(8,128)S(1)} collective-permute-done((f32[1,2,64,512]{3,2,1,0:T(8,128)S(1)}, f32[1,2,64,512]{3,2,1,0:T(8,128)S(1)}, u32[]{:S(2)}, u32[]{:S(2)}) %collective-permute-start.1) | collective-permute-done | bytes 262176 | tf_op jit(solution)/shard_map/ppermute | solution.py:35
  16.9 3.1 %collective-permute-start.2 = (f32[2,64,512]{2,1,0:T(8,128)S(1)}, f32[2,64,512]{2,1,0:T(8,128)S(1)}, u32[]{:S(2)}, u32[]{:S(2)}) collective-permute-start(f32[2,64,512]{2,1,0:T(8,128)S(1)} %fusion.1), channel_id=1, source_target_pairs={{0,4},{1,5},{2,6},{3,7},{4,0},{5,1},{6,2},{7,3},{8,12},{9,13},{10,... | collective-permute-start | bytes 786440 | tf_op jit(solution)/shard_map/ppermute | solution.py:35
  20.0 6.6 %collective-permute-done.7 = f32[1,2,64,512]{3,2,1,0:T(8,128)S(1)} collective-permute-done((f32[1,2,64,512]{3,2,1,0:T(8,128)S(1)}, f32[1,2,64,512]{3,2,1,0:T(8,128)S(1)}, u32[]{:S(2)}, u32[]{:S(2)}) %collective-permute-start.7) | collective-permute-done | bytes 262176 | tf_op jit(solution)/shard_map/ppermute | solution.py:35
  26.7 10.3 %collective-permute-done.2 = f32[2,64,512]{2,1,0:T(8,128)S(1)} collective-permute-done((f32[2,64,512]{2,1,0:T(8,128)S(1)}, f32[2,64,512]{2,1,0:T(8,128)S(1)}, u32[]{:S(2)}, u32[]{:S(2)}) %collective-permute-start.2) | collective-permute-done | bytes 262176 | tf_op jit(solution)/shard_map/ppermute | solution.py:35
  37.1 2.1 %collective-permute-start.4 = (f32[2,64,512]{2,1,0:T(8,128)S(1)}, f32[2,64,512]{2,1,0:T(8,128)S(1)}, u32[]{:S(2)}, u32[]{:S(2)}) collective-permute-start(f32[2,64,512]{2,1,0:T(8,128)S(1)} %add.38.refs_0_), channel_id=1, source_target_pairs={{0,2},{1,3},{2,0},{3,1},{4,6},{5,7},{6,4},{7,5},{8,10},{9,11},{10,... | collective-permute-start | bytes 786440 | tf_op jit(solution)/shard_map/ppermute | solution.py:35
  39.2 2.7 %collective-permute-done.8 = f32[2,64,512]{2,1,0:T(8,128)S(1)} collective-permute-done((f32[2,64,512]{2,1,0:T(8,128)S(1)}, f32[2,64,512]{2,1,0:T(8,128)S(1)}, u32[]{:S(2)}, u32[]{:S(2)}) %collective-permute-start.8) | collective-permute-done | bytes 262176 | tf_op jit(solution)/shard_map/ppermute | solution.py:35
  42.6 4.9 %collective-permute-done.4.refs_2_ = f32[2,64,512]{2,1,0:T(8,128)S(1)} collective-permute-done((f32[2,64,512]{2,1,0:T(8,128)S(1)}, f32[2,64,512]{2,1,0:T(8,128)S(1)}, u32[]{:S(2)}, u32[]{:S(2)}) %collective-permute-start.4) | collective-permute-done | bytes 262176 | tf_op jit(solution)/shard_map/ppermute | solution.py:35
  48.0 5.0 %collective-permute-done.10.refs_2_ = f32[2,64,512]{2,1,0:T(8,128)S(1)} collective-permute-done((f32[2,64,512]{2,1,0:T(8,128)S(1)}, f32[2,64,512]{2,1,0:T(8,128)S(1)}, u32[]{:S(2)}, u32[]{:S(2)}) %collective-permute-start.10) | collective-permute-done | bytes 262176 | tf_op jit(solution)/shard_map/ppermute | solution.py:35
  53.1 1.8 %forward.2 = (f32[2,256,512]{2,1,0:T(8,128)S(1)}, f32[512,1024]{1,0:T(8,128)S(1)}) custom-call(s32[1]{0:T(128)} %bitcast.me, bf16[1024,1024]{1,0:T(8,128)(2,1)S(1)} %copy-done, bf16[2,512,512]{2,1,0:T(8,128)(2,1)S(1)} %bitcast.19, f32[2,64,512]{2,1,0:T(8,128)S(1)} %add.38.refs_0_, f32[2,64,512]{2,1,0:T(8,128)S(1)} %collective-permute-done.3.refs_1_, ...), custom_call_target="tpu_custom_call" | custom-call | flops 1073741824 | bytes 4194304 | tf_op jit(solution)/shard_map/forward/pallas_call | solution.py:147
  54.9 2.0 %forward.3 = (f32[2,256,512]{2,1,0:T(8,128)S(1)}, bf16[2,512,512]{2,1,0:T(8,128)(2,1)S(1)}) custom-call(s32[1]{0:T(128)} %bitcast.me, bf16[1024,1024]{1,0:T(8,128)(2,1)S(1)} %copy-done, bf16[2,512,512]{2,1,0:T(8,128)(2,1)S(1)} %bitcast.20, f32[2,64,512]{2,1,0:T(8,128)S(1)} %add.41.refs_0_, f32[2,64,512]{2,1,0:T(8,128)S(1)} %collective-permute-done.9.refs_1_, ...), custom_call_target="tpu_custom_call" | custom-call | flops 1073741824 | bytes 4194304 | tf_op jit(solution)/shard_map/forward/pallas_call | solution.py:147
  58.4 0.9 adjoint.13
  59.4 2.3 %collective-permute-start.13 = (f32[2,80,512]{2,1,0:T(8,128)S(1)}, f32[2,80,512]{2,1,0:T(8,128)S(1)}, u32[]{:S(2)}, u32[]{:S(2)}) collective-permute-start(f32[2,80,512]{2,1,0:T(8,128)S(1)} %extend.1.own), channel_id=1, source_target_pairs={{8,0},{16,8},{24,16},{0,24},{9,1},{17,9},{25,17},{1,25},{10,2},{18... | collective-permute-start | bytes 983048 | tf_op jit(solution)/shard_map/ppermute | solution.py:296
  62.8 0.9 adjoint.12
  63.8 2.1 %collective-permute-start.18 = (f32[2,2,32,512]{3,2,1,0:T(8,128)S(1)}, f32[2,2,32,512]{3,2,1,0:T(8,128)S(1)}, u32[]{:S(2)}, u32[]{:S(2)}) collective-permute-start(f32[2,2,32,512]{3,2,1,0:T(8,128)S(1)} %slice.57), channel_id=1, source_target_pairs={{0,2},{1,3},{2,0},{3,1},{4,6},{5,7},{6,4},{7,5},{8,10},{9,11},{10,... | collective-permute-start | bytes 786440 | tf_op jit(solution)/shard_map/ppermute | solution.py:35
  65.8 4.1 %collective-permute-done.13.after = f32[2,80,512]{2,1,0:T(8,128)S(1)} collective-permute-done((f32[2,80,512]{2,1,0:T(8,128)S(1)}, f32[2,80,512]{2,1,0:T(8,128)S(1)}, u32[]{:S(2)}, u32[]{:S(2)}) %collective-permute-start.13) | collective-permute-done | bytes 327712 | tf_op jit(solution)/shard_map/ppermute | solution.py:296
  69.9 7.4 %collective-permute-done.12.before = f32[2,80,512]{2,1,0:T(8,128)S(1)} collective-permute-done((f32[2,80,512]{2,1,0:T(8,128)S(1)}, f32[2,80,512]{2,1,0:T(8,128)S(1)}, u32[]{:S(2)}, u32[]{:S(2)}) %collective-permute-start.12) | collective-permute-done | bytes 327712 | tf_op jit(solution)/shard_map/ppermute | solution.py:295
  77.9 1.8 %collective-permute-start.16 = (f32[1,2,32,512]{3,2,1,0:T(8,128)S(1)}, f32[1,2,32,512]{3,2,1,0:T(8,128)S(1)}, u32[]{:S(2)}, u32[]{:S(2)}) collective-permute-start(f32[1,2,32,512]{3,2,1,0:T(8,128)S(1)} %slice.55), channel_id=1, source_target_pairs={{0,4},{1,5},{2,6},{3,7},{4,0},{5,1},{6,2},{7,3},{8,12},{9,13},{10,... | collective-permute-start | bytes 393224 | tf_op jit(solution)/shard_map/ppermute | solution.py:35
  79.7 1.3 %collective-permute-start.19 = (f32[1,2,32,512]{3,2,1,0:T(8,128)S(1)}, f32[1,2,32,512]{3,2,1,0:T(8,128)S(1)}, u32[]{:S(2)}, u32[]{:S(2)}) collective-permute-start(f32[1,2,32,512]{3,2,1,0:T(8,128)S(1)} %slice.59), channel_id=1, source_target_pairs={{0,4},{1,5},{2,6},{3,7},{4,0},{5,1},{6,2},{7,3},{8,12},{9,13},{10,... | collective-permute-start | bytes 393224 | tf_op jit(solution)/shard_map/ppermute | solution.py:35
  81.0 9.7 %collective-permute-done.16 = f32[1,2,32,512]{3,2,1,0:T(8,128)S(1)} collective-permute-done((f32[1,2,32,512]{3,2,1,0:T(8,128)S(1)}, f32[1,2,32,512]{3,2,1,0:T(8,128)S(1)}, u32[]{:S(2)}, u32[]{:S(2)}) %collective-permute-start.16) | collective-permute-done | bytes 131104 | tf_op jit(solution)/shard_map/ppermute | solution.py:35
  90.7 1.7 %collective-permute-done.19 = f32[1,2,32,512]{3,2,1,0:T(8,128)S(1)} collective-permute-done((f32[1,2,32,512]{3,2,1,0:T(8,128)S(1)}, f32[1,2,32,512]{3,2,1,0:T(8,128)S(1)}, u32[]{:S(2)}, u32[]{:S(2)}) %collective-permute-start.19) | collective-permute-done | bytes 131104 | tf_op jit(solution)/shard_map/ppermute | solution.py:35
  (59 shorter events, 8.7 us)
Async XLA Ops:
  0.0 2.7 %copy-start = (bf16[1024,1024]{1,0:T(8,128)(2,1)S(1)}, bf16[1024,1024]{1,0:T(8,128)(2,1)}, u32[]{:S(2)}) copy-start(bf16[1024,1024]{1,0:T(8,128)(2,1)} %constant.8.clone.table) | copy-start | bytes 6291460
  0.0 2.7 %copy-start.1 = (bf16[1,1,2,512,512]{4,3,2,1,0:T(8,128)(2,1)S(1)}, bf16[1,1,2,512,512]{4,3,2,1,0:T(8,128)(2,1)}, u32[]{:S(2)}) copy-start(bf16[1,1,2,512,512]{4,3,2,1,0:T(8,128)(2,1)} %param.5) | copy-start | bytes 3145732
  3.6 2.9 %collective-permute-start = (f32[2,2,64,512]{3,2,1,0:T(8,128)S(1)}, f32[2,2,64,512]{3,2,1,0:T(8,128)S(1)}, u32[]{:S(2)}, u32[]{:S(2)}) collective-permute-start(f32[2,2,64,512]{3,2,1,0:T(8,128)S(1)} %adjoint.8), channel_id=1, source_target_pairs={{0,1},{1,0},{2,3},{3,2},{4,5},{5,4},{6,7},{7,6},{8,9},{9,8},{10,11... | collective-permute-start | bytes 1572872 | tf_op jit(solution)/shard_map/ppermute | solution.py:35
  5.5 4.2 %collective-permute-start.6 = (f32[2,2,64,512]{3,2,1,0:T(8,128)S(1)}, f32[2,2,64,512]{3,2,1,0:T(8,128)S(1)}, u32[]{:S(2)}, u32[]{:S(2)}) collective-permute-start(f32[2,2,64,512]{3,2,1,0:T(8,128)S(1)} %get-tuple-element.13), channel_id=1, source_target_pairs={{0,1},{1,0},{2,3},{3,2},{4,5},{5,4},{6,7},{7,6},{8,9},{9,8},{10,11... | collective-permute-start | bytes 1572872 | tf_op jit(solution)/shard_map/ppermute | solution.py:35
  6.6 10.2 %collective-permute-start.1 = (f32[1,2,64,512]{3,2,1,0:T(8,128)S(1)}, f32[1,2,64,512]{3,2,1,0:T(8,128)S(1)}, u32[]{:S(2)}, u32[]{:S(2)}) collective-permute-start(f32[1,2,64,512]{3,2,1,0:T(8,128)S(1)} %slice.49), channel_id=1, source_target_pairs={{0,2},{1,3},{2,0},{3,1},{4,6},{5,7},{6,4},{7,5},{8,10},{9,11},{10,... | collective-permute-start | bytes 786440 | tf_op jit(solution)/shard_map/ppermute | solution.py:35
  9.8 16.8 %collective-permute-start.7 = (f32[1,2,64,512]{3,2,1,0:T(8,128)S(1)}, f32[1,2,64,512]{3,2,1,0:T(8,128)S(1)}, u32[]{:S(2)}, u32[]{:S(2)}) collective-permute-start(f32[1,2,64,512]{3,2,1,0:T(8,128)S(1)} %slice.51), channel_id=1, source_target_pairs={{0,2},{1,3},{2,0},{3,1},{4,6},{5,7},{6,4},{7,5},{8,10},{9,11},{10,... | collective-permute-start | bytes 786440 | tf_op jit(solution)/shard_map/ppermute | solution.py:35
  16.9 20.2 %collective-permute-start.2 = (f32[2,64,512]{2,1,0:T(8,128)S(1)}, f32[2,64,512]{2,1,0:T(8,128)S(1)}, u32[]{:S(2)}, u32[]{:S(2)}) collective-permute-start(f32[2,64,512]{2,1,0:T(8,128)S(1)} %fusion.1), channel_id=1, source_target_pairs={{0,4},{1,5},{2,6},{3,7},{4,0},{5,1},{6,2},{7,3},{8,12},{9,13},{10,... | collective-permute-start | bytes 786440 | tf_op jit(solution)/shard_map/ppermute | solution.py:35
  26.6 15.3 %collective-permute-start.8 = (f32[2,64,512]{2,1,0:T(8,128)S(1)}, f32[2,64,512]{2,1,0:T(8,128)S(1)}, u32[]{:S(2)}, u32[]{:S(2)}) collective-permute-start(f32[2,64,512]{2,1,0:T(8,128)S(1)} %fusion), channel_id=1, source_target_pairs={{0,4},{1,5},{2,6},{3,7},{4,0},{5,1},{6,2},{7,3},{8,12},{9,13},{10,... | collective-permute-start | bytes 786440 | tf_op jit(solution)/shard_map/ppermute | solution.py:35
  37.1 10.4 %collective-permute-start.4 = (f32[2,64,512]{2,1,0:T(8,128)S(1)}, f32[2,64,512]{2,1,0:T(8,128)S(1)}, u32[]{:S(2)}, u32[]{:S(2)}) collective-permute-start(f32[2,64,512]{2,1,0:T(8,128)S(1)} %add.38.refs_0_), channel_id=1, source_target_pairs={{0,2},{1,3},{2,0},{3,1},{4,6},{5,7},{6,4},{7,5},{8,10},{9,11},{10,... | collective-permute-start | bytes 786440 | tf_op jit(solution)/shard_map/ppermute | solution.py:35
  41.9 12.9 %copy-start.3 = (bf16[1,1,2,512,512]{4,3,2,1,0:T(8,128)(2,1)S(1)}, bf16[1,1,2,512,512]{4,3,2,1,0:T(8,128)(2,1)}, u32[]{:S(2)}) copy-start(bf16[1,1,2,512,512]{4,3,2,1,0:T(8,128)(2,1)} %param.4) | copy-start | bytes 3145732
  42.0 12.9 %copy-start.5 = (s32[1,512,512]{2,1,0:T(8,128)S(1)}, s32[1,512,512]{2,1,0:T(8,128)}, u32[]{:S(2)}) copy-start(s32[1,512,512]{2,1,0:T(8,128)} %param.6) | copy-start | bytes 3145732
  42.0 11.1 %collective-permute-start.10 = (f32[2,64,512]{2,1,0:T(8,128)S(1)}, f32[2,64,512]{2,1,0:T(8,128)S(1)}, u32[]{:S(2)}, u32[]{:S(2)}) collective-permute-start(f32[2,64,512]{2,1,0:T(8,128)S(1)} %add.41.refs_0_), channel_id=1, source_target_pairs={{0,2},{1,3},{2,0},{3,1},{4,6},{5,7},{6,4},{7,5},{8,10},{9,11},{10,... | collective-permute-start | bytes 786440 | tf_op jit(solution)/shard_map/ppermute | solution.py:35
  42.6 10.5 %collective-permute-start.3 = (f32[2,64,512]{2,1,0:T(8,128)S(1)}, f32[2,64,512]{2,1,0:T(8,128)S(1)}, u32[]{:S(2)}, u32[]{:S(2)}) collective-permute-start(f32[2,64,512]{2,1,0:T(8,128)S(1)} %add.38.refs_0_), channel_id=1, source_target_pairs={{0,1},{1,0},{2,3},{3,2},{4,5},{5,4},{6,7},{7,6},{8,9},{9,8},{10,11... | collective-permute-start | bytes 786440 | tf_op jit(solution)/shard_map/ppermute | solution.py:35
  47.5 5.5 %collective-permute-start.5 = (f32[2,64,512]{2,1,0:T(8,128)S(1)}, f32[2,64,512]{2,1,0:T(8,128)S(1)}, u32[]{:S(2)}, u32[]{:S(2)}) collective-permute-start(f32[2,64,512]{2,1,0:T(8,128)S(1)} %collective-permute-done.4.refs_2_), channel_id=1, source_target_pairs={{0,1},{1,0},{2,3},{3,2},{4,5},{5,4},{6,7},{7,6},{8,9},{9,8},{10,11... | collective-permute-start | bytes 786440 | tf_op jit(solution)/shard_map/ppermute | solution.py:35
  47.5 7.4 %collective-permute-start.9 = (f32[2,64,512]{2,1,0:T(8,128)S(1)}, f32[2,64,512]{2,1,0:T(8,128)S(1)}, u32[]{:S(2)}, u32[]{:S(2)}) collective-permute-start(f32[2,64,512]{2,1,0:T(8,128)S(1)} %add.41.refs_0_), channel_id=1, source_target_pairs={{0,1},{1,0},{2,3},{3,2},{4,5},{5,4},{6,7},{7,6},{8,9},{9,8},{10,11... | collective-permute-start | bytes 786440 | tf_op jit(solution)/shard_map/ppermute | solution.py:35
  53.0 1.8 %collective-permute-start.11 = (f32[2,64,512]{2,1,0:T(8,128)S(1)}, f32[2,64,512]{2,1,0:T(8,128)S(1)}, u32[]{:S(2)}, u32[]{:S(2)}) collective-permute-start(f32[2,64,512]{2,1,0:T(8,128)S(1)} %collective-permute-done.10.refs_2_), channel_id=1, source_target_pairs={{0,1},{1,0},{2,3},{3,2},{4,5},{5,4},{6,7},{7,6},{8,9},{9,8},{10,11... | collective-permute-start | bytes 786440 | tf_op jit(solution)/shard_map/ppermute | solution.py:35
  57.8 4.8 %collective-permute-start.14 = (f32[4,2,32,512]{3,2,1,0:T(8,128)S(1)}, f32[4,2,32,512]{3,2,1,0:T(8,128)S(1)}, u32[]{:S(2)}, u32[]{:S(2)}) collective-permute-start(f32[4,2,32,512]{3,2,1,0:T(8,128)S(1)} %adjoint.11), channel_id=1, source_target_pairs={{0,1},{1,0},{2,3},{3,2},{4,5},{5,4},{6,7},{7,6},{8,9},{9,8},{10,11... | collective-permute-start | bytes 1572872 | tf_op jit(solution)/shard_map/ppermute | solution.py:35
  59.2 4.4 %collective-permute-start.17 = (f32[4,2,32,512]{3,2,1,0:T(8,128)S(1)}, f32[4,2,32,512]{3,2,1,0:T(8,128)S(1)}, u32[]{:S(2)}, u32[]{:S(2)}) collective-permute-start(f32[4,2,32,512]{3,2,1,0:T(8,128)S(1)} %adjoint.13), channel_id=1, source_target_pairs={{0,1},{1,0},{2,3},{3,2},{4,5},{5,4},{6,7},{7,6},{8,9},{9,8},{10,11... | collective-permute-start | bytes 1572872 | tf_op jit(solution)/shard_map/ppermute | solution.py:35
  59.4 10.6 %collective-permute-start.13 = (f32[2,80,512]{2,1,0:T(8,128)S(1)}, f32[2,80,512]{2,1,0:T(8,128)S(1)}, u32[]{:S(2)}, u32[]{:S(2)}) collective-permute-start(f32[2,80,512]{2,1,0:T(8,128)S(1)} %extend.1.own), channel_id=1, source_target_pairs={{8,0},{16,8},{24,16},{0,24},{9,1},{17,9},{25,17},{1,25},{10,2},{18... | collective-permute-start | bytes 983048 | tf_op jit(solution)/shard_map/ppermute | solution.py:296
  61.7 15.6 %collective-permute-start.12 = (f32[2,80,512]{2,1,0:T(8,128)S(1)}, f32[2,80,512]{2,1,0:T(8,128)S(1)}, u32[]{:S(2)}, u32[]{:S(2)}) collective-permute-start(f32[2,80,512]{2,1,0:T(8,128)S(1)} %extend.1.own), channel_id=1, source_target_pairs={{0,8},{8,16},{16,24},{24,0},{1,9},{9,17},{17,25},{25,1},{2,10},{10... | collective-permute-start | bytes 983048 | tf_op jit(solution)/shard_map/ppermute | solution.py:295
  62.7 15.1 %collective-permute-start.15 = (f32[2,2,32,512]{3,2,1,0:T(8,128)S(1)}, f32[2,2,32,512]{3,2,1,0:T(8,128)S(1)}, u32[]{:S(2)}, u32[]{:S(2)}) collective-permute-start(f32[2,2,32,512]{3,2,1,0:T(8,128)S(1)} %slice.53), channel_id=1, source_target_pairs={{0,2},{1,3},{2,0},{3,1},{4,6},{5,7},{6,4},{7,5},{8,10},{9,11},{10,... | collective-permute-start | bytes 786440 | tf_op jit(solution)/shard_map/ppermute | solution.py:35
  63.8 15.9 %collective-permute-start.18 = (f32[2,2,32,512]{3,2,1,0:T(8,128)S(1)}, f32[2,2,32,512]{3,2,1,0:T(8,128)S(1)}, u32[]{:S(2)}, u32[]{:S(2)}) collective-permute-start(f32[2,2,32,512]{3,2,1,0:T(8,128)S(1)} %slice.57), channel_id=1, source_target_pairs={{0,2},{1,3},{2,0},{3,1},{4,6},{5,7},{6,4},{7,5},{8,10},{9,11},{10,... | collective-permute-start | bytes 786440 | tf_op jit(solution)/shard_map/ppermute | solution.py:35
  77.9 12.8 %collective-permute-start.16 = (f32[1,2,32,512]{3,2,1,0:T(8,128)S(1)}, f32[1,2,32,512]{3,2,1,0:T(8,128)S(1)}, u32[]{:S(2)}, u32[]{:S(2)}) collective-permute-start(f32[1,2,32,512]{3,2,1,0:T(8,128)S(1)} %slice.55), channel_id=1, source_target_pairs={{0,4},{1,5},{2,6},{3,7},{4,0},{5,1},{6,2},{7,3},{8,12},{9,13},{10,... | collective-permute-start | bytes 393224 | tf_op jit(solution)/shard_map/ppermute | solution.py:35
  79.7 12.7 %collective-permute-start.19 = (f32[1,2,32,512]{3,2,1,0:T(8,128)S(1)}, f32[1,2,32,512]{3,2,1,0:T(8,128)S(1)}, u32[]{:S(2)}, u32[]{:S(2)}) collective-permute-start(f32[1,2,32,512]{3,2,1,0:T(8,128)S(1)} %slice.59), channel_id=1, source_target_pairs={{0,4},{1,5},{2,6},{3,7},{4,0},{5,1},{6,2},{7,3},{8,12},{9,13},{10,... | collective-permute-start | bytes 393224 | tf_op jit(solution)/shard_map/ppermute | solution.py:35
  (2 other events, 2.6 us)

commit v2 on v1

v2 whole, which is shorter than its diff:
```python
from functools import partial
import math

import jax
import jax.numpy as jnp
import ml_dtypes
import numpy as np
from jax import lax
from jax.experimental import pallas as pl
from jax.experimental.pallas import tpu as pltpu
from jax.sharding import PartitionSpec as P

STEP_SIZE = 0.25
TV_WEIGHT = 0.5
TV_SMOOTH = 0.25
CHUNKS = (5, 3)
PARTS = (2, 2)

F32 = jnp.float32
BF16 = jnp.bfloat16
VMEM = pl.BlockSpec(memory_space=pltpu.VMEM)
ANY = pl.BlockSpec(memory_space=pl.ANY)
SMEM = pl.BlockSpec(memory_space=pltpu.SMEM)
PARAMS = pltpu.CompilerParams(vmem_limit_bytes=24 * 2**20)


def dft_table(length):
    indices = np.arange(length, dtype=np.int64)
    angles = (indices[:, None] * indices[None, :] % length) * (2.0 * math.pi / length)
    factor = 1.0 / math.sqrt(length)
    table = np.concatenate([-np.sin(angles) * factor, np.cos(angles) * factor])
    return table.astype(ml_dtypes.bfloat16)


def bit_orders(count):
    top = count.bit_length() - 2
    return list(range(1, top + 1)), list(range(top, 0, -1))


def swap_cores(value):
    count = lax.axis_size("coil")
    return lax.ppermute(value, "coil", [(i, i ^ 1) for i in range(count)])


def swap_chips(value, step):
    count = lax.axis_size("coil")
    orders = bit_orders(count)
    return lax.ppermute(
        value, "coil", [(i, i ^ (1 << orders[i & 1][step])) for i in range(count)]
    )


def by_core(device, flip, values):
    return jnp.where((device & 1) ^ flip == 0, values[0], values[1])


def halving_order(steps):
    places = [0]
    for step in reversed(range(steps)):
        places = places + [place | (1 << step) for place in places]
    return places


def flops(cost):
    return pl.CostEstimate(flops=cost, bytes_accessed=4 * 2**20, transcendentals=0)


def adjoint_kernel(groups, me, table, data, sens, ready, *refs):
    del ready
    outs, (lhs, rhs) = refs[: len(groups)], refs[len(groups) :]
    length = sens.shape[1]
    device = me[0]
    blocks, at = [], 0
    for out, group in zip(outs, groups):
        for place, (start, size) in enumerate(group):
            blocks.append((out, place, at, pl.multiple_of(start(device), 16), size))
            at += size
    total = at
    for _, _, at, start, size in blocks:
        sine = table[pl.ds(start, size), :]
        cosine = table[pl.ds(pl.multiple_of(length + start, 16), size), :]
        lhs[at : at + size, :length] = cosine
        lhs[at : at + size, length:] = sine
        lhs[total + at : total + at + size, :length] = -sine
        lhs[total + at : total + at + size, length:] = cosine
    upper = jnp.dot(lhs[...], data[...], preferred_element_type=F32).astype(BF16)
    real, imag = upper[:total], upper[total:]
    rhs[:total, :length] = imag
    rhs[:total, length:] = real
    rhs[total:, :length] = -real
    rhs[total:, length:] = imag
    back = jnp.dot(rhs[...], table[...], preferred_element_type=F32)
    for out, place, at, start, size in blocks:
        rows = pl.ds(start, size)
        real, imag = back[at : at + size], back[total + at : total + at + size]
        sens_real, sens_imag = sens[0, rows, :].astype(F32), sens[1, rows, :].astype(F32)
        out[place, 0] = sens_real * real + sens_imag * imag
        out[place, 1] = sens_real * imag - sens_imag * real


def adjoint(groups, me, table, data, sens, ready=None):
    length = sens.shape[1]
    total = sum(size for group in groups for _, size in group)
    return pl.pallas_call(
        partial(adjoint_kernel, groups),
        out_shape=[
            jax.ShapeDtypeStruct((len(group), 2, group[0][1], length), F32) for group in groups
        ],
        in_specs=[SMEM, VMEM, VMEM, VMEM, ANY],
        out_specs=[VMEM] * len(groups),
        scratch_shapes=[pltpu.VMEM((2 * total, 2 * length), BF16)] * 2,
        compiler_params=PARAMS,
        cost_estimate=flops(16 * total * length * length),
        name="adjoint",
    )(me, table, data.reshape(2 * length, length), sens, me if ready is None else ready)


def columns_kernel(blocks, me, table, out, rows):
    length = out.shape[0]
    total = sum(size for _, size in blocks)
    at = 0
    for start, size in blocks:
        row = pl.multiple_of(start(me[0]), 16)
        rows[at : at + size, :] = table[pl.ds(pl.multiple_of(length + row, 16), size), :]
        rows[total + at : total + at + size, :] = table[pl.ds(row, size), :]
        at += size
    out[...] = rows[...].T


def columns(blocks, me, table):
    length = table.shape[1]
    total = 2 * sum(size for _, size in blocks)
    return pl.pallas_call(
        partial(columns_kernel, blocks),
        out_shape=jax.ShapeDtypeStruct((length, total), BF16),
        in_specs=[SMEM, VMEM],
        out_specs=VMEM,
        scratch_shapes=[pltpu.VMEM((total, length), BF16)],
        compiler_params=PARAMS,
        name="columns",
    )(me, table)


def forward_kernel(blocks, last, me, table, left, sens, *refs):
    pieces, refs = refs[: len(blocks)], refs[len(blocks) :]
    if last:
        before, kspace, sampling, out, lhs, mid = refs
    else:
        out, lhs, mid = refs
    length = sens.shape[1]
    total = sum(size for _, size in blocks)
    at = 0
    for (start, size), piece in zip(blocks, pieces):
        place = pl.ds(pl.multiple_of(start(me[0]), 16), size)
        real, imag = piece[0], piece[1]
        sens_real, sens_imag = sens[0, place, :].astype(F32), sens[1, place, :].astype(F32)
        coil_real = (sens_real * real - sens_imag * imag).astype(BF16)
        coil_imag = (sens_real * imag + sens_imag * real).astype(BF16)
        top, bottom = pl.ds(at, size), pl.ds(total + at, size)
        lhs[top, :length] = -coil_imag
        lhs[top, length:] = coil_real
        lhs[bottom, :length] = coil_real
        lhs[bottom, length:] = coil_imag
        at += size
    middle = jnp.dot(lhs[...], table[...], preferred_element_type=F32).astype(BF16)
    mid[:total, :length] = middle[:total]
    mid[:total, length:] = middle[total:]
    mid[total:, :length] = -middle[total:]
    mid[total:, length:] = middle[:total]
    freq = jnp.dot(left[...], mid[...], preferred_element_type=F32)
    if last:
        freq += before[...]
        weight = sampling[...].astype(F32)
        out[0] = (weight * (freq[:, :length] - kspace[0].astype(F32))).astype(BF16)
        out[1] = (weight * (freq[:, length:] - kspace[1].astype(F32))).astype(BF16)
    else:
        out[...] = freq


def forward(blocks, me, table, sens, pieces, rest=()):
    length = sens.shape[1]
    total = sum(size for _, size in blocks)
    left = columns(blocks, me, table)
    freq = jax.ShapeDtypeStruct((length, 2 * length), F32)
    resid = jax.ShapeDtypeStruct((2, length, length), BF16)
    return pl.pallas_call(
        partial(forward_kernel, blocks, bool(rest)),
        out_shape=resid if rest else freq,
        in_specs=[SMEM] + [VMEM] * (3 + len(pieces) + len(rest)),
        out_specs=VMEM,
        scratch_shapes=[pltpu.VMEM((2 * total, 2 * length), BF16)] * 2,
        compiler_params=PARAMS,
        cost_estimate=flops(16 * total * length * length),
        name="forward",
    )(me, table, left, sens, *pieces, *rest)


def extend_kernel(blocks, me, ready, *refs):
    del ready
    pieces, (out, volume) = refs[:-2], refs[-2:]
    length = volume.shape[1]
    own = out.shape[1] - 16
    for (start, size), piece in zip(blocks, pieces):
        volume[:, pl.ds(pl.multiple_of(start(me[0]), 16), size), :] = piece[...]
    first = me[0] * own
    for at, row, count in (
        (0, (first + length - 8) & (length - 1), 8),
        (8, first, own),
        (8 + own, (first + own) & (length - 1), 8),
    ):
        out[:, at : at + count, :] = volume[:, pl.ds(pl.multiple_of(row, 8), count), :]


def tv_kernel(own, before, after, *refs):
    out = refs[-1]
    size = out.shape[1]
    length = out.shape[2]

    def parts(ref, first, count):
        return [ref[part, first : first + count, :] for part in (0, 1)]

    def next_column(values):
        return [pltpu.roll(value, length - 1, 1) for value in values]

    def minus(left, right):
        return [a - b for a, b in zip(left, right)]

    def fluxes(here, slices, rows):
        columns = minus(next_column(here), here)
        squares = TV_SMOOTH
        for change in (slices, rows, columns):
            squares = squares + (change[0] * change[0] + change[1] * change[1])
        weight = lax.rsqrt(squares)
        return [[weight * value for value in change] for change in (slices, rows, columns)]

    count = size + 1
    here = parts(own, 7, count)
    slices, rows, columns = fluxes(
        here, minus(parts(after, 7, count), here), minus(parts(own, 8, count), here)
    )
    back = parts(before, 8, size)
    center = parts(own, 8, size)
    back_slices, _, _ = fluxes(back, minus(center, back), minus(parts(before, 9, size), back))
    for part in (0, 1):
        col = columns[part][1:]
        tv = (
            (back_slices[part] - slices[part][1:])
            + (rows[part][:-1] - rows[part][1:])
            + (pltpu.roll(col, 1, 1) - col)
        )
        out[part] = center[part] - (STEP_SIZE * TV_WEIGHT) * tv


def shards(kspace, sensitivity, sampling):
    kspace, sens, sampling = kspace[0, 0], sensitivity[0, 0], sampling[0]
    length = sampling.shape[0]
    count = lax.axis_size("coil")
    slabs = lax.axis_size("slab")
    top = count.bit_length() - 2
    size = length // count
    half = count // 2
    table = jnp.asarray(dft_table(length))
    me = lax.axis_index("coil").astype(jnp.int32).reshape(1)

    measured = kspace * sampling.astype(BF16)[None]

    orders = bit_orders(count)
    eighth = length // 8
    chunks = CHUNKS if eighth % (16 * half) == 0 or half <= 4 else (4, 4)
    chunks = [rows * eighth for rows in chunks]

    def chunk_block(chunk, flip, place):
        size = chunks[chunk] // half

        def start(device):
            own = [
                sum(((device >> bit) & 1) << step for step, bit in enumerate(order[:-1]))
                for order in orders
            ]
            block = (by_core(device, flip, own) ^ place) * 2 + ((device & 1) ^ flip)
            return sum(chunks[:chunk]) + block * size

        return start, size

    places = halving_order(top - 1)
    groups = [
        [[chunk_block(chunk, flip, place) for place in places] for chunk in range(len(chunks))]
        for flip in (1, 0)
    ]
    others = adjoint(groups[0], me, table, measured, sens)
    owns = adjoint(groups[1], me, table, measured, sens, others[0])
    currents = [own + swap_cores(other) for own, other in zip(owns, others)]
    arrived = []
    for current in currents:
        for step in range(top - 1):
            middle = current.shape[0] // 2
            current = current[:middle] + swap_chips(current[middle:], step)
        current = current[0]
        pieces = {0: current + swap_chips(current, top - 1)}
        for step in reversed(range(top - 1)):
            for place in list(pieces):
                pieces[place | (1 << step)] = swap_chips(pieces[place], step)
        arrived.append(pieces)
    early = [
        (chunk_block(chunk, flip, 0), swap_cores(pieces[0]) if flip else pieces[0])
        for chunk, pieces in enumerate(arrived)
        for flip in (0, 1)
    ]
    freq = forward([b for b, _ in early], me, table, sens, [p for _, p in early])
    late = []
    for chunk, pieces in enumerate(arrived):
        for place in range(1, half // 2):
            piece, freq = lax.optimization_barrier((pieces[place], freq))
            late.append((chunk_block(chunk, 0, place), piece))
            late.append((chunk_block(chunk, 1, place), swap_cores(piece)))
    resid = forward(
        [b for b, _ in late], me, table, sens, [p for _, p in late], [freq, kspace, sampling]
    )

    parts = [part * size // 4 for part in PARTS] if size >= 64 else [size]

    def row_block(part, flip, place):
        masks = [
            sum(((place >> step) & 1) << bit for step, bit in enumerate(order)) for order in orders
        ]
        first = sum(parts[:part])
        return (
            lambda device: (device ^ flip ^ by_core(device, flip, masks)) * size + first,
            parts[part],
        )

    places = halving_order(top)
    groups = [
        [[row_block(part, flip, place) for place in places] for part in range(len(parts))]
        for flip in (1, 0)
    ]
    others = adjoint(groups[0], me, table, resid, sens)
    owns = adjoint(groups[1], me, table, resid, sens, others[0])
    summed = [own + swap_cores(other) for own, other in zip(owns, others)]
    gradient, halves = [], []
    for current in summed:
        for step in range(top):
            middle = current.shape[0] // 2
            current = current[:middle] + swap_chips(current[middle:], step)
            halves.append(current)
        gradient.append(current[0])

    extended = pl.pallas_call(
        partial(extend_kernel, [b for b, _ in early + late]),
        out_shape=jax.ShapeDtypeStruct((2, size + 16, length), F32),
        in_specs=[SMEM, ANY] + [VMEM] * len(early + late),
        out_specs=VMEM,
        scratch_shapes=[pltpu.VMEM((2, length, length), F32)],
        compiler_params=PARAMS,
        name="extend",
    )(me, summed[-1], *[p for _, p in early + late])
    ahead = [(i, (i + 1) % slabs) for i in range(slabs)]
    behind = [(target, source) for source, target in ahead]
    before = lax.ppermute(extended, "slab", ahead)
    after = lax.ppermute(extended, "slab", behind)
    base = pl.pallas_call(
        tv_kernel,
        out_shape=jax.ShapeDtypeStruct((2, size, length), F32),
        in_specs=[VMEM, VMEM, VMEM] + [ANY] * len(parts),
        out_specs=VMEM,
        compiler_params=PARAMS,
        name="total_variation",
    )(extended, before, after, *halves[::top])
    return (base - STEP_SIZE * jnp.concatenate(gradient, axis=1))[None]


def solution(mesh):
    placed = (
        P("slab", "coil", None, None, None),
        P("slab", "coil", None, None, None),
        P("slab", None, None),
    )
    return jax.shard_map(
        shards, mesh=mesh, in_specs=placed, out_specs=P("slab", None, "coil", None), check_vma=False
    )
```

time: 93.3 us -> 77.2 us (0.83)
  waiting for transfers between devices: 58.9 us -> 38 us
  starting transfers between devices: 18.9 us -> 25.8 us
  local copies, waits for them, and re-layouts: 2.72 us -> 0.55 us
  other arithmetic: 1.33 us -> 3.04 us
  Pallas kernels: 11 us -> 9.47 us
    ppermute x18, waiting for transfers between devices: 47.4 us -> 36 us  [the longest x10 34.8 us: swap_chips(): lax.ppermute(value, 'coil', [(i, i ^ 1 << orders[i & 1][step]) for i in r...]
    ppermute x18, starting transfers between devices: 16.6 us -> 23.3 us  [the longest x10 18.9 us: swap_chips(): lax.ppermute(value, 'coil', [(i, i ^ 1 << orders[i & 1][step]) for i in r...]
    ppermute x1, waiting for transfers between devices: 7.39 us -> 2 us  [shards(): before = lax.ppermute(extended, 'slab', ahead)]
    ppermute x1, waiting for transfers between devices: 4.1 us -> 0.01 us  [shards(): after = lax.ppermute(extended, 'slab', behind)]
    unnamed x12 -> x8, local copies, waits for them, and re-layouts: 2.62 us -> 0.46 us
    mul x0 -> x2, other arithmetic: none -> 1.71 us  [shards(): measured = kspace * sampling.astype(BF16)[None]]
    pallas_call x11 -> x9, Pallas kernels: 10.5 us -> 8.98 us  [the longest x4 5.55 us: adjoint(): pl.pallas_call(partial(adjoint_kernel, groups), out_shape=[jax.ShapeDtype...]
  transfers between devices with their start and end apart: 20 -> 20, of which waited for: 10 -> 12; matrix products, arithmetic and copies ran while one was open for 1% -> 1% of each run, Pallas kernels for 8% -> 7%
where the time goes in v2:
time: 77.2 us; the launch traced here: 77.1 us
  waiting for transfers between devices  38 us (49%)
  starting transfers between devices  25.8 us (33%)
  Pallas kernels  9.47 us (12%)
  other arithmetic  3.04 us (4%)
    ppermute x10, waiting for transfers between devices, swap_chips(): lax.ppermute(value, 'coil', [(i, i ^ 1 << orders[i & 1][step]) for i in r...  34.8 us
    ppermute x10, starting transfers between devices, swap_chips(): lax.ppermute(value, 'coil', [(i, i ^ 1 << orders[i & 1][step]) for i in r...  18.9 us
    pallas_call x4, Pallas kernels, adjoint(): pl.pallas_call(partial(adjoint_kernel, groups), out_shape=[jax.ShapeDtype...  5.55 us
    ppermute x8, starting transfers between devices, swap_cores(): return lax.ppermute(value, 'coil', [(i, i ^ 1) for i in range(count)])  4.4 us
    pallas_call x2, Pallas kernels, forward(): pl.pallas_call(partial(forward_kernel, blocks, bool(rest)), out_shape=res...  2.89 us
    ppermute x1, starting transfers between devices, shards(): after = lax.ppermute(extended, 'slab', behind)  2.5 us
    ppermute x1, waiting for transfers between devices, shards(): before = lax.ppermute(extended, 'slab', ahead)  2 us
    mul x2, other arithmetic, shards(): measured = kspace * sampling.astype(BF16)[None]  1.71 us
  transfers between devices with their start and end apart: 20, of which 12 were waited for; matrix products, arithmetic and copies ran while one was open for 1% of the time, Pallas kernels for 7%

profile of v2, /device:TPU:0, one launch (start us, length us, event | category | flops | bytes accessed | tf_op | source)
XLA Modules:
  0.0 77.1 jit_solution(2861881507934812663)
XLA Ops:
  0.0 1.5 %convert_bitcast_fusion = bf16[512,512]{1,0:T(8,128)(2,1)S(1)} fusion(s32[1,512,512]{2,1,0:T(8,128)} %param.6), kind=kLoop, calls=%fused_computation.1 | loop fusion | flops 262144 | bytes 1572864 | tf_op jit(solution)/shard_map/mul | solution.py:265
  2.2 1.4 %adjoint.4 = (f32[2,2,80,512]{3,2,1,0:T(8,128)S(1)}, f32[2,2,48,512]{3,2,1,0:T(8,128)S(1)}) custom-call(s32[1]{0:T(128)} %bitcast.me.ready, bf16[1024,512]{1,0:T(8,128)(2,1)S(1)} %copy-done, bf16[1024,512]{1,0:T(8,128)(2,1)S(1)} %bitcast_multiply_fusion.data, bf16[2,512,512]{2,1,0:T(8,128)(2,1)S(1)} %bitcast.23, s32[1]{0:T(128)} %bitcast.me.ready), custom_call_target="tpu_custom_call" | custom-call | flops 1073741824 | bytes 4194304 | tf_op jit(solution)/shard_map/adjoint/pallas_call | solution.py:104
  4.2 1.4 %adjoint.5 = (f32[2,2,80,512]{3,2,1,0:T(8,128)S(1)}, f32[2,2,48,512]{3,2,1,0:T(8,128)S(1)}) custom-call(s32[1]{0:T(128)} %bitcast.me.ready, bf16[1024,512]{1,0:T(8,128)(2,1)S(1)} %copy-done, bf16[1024,512]{1,0:T(8,128)(2,1)S(1)} %bitcast_multiply_fusion.data, bf16[2,512,512]{2,1,0:T(8,128)(2,1)S(1)} %bitcast.24, f32[2,2,80,512]{3,2,1,0:T(8,128)S(1)} %get-tuple-element.17.ready), custom_call_target="tpu_custom_call" | custom-call | flops 1073741824 | bytes 4194304 | tf_op jit(solution)/shard_map/adjoint/pallas_call | solution.py:104
  6.0 3.0 %collective-permute-start.1 = (f32[1,2,80,512]{3,2,1,0:T(8,128)S(1)}, f32[1,2,80,512]{3,2,1,0:T(8,128)S(1)}, u32[]{:S(2)}, u32[]{:S(2)}) collective-permute-start(f32[1,2,80,512]{3,2,1,0:T(8,128)S(1)} %slice.49), channel_id=1, source_target_pairs={{0,2},{1,5},{2,0},{3,7},{4,6},{5,1},{6,4},{7,3},{8,10},{9,13},{10,... | collective-permute-start | bytes 983048 | tf_op jit(solution)/shard_map/ppermute | solution.py:48
  9.5 7.7 %collective-permute-done.1 = f32[1,2,80,512]{3,2,1,0:T(8,128)S(1)} collective-permute-done((f32[1,2,80,512]{3,2,1,0:T(8,128)S(1)}, f32[1,2,80,512]{3,2,1,0:T(8,128)S(1)}, u32[]{:S(2)}, u32[]{:S(2)}) %collective-permute-start.1) | collective-permute-done | bytes 327712 | tf_op jit(solution)/shard_map/ppermute | solution.py:48
  17.2 3.5 %collective-permute-start.2 = (f32[2,80,512]{2,1,0:T(8,128)S(1)}, f32[2,80,512]{2,1,0:T(8,128)S(1)}, u32[]{:S(2)}, u32[]{:S(2)}) collective-permute-start(f32[2,80,512]{2,1,0:T(8,128)S(1)} %fusion), channel_id=1, source_target_pairs={{0,4},{1,3},{2,6},{3,1},{4,0},{5,7},{6,2},{7,5},{8,12},{9,11},{10,... | collective-permute-start | bytes 983048 | tf_op jit(solution)/shard_map/ppermute | solution.py:48
  20.7 1.4 %collective-permute-done.6 = f32[1,2,48,512]{3,2,1,0:T(8,128)S(1)} collective-permute-done((f32[1,2,48,512]{3,2,1,0:T(8,128)S(1)}, f32[1,2,48,512]{3,2,1,0:T(8,128)S(1)}, u32[]{:S(2)}, u32[]{:S(2)}) %collective-permute-start.6) | collective-permute-done | bytes 196640 | tf_op jit(solution)/shard_map/ppermute | solution.py:48
  22.1 2.5 %collective-permute-start.7 = (f32[2,48,512]{2,1,0:T(8,128)S(1)}, f32[2,48,512]{2,1,0:T(8,128)S(1)}, u32[]{:S(2)}, u32[]{:S(2)}) collective-permute-start(f32[2,48,512]{2,1,0:T(8,128)S(1)} %fusion.3), channel_id=1, source_target_pairs={{0,4},{1,3},{2,6},{3,1},{4,0},{5,7},{6,2},{7,5},{8,12},{9,11},{10,... | collective-permute-start | bytes 589832 | tf_op jit(solution)/shard_map/ppermute | solution.py:48
  24.6 4.2 %collective-permute-done.2 = f32[2,80,512]{2,1,0:T(8,128)S(1)} collective-permute-done((f32[2,80,512]{2,1,0:T(8,128)S(1)}, f32[2,80,512]{2,1,0:T(8,128)S(1)}, u32[]{:S(2)}, u32[]{:S(2)}) %collective-permute-start.2) | collective-permute-done | bytes 327712 | tf_op jit(solution)/shard_map/ppermute | solution.py:48
  30.0 1.7 %collective-permute-start.3 = (f32[2,80,512]{2,1,0:T(8,128)S(1)}, f32[2,80,512]{2,1,0:T(8,128)S(1)}, u32[]{:S(2)}, u32[]{:S(2)}) collective-permute-start(f32[2,80,512]{2,1,0:T(8,128)S(1)} %add.38.refs_0_), channel_id=1, source_target_pairs={{0,2},{1,5},{2,0},{3,7},{4,6},{5,1},{6,4},{7,3},{8,10},{9,13},{10,... | collective-permute-start | bytes 983048 | tf_op jit(solution)/shard_map/ppermute | solution.py:48
  33.1 2.5 %collective-permute-start.10 = (f32[2,48,512]{2,1,0:T(8,128)S(1)}, f32[2,48,512]{2,1,0:T(8,128)S(1)}, u32[]{:S(2)}, u32[]{:S(2)}) collective-permute-start(f32[2,48,512]{2,1,0:T(8,128)S(1)} %add.41.refs_2_), channel_id=1, source_target_pairs={{0,2},{1,5},{2,0},{3,7},{4,6},{5,1},{6,4},{7,3},{8,10},{9,13},{10,... | collective-permute-start | bytes 589832 | tf_op jit(solution)/shard_map/ppermute | solution.py:48
  35.6 1.4 %forward.2.refs_4_ = f32[512,1024]{1,0:T(8,128)S(1)} custom-call(s32[1]{0:T(128)} %bitcast.me.ready, bf16[1024,512]{1,0:T(8,128)(2,1)S(1)} %copy-done, bf16[512,512]{1,0:T(8,128)(2,1)S(1)} %columns.3.left, bf16[2,512,512]{2,1,0:T(8,128)(2,1)S(1)} %bitcast.25, f32[2,80,512]{2,1,0:T(8,128)S(1)} %add.38.refs_0_, ...), custom_call_target="tpu_custom_call" | custom-call | flops 1073741824 | bytes 4194304 | tf_op jit(solution)/shard_map/forward/pallas_call | solution.py:186
  36.9 3.1 %collective-permute-done.3.refs_0_.refs_4_ = f32[2,80,512]{2,1,0:T(8,128)S(1)} collective-permute-done((f32[2,80,512]{2,1,0:T(8,128)S(1)}, f32[2,80,512]{2,1,0:T(8,128)S(1)}, u32[]{:S(2)}, u32[]{:S(2)}) %collective-permute-start.3) | collective-permute-done | bytes 327712 | tf_op jit(solution)/shard_map/ppermute | solution.py:48
  40.9 3.3 %collective-permute-done.10.refs_2_.refs_6_ = f32[2,48,512]{2,1,0:T(8,128)S(1)} collective-permute-done((f32[2,48,512]{2,1,0:T(8,128)S(1)}, f32[2,48,512]{2,1,0:T(8,128)S(1)}, u32[]{:S(2)}, u32[]{:S(2)}) %collective-permute-start.10) | collective-permute-done | bytes 196640 | tf_op jit(solution)/shard_map/ppermute | solution.py:48
  46.2 1.5 %forward.3 = bf16[2,512,512]{2,1,0:T(8,128)(2,1)S(1)} custom-call(s32[1]{0:T(128)} %bitcast.me.ready, bf16[1024,512]{1,0:T(8,128)(2,1)S(1)} %copy-done, bf16[512,512]{1,0:T(8,128)(2,1)S(1)} %columns.2.left, bf16[2,512,512]{2,1,0:T(8,128)(2,1)S(1)} %bitcast.26, f32[2,80,512]{2,1,0:T(8,128)S(1)} %collective-permute-done.3.refs_0_.refs_4_, ...), custom_call_target="tpu_custom_call" | custom-call | flops 1073741824 | bytes 4194304 | tf_op jit(solution)/shard_map/forward/pallas_call | solution.py:186
  47.8 1.4 %adjoint.6 = (f32[4,2,32,512]{3,2,1,0:T(8,128)S(1)}, f32[4,2,32,512]{3,2,1,0:T(8,128)S(1)}) custom-call(s32[1]{0:T(128)} %bitcast.me.ready, bf16[1024,512]{1,0:T(8,128)(2,1)S(1)} %copy-done, bf16[1024,512]{1,0:T(8,128)(2,1)S(1)} %bitcast.29, bf16[2,512,512]{2,1,0:T(8,128)(2,1)S(1)} %bitcast.27, s32[1]{0:T(128)} %bitcast.me.ready), custom_call_target="tpu_custom_call" | custom-call | flops 1073741824 | bytes 4194304 | tf_op jit(solution)/shard_map/adjoint/pallas_call | solution.py:104
  49.7 1.4 %adjoint.7 = (f32[4,2,32,512]{3,2,1,0:T(8,128)S(1)}, f32[4,2,32,512]{3,2,1,0:T(8,128)S(1)}) custom-call(s32[1]{0:T(128)} %bitcast.me.ready, bf16[1024,512]{1,0:T(8,128)(2,1)S(1)} %copy-done, bf16[1024,512]{1,0:T(8,128)(2,1)S(1)} %bitcast.30, bf16[2,512,512]{2,1,0:T(8,128)(2,1)S(1)} %bitcast.28, f32[4,2,32,512]{3,2,1,0:T(8,128)S(1)} %get-tuple-element.25.ready), custom_call_target="tpu_custom_call" | custom-call | flops 1073741824 | bytes 4194304 | tf_op jit(solution)/shard_map/adjoint/pallas_call | solution.py:104
  51.3 1.6 %collective-permute-start.17 = (f32[2,2,32,512]{3,2,1,0:T(8,128)S(1)}, f32[2,2,32,512]{3,2,1,0:T(8,128)S(1)}, u32[]{:S(2)}, u32[]{:S(2)}) collective-permute-start(f32[2,2,32,512]{3,2,1,0:T(8,128)S(1)} %slice.55), channel_id=1, source_target_pairs={{0,2},{1,5},{2,0},{3,7},{4,6},{5,1},{6,4},{7,3},{8,10},{9,13},{10,... | collective-permute-start | bytes 786440 | tf_op jit(solution)/shard_map/ppermute | solution.py:48
  53.7 2.5 %collective-permute-start.14 = (f32[2,80,512]{2,1,0:T(8,128)S(1)}, f32[2,80,512]{2,1,0:T(8,128)S(1)}, u32[]{:S(2)}, u32[]{:S(2)}) collective-permute-start(f32[2,80,512]{2,1,0:T(8,128)S(1)} %extend.1.own), channel_id=1, source_target_pairs={{8,0},{16,8},{24,16},{0,24},{9,1},{17,9},{25,17},{1,25},{10,2},{18... | collective-permute-start | bytes 983048 | tf_op jit(solution)/shard_map/ppermute | solution.py:360
  56.2 4.3 %collective-permute-done.17 = f32[2,2,32,512]{3,2,1,0:T(8,128)S(1)} collective-permute-done((f32[2,2,32,512]{3,2,1,0:T(8,128)S(1)}, f32[2,2,32,512]{3,2,1,0:T(8,128)S(1)}, u32[]{:S(2)}, u32[]{:S(2)}) %collective-permute-start.17) | collective-permute-done | bytes 262176 | tf_op jit(solution)/shard_map/ppermute | solution.py:48
  60.5 2.1 %collective-permute-start.19 = (f32[1,2,32,512]{3,2,1,0:T(8,128)S(1)}, f32[1,2,32,512]{3,2,1,0:T(8,128)S(1)}, u32[]{:S(2)}, u32[]{:S(2)}) collective-permute-start(f32[1,2,32,512]{3,2,1,0:T(8,128)S(1)} %slice.59), channel_id=1, source_target_pairs={{0,4},{1,3},{2,6},{3,1},{4,0},{5,7},{6,2},{7,5},{8,12},{9,11},{10,... | collective-permute-start | bytes 393224 | tf_op jit(solution)/shard_map/ppermute | solution.py:48
  62.6 6.3 %collective-permute-done.16 = f32[2,2,32,512]{3,2,1,0:T(8,128)S(1)} collective-permute-done((f32[2,2,32,512]{3,2,1,0:T(8,128)S(1)}, f32[2,2,32,512]{3,2,1,0:T(8,128)S(1)}, u32[]{:S(2)}, u32[]{:S(2)}) %collective-permute-start.16) | collective-permute-done | bytes 262176 | tf_op jit(solution)/shard_map/ppermute | solution.py:48
  70.1 2.0 %collective-permute-done.13.before = f32[2,80,512]{2,1,0:T(8,128)S(1)} collective-permute-done((f32[2,80,512]{2,1,0:T(8,128)S(1)}, f32[2,80,512]{2,1,0:T(8,128)S(1)}, u32[]{:S(2)}, u32[]{:S(2)}) %collective-permute-start.13) | collective-permute-done | bytes 327712 | tf_op jit(solution)/shard_map/ppermute | solution.py:359
  72.6 3.7 %collective-permute-done.18 = f32[1,2,32,512]{3,2,1,0:T(8,128)S(1)} collective-permute-done((f32[1,2,32,512]{3,2,1,0:T(8,128)S(1)}, f32[1,2,32,512]{3,2,1,0:T(8,128)S(1)}, u32[]{:S(2)}, u32[]{:S(2)}) %collective-permute-start.18) | collective-permute-done | bytes 131104 | tf_op jit(solution)/shard_map/ppermute | solution.py:48
  (55 shorter events, 11.6 us)
Async XLA Ops:
  0.0 1.5 %copy-start.1 = (bf16[1,1,2,512,512]{4,3,2,1,0:T(8,128)(2,1)S(1)}, bf16[1,1,2,512,512]{4,3,2,1,0:T(8,128)(2,1)}, u32[]{:S(2)}) copy-start(bf16[1,1,2,512,512]{4,3,2,1,0:T(8,128)(2,1)} %param.4) | copy-start | bytes 3145732
  0.0 1.9 %copy-start = (bf16[1024,512]{1,0:T(8,128)(2,1)S(1)}, bf16[1024,512]{1,0:T(8,128)(2,1)}, u32[]{:S(2)}) copy-start(bf16[1024,512]{1,0:T(8,128)(2,1)} %constant.8.clone.table) | copy-start | bytes 3145732
  0.0 2.2 %copy-start.3 = (bf16[1,1,2,512,512]{4,3,2,1,0:T(8,128)(2,1)S(1)}, bf16[1,1,2,512,512]{4,3,2,1,0:T(8,128)(2,1)}, u32[]{:S(2)}) copy-start(bf16[1,1,2,512,512]{4,3,2,1,0:T(8,128)(2,1)} %param.5) | copy-start | bytes 3145732
  3.6 2.2 %collective-permute-start = (f32[2,2,80,512]{3,2,1,0:T(8,128)S(1)}, f32[2,2,80,512]{3,2,1,0:T(8,128)S(1)}, u32[]{:S(2)}, u32[]{:S(2)}) collective-permute-start(f32[2,2,80,512]{3,2,1,0:T(8,128)S(1)} %get-tuple-element.17.ready), channel_id=1, source_target_pairs={{0,1},{1,0},{2,3},{3,2},{4,5},{5,4},{6,7},{7,6},{8,9},{9,8},{10,11... | collective-permute-start | bytes 1966088 | tf_op jit(solution)/shard_map/ppermute | solution.py:42
  4.1 4.9 %collective-permute-start.5 = (f32[2,2,48,512]{3,2,1,0:T(8,128)S(1)}, f32[2,2,48,512]{3,2,1,0:T(8,128)S(1)}, u32[]{:S(2)}, u32[]{:S(2)}) collective-permute-start(f32[2,2,48,512]{3,2,1,0:T(8,128)S(1)} %get-tuple-element.20), channel_id=1, source_target_pairs={{0,1},{1,0},{2,3},{3,2},{4,5},{5,4},{6,7},{7,6},{8,9},{9,8},{10,11... | collective-permute-start | bytes 1179656 | tf_op jit(solution)/shard_map/ppermute | solution.py:42
  6.0 11.2 %collective-permute-start.1 = (f32[1,2,80,512]{3,2,1,0:T(8,128)S(1)}, f32[1,2,80,512]{3,2,1,0:T(8,128)S(1)}, u32[]{:S(2)}, u32[]{:S(2)}) collective-permute-start(f32[1,2,80,512]{3,2,1,0:T(8,128)S(1)} %slice.49), channel_id=1, source_target_pairs={{0,2},{1,5},{2,0},{3,7},{4,6},{5,1},{6,4},{7,3},{8,10},{9,13},{10,... | collective-permute-start | bytes 983048 | tf_op jit(solution)/shard_map/ppermute | solution.py:48
  9.0 13.0 %collective-permute-start.6 = (f32[1,2,48,512]{3,2,1,0:T(8,128)S(1)}, f32[1,2,48,512]{3,2,1,0:T(8,128)S(1)}, u32[]{:S(2)}, u32[]{:S(2)}) collective-permute-start(f32[1,2,48,512]{3,2,1,0:T(8,128)S(1)} %slice.51), channel_id=1, source_target_pairs={{0,2},{1,5},{2,0},{3,7},{4,6},{5,1},{6,4},{7,3},{8,10},{9,13},{10,... | collective-permute-start | bytes 589832 | tf_op jit(solution)/shard_map/ppermute | solution.py:48
  17.2 11.7 %collective-permute-start.2 = (f32[2,80,512]{2,1,0:T(8,128)S(1)}, f32[2,80,512]{2,1,0:T(8,128)S(1)}, u32[]{:S(2)}, u32[]{:S(2)}) collective-permute-start(f32[2,80,512]{2,1,0:T(8,128)S(1)} %fusion), channel_id=1, source_target_pairs={{0,4},{1,3},{2,6},{3,1},{4,0},{5,7},{6,2},{7,5},{8,12},{9,11},{10,... | collective-permute-start | bytes 983048 | tf_op jit(solution)/shard_map/ppermute | solution.py:48
  22.1 10.4 %collective-permute-start.7 = (f32[2,48,512]{2,1,0:T(8,128)S(1)}, f32[2,48,512]{2,1,0:T(8,128)S(1)}, u32[]{:S(2)}, u32[]{:S(2)}) collective-permute-start(f32[2,48,512]{2,1,0:T(8,128)S(1)} %fusion.3), channel_id=1, source_target_pairs={{0,4},{1,3},{2,6},{3,1},{4,0},{5,7},{6,2},{7,5},{8,12},{9,11},{10,... | collective-permute-start | bytes 589832 | tf_op jit(solution)/shard_map/ppermute | solution.py:48
  28.9 6.7 %collective-permute-start.4 = (f32[2,80,512]{2,1,0:T(8,128)S(1)}, f32[2,80,512]{2,1,0:T(8,128)S(1)}, u32[]{:S(2)}, u32[]{:S(2)}) collective-permute-start(f32[2,80,512]{2,1,0:T(8,128)S(1)} %add.38.refs_0_), channel_id=1, source_target_pairs={{0,1},{1,0},{2,3},{3,2},{4,5},{5,4},{6,7},{7,6},{8,9},{9,8},{10,11... | collective-permute-start | bytes 983048 | tf_op jit(solution)/shard_map/ppermute | solution.py:42
  30.0 10.0 %collective-permute-start.3 = (f32[2,80,512]{2,1,0:T(8,128)S(1)}, f32[2,80,512]{2,1,0:T(8,128)S(1)}, u32[]{:S(2)}, u32[]{:S(2)}) collective-permute-start(f32[2,80,512]{2,1,0:T(8,128)S(1)} %add.38.refs_0_), channel_id=1, source_target_pairs={{0,2},{1,5},{2,0},{3,7},{4,6},{5,1},{6,4},{7,3},{8,10},{9,13},{10,... | collective-permute-start | bytes 983048 | tf_op jit(solution)/shard_map/ppermute | solution.py:48
  32.5 3.0 %collective-permute-start.8 = (f32[2,48,512]{2,1,0:T(8,128)S(1)}, f32[2,48,512]{2,1,0:T(8,128)S(1)}, u32[]{:S(2)}, u32[]{:S(2)}) collective-permute-start(f32[2,48,512]{2,1,0:T(8,128)S(1)} %add.41.refs_2_), channel_id=1, source_target_pairs={{0,1},{1,0},{2,3},{3,2},{4,5},{5,4},{6,7},{7,6},{8,9},{9,8},{10,11... | collective-permute-start | bytes 589832 | tf_op jit(solution)/shard_map/ppermute | solution.py:42
  33.1 11.2 %collective-permute-start.10 = (f32[2,48,512]{2,1,0:T(8,128)S(1)}, f32[2,48,512]{2,1,0:T(8,128)S(1)}, u32[]{:S(2)}, u32[]{:S(2)}) collective-permute-start(f32[2,48,512]{2,1,0:T(8,128)S(1)} %add.41.refs_2_), channel_id=1, source_target_pairs={{0,2},{1,5},{2,0},{3,7},{4,6},{5,1},{6,4},{7,3},{8,10},{9,13},{10,... | collective-permute-start | bytes 589832 | tf_op jit(solution)/shard_map/ppermute | solution.py:48
  36.9 9.3 %copy-start.2 = (s32[1,512,512]{2,1,0:T(8,128)S(1)}, s32[1,512,512]{2,1,0:T(8,128)}, u32[]{:S(2)}) copy-start(s32[1,512,512]{2,1,0:T(8,128)} %param.6) | copy-start | bytes 3145732
  40.0 6.2 %collective-permute-start.9 = (f32[2,80,512]{2,1,0:T(8,128)S(1)}, f32[2,80,512]{2,1,0:T(8,128)S(1)}, u32[]{:S(2)}, u32[]{:S(2)}) collective-permute-start(f32[2,80,512]{2,1,0:T(8,128)S(1)} %collective-permute-done.3.refs_0_.refs_4_), channel_id=1, source_target_pairs={{0,1},{1,0},{2,3},{3,2},{4,5},{5,4},{6,7},{7,6},{8,9},{9,8},{10,11... | collective-permute-start | bytes 983048 | tf_op jit(solution)/shard_map/ppermute | solution.py:42
  44.2 2.0 %collective-permute-start.11 = (f32[2,48,512]{2,1,0:T(8,128)S(1)}, f32[2,48,512]{2,1,0:T(8,128)S(1)}, u32[]{:S(2)}, u32[]{:S(2)}) collective-permute-start(f32[2,48,512]{2,1,0:T(8,128)S(1)} %collective-permute-done.10.refs_2_.refs_6_), channel_id=1, source_target_pairs={{0,1},{1,0},{2,3},{3,2},{4,5},{5,4},{6,7},{7,6},{8,9},{9,8},{10,11... | collective-permute-start | bytes 589832 | tf_op jit(solution)/shard_map/ppermute | solution.py:42
  49.2 2.0 %collective-permute-start.12 = (f32[4,2,32,512]{3,2,1,0:T(8,128)S(1)}, f32[4,2,32,512]{3,2,1,0:T(8,128)S(1)}, u32[]{:S(2)}, u32[]{:S(2)}) collective-permute-start(f32[4,2,32,512]{3,2,1,0:T(8,128)S(1)} %get-tuple-element.27), channel_id=1, source_target_pairs={{0,1},{1,0},{2,3},{3,2},{4,5},{5,4},{6,7},{7,6},{8,9},{9,8},{10,11... | collective-permute-start | bytes 1572872 | tf_op jit(solution)/shard_map/ppermute | solution.py:42
  49.6 3.2 %collective-permute-start.15 = (f32[4,2,32,512]{3,2,1,0:T(8,128)S(1)}, f32[4,2,32,512]{3,2,1,0:T(8,128)S(1)}, u32[]{:S(2)}, u32[]{:S(2)}) collective-permute-start(f32[4,2,32,512]{3,2,1,0:T(8,128)S(1)} %get-tuple-element.25.ready), channel_id=1, source_target_pairs={{0,1},{1,0},{2,3},{3,2},{4,5},{5,4},{6,7},{7,6},{8,9},{9,8},{10,11... | collective-permute-start | bytes 1572872 | tf_op jit(solution)/shard_map/ppermute | solution.py:42
  51.3 9.2 %collective-permute-start.17 = (f32[2,2,32,512]{3,2,1,0:T(8,128)S(1)}, f32[2,2,32,512]{3,2,1,0:T(8,128)S(1)}, u32[]{:S(2)}, u32[]{:S(2)}) collective-permute-start(f32[2,2,32,512]{3,2,1,0:T(8,128)S(1)} %slice.55), channel_id=1, source_target_pairs={{0,2},{1,5},{2,0},{3,7},{4,6},{5,1},{6,4},{7,3},{8,10},{9,13},{10,... | collective-permute-start | bytes 786440 | tf_op jit(solution)/shard_map/ppermute | solution.py:48
  52.9 16.0 %collective-permute-start.16 = (f32[2,2,32,512]{3,2,1,0:T(8,128)S(1)}, f32[2,2,32,512]{3,2,1,0:T(8,128)S(1)}, u32[]{:S(2)}, u32[]{:S(2)}) collective-permute-start(f32[2,2,32,512]{3,2,1,0:T(8,128)S(1)} %slice.53), channel_id=1, source_target_pairs={{0,2},{1,5},{2,0},{3,7},{4,6},{5,1},{6,4},{7,3},{8,10},{9,13},{10,... | collective-permute-start | bytes 786440 | tf_op jit(solution)/shard_map/ppermute | solution.py:48
  53.7 16.3 %collective-permute-start.14 = (f32[2,80,512]{2,1,0:T(8,128)S(1)}, f32[2,80,512]{2,1,0:T(8,128)S(1)}, u32[]{:S(2)}, u32[]{:S(2)}) collective-permute-start(f32[2,80,512]{2,1,0:T(8,128)S(1)} %extend.1.own), channel_id=1, source_target_pairs={{8,0},{16,8},{24,16},{0,24},{9,1},{17,9},{25,17},{1,25},{10,2},{18... | collective-permute-start | bytes 983048 | tf_op jit(solution)/shard_map/ppermute | solution.py:360
  56.2 15.8 %collective-permute-start.13 = (f32[2,80,512]{2,1,0:T(8,128)S(1)}, f32[2,80,512]{2,1,0:T(8,128)S(1)}, u32[]{:S(2)}, u32[]{:S(2)}) collective-permute-start(f32[2,80,512]{2,1,0:T(8,128)S(1)} %extend.1.own), channel_id=1, source_target_pairs={{0,8},{8,16},{16,24},{24,0},{1,9},{9,17},{17,25},{25,1},{2,10},{10... | collective-permute-start | bytes 983048 | tf_op jit(solution)/shard_map/ppermute | solution.py:359
  60.5 12.0 %collective-permute-start.19 = (f32[1,2,32,512]{3,2,1,0:T(8,128)S(1)}, f32[1,2,32,512]{3,2,1,0:T(8,128)S(1)}, u32[]{:S(2)}, u32[]{:S(2)}) collective-permute-start(f32[1,2,32,512]{3,2,1,0:T(8,128)S(1)} %slice.59), channel_id=1, source_target_pairs={{0,4},{1,3},{2,6},{3,1},{4,0},{5,7},{6,2},{7,5},{8,12},{9,11},{10,... | collective-permute-start | bytes 393224 | tf_op jit(solution)/shard_map/ppermute | solution.py:48
  69.0 7.3 %collective-permute-start.18 = (f32[1,2,32,512]{3,2,1,0:T(8,128)S(1)}, f32[1,2,32,512]{3,2,1,0:T(8,128)S(1)}, u32[]{:S(2)}, u32[]{:S(2)}) collective-permute-start(f32[1,2,32,512]{3,2,1,0:T(8,128)S(1)} %slice.57), channel_id=1, source_target_pairs={{0,4},{1,3},{2,6},{3,1},{4,0},{5,7},{6,2},{7,5},{8,12},{9,11},{10,... | collective-permute-start | bytes 393224 | tf_op jit(solution)/shard_map/ppermute | solution.py:48

commit v3 on v2

--- a/solution.py
+++ b/solution.py
@@ -14,7 +14,7 @@
 TV_WEIGHT = 0.5
 TV_SMOOTH = 0.25
 CHUNKS = (5, 3)
-PARTS = (2, 2)
+PARTS = (4,)
 
 F32 = jnp.float32
 BF16 = jnp.bfloat16
@@ -115,38 +115,52 @@
     )(me, table, data.reshape(2 * length, length), sens, me if ready is None else ready)
 
 
-def columns_kernel(blocks, me, table, out, rows):
-    length = out.shape[0]
-    total = sum(size for _, size in blocks)
-    at = 0
-    for start, size in blocks:
-        row = pl.multiple_of(start(me[0]), 16)
-        rows[at : at + size, :] = table[pl.ds(pl.multiple_of(length + row, 16), size), :]
-        rows[total + at : total + at + size, :] = table[pl.ds(row, size), :]
-        at += size
-    out[...] = rows[...].T
-
-
-def columns(blocks, me, table):
+def core_sums(groups, me, table, data, sens):
+    halves = []
+    ready = None
+    for half in (1, 0):
+        ours = [
+            [group[half * (len(group) // 2) : (half + 1) * (len(group) // 2)] for group in part]
+            for part in groups
+        ]
+        others = adjoint(ours[0], me, table, data, sens, ready)
+        owns = adjoint(ours[1], me, table, data, sens, others[0])
+        halves.append([own + swap_cores(other) for own, other in zip(owns, others)])
+        ready = owns[0]
+    return list(zip(halves[1], halves[0]))
+
+
+def columns_kernel(groups, me, table, *refs):
+    outs, rows = refs[:-1], refs[-1]
     length = table.shape[1]
-    total = 2 * sum(size for _, size in blocks)
+    for blocks, out in zip(groups, outs):
+        total = sum(size for _, size in blocks)
+        at = 0
+        for start, size in blocks:
+            row = pl.multiple_of(start(me[0]), 16)
+            rows[at : at + size, :] = table[pl.ds(pl.multiple_of(length + row, 16), size), :]
+            rows[total + at : total + at + size, :] = table[pl.ds(row, size), :]
+            at += size
+        out[...] = rows[: 2 * total, :].T
+
+
+def columns(groups, me, table):
+    length = table.shape[1]
+    totals = [2 * sum(size for _, size in blocks) for blocks in groups]
     return pl.pallas_call(
-        partial(columns_kernel, blocks),
-        out_shape=jax.ShapeDtypeStruct((length, total), BF16),
+        partial(columns_kernel, groups),
+        out_shape=[jax.ShapeDtypeStruct((length, total), BF16) for total in totals],
         in_specs=[SMEM, VMEM],
-        out_specs=VMEM,
-        scratch_shapes=[pltpu.VMEM((total, length), BF16)],
+        out_specs=[VMEM] * len(groups),
+        scratch_shapes=[pltpu.VMEM((max(totals), length), BF16)],
         compiler_params=PARAMS,
         name="columns",
     )(me, table)
 
 
-def forward_kernel(blocks, last, me, table, left, sens, *refs):
+def forward_kernel(blocks, stage, me, table, left, sens, *refs):
     pieces, refs = refs[: len(blocks)], refs[len(blocks) :]
-    if last:
-        before, kspace, sampling, out, lhs, mid = refs
-    else:
-        out, lhs, mid = refs
+    rest, (out, lhs, mid) = refs[:-3], refs[-3:]
     length = sens.shape[1]
     total = sum(size for _, size in blocks)
     at = 0
@@ -168,24 +182,28 @@
     mid[total:, :length] = -middle[total:]
     mid[total:, length:] = middle[:total]
     freq = jnp.dot(left[...], mid[...], preferred_element_type=F32)
-    if last:
-        freq += before[...]
-        weight = sampling[...].astype(F32)
-        out[0] = (weight * (freq[:, :length] - kspace[0].astype(F32))).astype(BF16)
-        out[1] = (weight * (freq[:, length:] - kspace[1].astype(F32))).astype(BF16)
+    if stage == "first":
+        (kspace,) = rest
+        out[:, :length] = freq[:, :length] - kspace[0].astype(F32)
+        out[:, length:] = freq[:, length:] - kspace[1].astype(F32)
+    elif stage == "next":
+        (before,) = rest
+        out[...] = before[...] + freq
     else:
-        out[...] = freq
-
-
-def forward(blocks, me, table, sens, pieces, rest=()):
+        before, mask = rest
+        weight = mask[...].astype(F32)
+        out[0] = (weight * (before[:, :length] + freq[:, :length])).astype(BF16)
+        out[1] = (weight * (before[:, length:] + freq[:, length:])).astype(BF16)
+
+
+def forward(blocks, stage, me, table, left, sens, pieces, rest):
     length = sens.shape[1]
     total = sum(size for _, size in blocks)
-    left = columns(blocks, me, table)
     freq = jax.ShapeDtypeStruct((length, 2 * length), F32)
     resid = jax.ShapeDtypeStruct((2, length, length), BF16)
     return pl.pallas_call(
-        partial(forward_kernel, blocks, bool(rest)),
-        out_shape=resid if rest else freq,
+        partial(forward_kernel, blocks, stage),
+        out_shape=resid if stage == "last" else freq,
         in_specs=[SMEM] + [VMEM] * (3 + len(pieces) + len(rest)),
         out_specs=VMEM,
         scratch_shapes=[pltpu.VMEM((2 * total, 2 * length), BF16)] * 2,
@@ -262,7 +280,8 @@
     table = jnp.asarray(dft_table(length))
     me = lax.axis_index("coil").astype(jnp.int32).reshape(1)
 
-    measured = kspace * sampling.astype(BF16)[None]
+    mask = sampling.astype(BF16)
+    measured = kspace * mask[None]
 
     orders = bit_orders(count)
     eighth = length // 8
@@ -287,12 +306,12 @@
         [[chunk_block(chunk, flip, place) for place in places] for chunk in range(len(chunks))]
         for flip in (1, 0)
     ]
-    others = adjoint(groups[0], me, table, measured, sens)
-    owns = adjoint(groups[1], me, table, measured, sens, others[0])
-    currents = [own + swap_cores(other) for own, other in zip(owns, others)]
+    currents = core_sums(groups, me, table, measured, sens)
     arrived = []
     for current in currents:
-        for step in range(top - 1):
+        keep, send = current
+        current = keep + swap_chips(send, 0)
+        for step in range(1, top - 1):
             middle = current.shape[0] // 2
             current = current[:middle] + swap_chips(current[middle:], step)
         current = current[0]
@@ -306,16 +325,22 @@
         for chunk, pieces in enumerate(arrived)
         for flip in (0, 1)
     ]
-    freq = forward([b for b, _ in early], me, table, sens, [p for _, p in early])
-    late = []
-    for chunk, pieces in enumerate(arrived):
+    late_blocks = [
+        [chunk_block(chunk, flip, place) for chunk in range(len(chunks)) for place in range(1, half // 2)]
+        for flip in (0, 1)
+    ]
+    lefts = columns([[b for b, _ in early], *late_blocks], me, table)
+    pieces = [p for _, p in early]
+    freq = forward([b for b, _ in early], "first", me, table, lefts[0], sens, pieces, [kspace])
+    late = [[], []]
+    for chunk in arrived:
         for place in range(1, half // 2):
-            piece, freq = lax.optimization_barrier((pieces[place], freq))
-            late.append((chunk_block(chunk, 0, place), piece))
-            late.append((chunk_block(chunk, 1, place), swap_cores(piece)))
-    resid = forward(
-        [b for b, _ in late], me, table, sens, [p for _, p in late], [freq, kspace, sampling]
-    )
+            piece, freq = lax.optimization_barrier((chunk[place], freq))
+            late[0].append(piece)
+            late[1].append(swap_cores(piece))
+    freq = forward(late_blocks[0], "next", me, table, lefts[1], sens, late[0], [freq])
+    resid = forward(late_blocks[1], "last", me, table, lefts[2], sens, late[1], [freq, mask])
+    late = [*zip(late_blocks[0], late[0]), *zip(late_blocks[1], late[1])]
 
     parts = [part * size // 4 for part in PARTS] if size >= 64 else [size]
 
@@ -334,15 +359,15 @@
         [[row_block(part, flip, place) for place in places] for part in range(len(parts))]
         for flip in (1, 0)
     ]
-    others = adjoint(groups[0], me, table, resid, sens)
-    owns = adjoint(groups[1], me, table, resid, sens, others[0])
-    summed = [own + swap_cores(other) for own, other in zip(owns, others)]
+    summed = core_sums(groups, me, table, resid, sens)
     gradient, halves = [], []
     for current in summed:
-        for step in range(top):
+        keep, send = current
+        current = keep + swap_chips(send, 0)
+        halves.append(current)
+        for step in range(1, top):
             middle = current.shape[0] // 2
             current = current[:middle] + swap_chips(current[middle:], step)
-            halves.append(current)
         gradient.append(current[0])
 
     extended = pl.pallas_call(
@@ -353,7 +378,7 @@
         scratch_shapes=[pltpu.VMEM((2, length, length), F32)],
         compiler_params=PARAMS,
         name="extend",
-    )(me, summed[-1], *[p for _, p in early + late])
+    )(me, summed[-1][1], *[p for _, p in early + late])
     ahead = [(i, (i + 1) % slabs) for i in range(slabs)]
     behind = [(target, source) for source, target in ahead]
     before = lax.ppermute(extended, "slab", ahead)
@@ -365,7 +390,7 @@
         out_specs=VMEM,
         compiler_params=PARAMS,
         name="total_variation",
-    )(extended, before, after, *halves[::top])
+    )(extended, before, after, *halves)
     return (base - STEP_SIZE * jnp.concatenate(gradient, axis=1))[None]
 
 

time: 77.2 us -> 75.9 us (0.983)
  waiting for transfers between devices: 38 us -> 35.6 us
  Pallas kernels: 9.47 us -> 10.8 us
    ppermute x10 -> x8, waiting for transfers between devices: 34.8 us -> 30.9 us  [swap_chips(): lax.ppermute(value, 'coil', [(i, i ^ 1 << orders[i & 1][step]) for i in r...]
    ppermute x1, waiting for transfers between devices: 2 us -> 4.17 us  [shards(): before = lax.ppermute(extended, 'slab', ahead)]
    ppermute x8 -> x10, starting transfers between devices: 4.4 us -> 5.87 us  [swap_cores(): return lax.ppermute(value, 'coil', [(i, i ^ 1) for i in range(count)])]
    ppermute x10 -> x8, starting transfers between devices: 18.9 us -> 17.5 us  [swap_chips(): lax.ppermute(value, 'coil', [(i, i ^ 1 << orders[i & 1][step]) for i in r...]
    pallas_call x4 -> x8, Pallas kernels: 5.55 us -> 6.7 us  [adjoint(): pl.pallas_call(partial(adjoint_kernel, groups), out_shape=[jax.ShapeDtype...]
  transfers between devices with their start and end apart: 20 -> 20, of which waited for: 12 -> 11; matrix products, arithmetic and copies ran while one was open for 1% -> 1% of each run, Pallas kernels for 7% -> 11%
where the time goes in v3:
time: 75.9 us; the launch traced here: 75.8 us
  waiting for transfers between devices  35.6 us (47%)
  starting transfers between devices  25.9 us (34%)
  Pallas kernels  10.8 us (14%)
  other arithmetic  2.95 us (4%)
    ppermute x8, waiting for transfers between devices, swap_chips(): lax.ppermute(value, 'coil', [(i, i ^ 1 << orders[i & 1][step]) for i in r...  30.9 us
    ppermute x8, starting transfers between devices, swap_chips(): lax.ppermute(value, 'coil', [(i, i ^ 1 << orders[i & 1][step]) for i in r...  17.5 us
    pallas_call x8, Pallas kernels, adjoint(): pl.pallas_call(partial(adjoint_kernel, groups), out_shape=[jax.ShapeDtype...  6.7 us
    ppermute x10, starting transfers between devices, swap_cores(): return lax.ppermute(value, 'coil', [(i, i ^ 1) for i in range(count)])  5.87 us
    ppermute x1, waiting for transfers between devices, shards(): before = lax.ppermute(extended, 'slab', ahead)  4.17 us
    pallas_call x3, Pallas kernels, forward(): pl.pallas_call(partial(forward_kernel, blocks, stage), out_shape=resid if...  3.11 us
    ppermute x1, starting transfers between devices, shards(): after = lax.ppermute(extended, 'slab', behind)  2.5 us
    mul x2, other arithmetic, shards(): measured = kspace * mask[None]  1.71 us
  transfers between devices with their start and end apart: 20, of which 11 were waited for; matrix products, arithmetic and copies ran while one was open for 1% of the time, Pallas kernels for 11%

profile of v3, /device:TPU:0, one launch (start us, length us, event | category | flops | bytes accessed | tf_op | source)
XLA Modules:
  0.0 75.8 jit_solution(13843594525096184243)
XLA Ops:
  0.0 1.5 %convert_bitcast_fusion.refs_3_ = bf16[512,512]{1,0:T(8,128)(2,1)S(1)} fusion(s32[1,512,512]{2,1,0:T(8,128)} %param.6), kind=kLoop, calls=%fused_computation.2 | loop fusion | flops 262144 | bytes 1572864 | tf_op jit(solution)/shard_map/mul | solution.py:284
  5.4 3.1 %collective-permute-start.2 = (f32[1,2,80,512]{3,2,1,0:T(8,128)S(1)}, f32[1,2,80,512]{3,2,1,0:T(8,128)S(1)}, u32[]{:S(2)}, u32[]{:S(2)}) collective-permute-start(f32[1,2,80,512]{3,2,1,0:T(8,128)S(1)} %add.37), channel_id=1, source_target_pairs={{0,2},{1,5},{2,0},{3,7},{4,6},{5,1},{6,4},{7,3},{8,10},{9,13},{10,... | collective-permute-start | bytes 983048 | tf_op jit(solution)/shard_map/ppermute | solution.py:48
  10.3 1.6 %collective-permute-start.8 = (f32[1,2,48,512]{3,2,1,0:T(8,128)S(1)}, f32[1,2,48,512]{3,2,1,0:T(8,128)S(1)}, u32[]{:S(2)}, u32[]{:S(2)}) collective-permute-start(f32[1,2,48,512]{3,2,1,0:T(8,128)S(1)} %add.41), channel_id=1, source_target_pairs={{0,2},{1,5},{2,0},{3,7},{4,6},{5,1},{6,4},{7,3},{8,10},{9,13},{10,... | collective-permute-start | bytes 589832 | tf_op jit(solution)/shard_map/ppermute | solution.py:48
  12.0 4.7 %collective-permute-done.2 = f32[1,2,80,512]{3,2,1,0:T(8,128)S(1)} collective-permute-done((f32[1,2,80,512]{3,2,1,0:T(8,128)S(1)}, f32[1,2,80,512]{3,2,1,0:T(8,128)S(1)}, u32[]{:S(2)}, u32[]{:S(2)}) %collective-permute-start.2) | collective-permute-done | bytes 327712 | tf_op jit(solution)/shard_map/ppermute | solution.py:48
  16.8 3.5 %collective-permute-start.3 = (f32[2,80,512]{2,1,0:T(8,128)S(1)}, f32[2,80,512]{2,1,0:T(8,128)S(1)}, u32[]{:S(2)}, u32[]{:S(2)}) collective-permute-start(f32[2,80,512]{2,1,0:T(8,128)S(1)} %add_bitcast_fusion), channel_id=1, source_target_pairs={{0,4},{1,3},{2,6},{3,1},{4,0},{5,7},{6,2},{7,5},{8,12},{9,11},{10,... | collective-permute-start | bytes 983048 | tf_op jit(solution)/shard_map/ppermute | solution.py:48
  20.2 1.4 %collective-permute-done.8 = f32[1,2,48,512]{3,2,1,0:T(8,128)S(1)} collective-permute-done((f32[1,2,48,512]{3,2,1,0:T(8,128)S(1)}, f32[1,2,48,512]{3,2,1,0:T(8,128)S(1)}, u32[]{:S(2)}, u32[]{:S(2)}) %collective-permute-start.8) | collective-permute-done | bytes 196640 | tf_op jit(solution)/shard_map/ppermute | solution.py:48
  21.7 2.4 %collective-permute-start.9 = (f32[2,48,512]{2,1,0:T(8,128)S(1)}, f32[2,48,512]{2,1,0:T(8,128)S(1)}, u32[]{:S(2)}, u32[]{:S(2)}) collective-permute-start(f32[2,48,512]{2,1,0:T(8,128)S(1)} %add_bitcast_fusion.1), channel_id=1, source_target_pairs={{0,4},{1,3},{2,6},{3,1},{4,0},{5,7},{6,2},{7,5},{8,12},{9,11},{10,... | collective-permute-start | bytes 589832 | tf_op jit(solution)/shard_map/ppermute | solution.py:48
  24.1 4.3 %collective-permute-done.3 = f32[2,80,512]{2,1,0:T(8,128)S(1)} collective-permute-done((f32[2,80,512]{2,1,0:T(8,128)S(1)}, f32[2,80,512]{2,1,0:T(8,128)S(1)}, u32[]{:S(2)}, u32[]{:S(2)}) %collective-permute-start.3) | collective-permute-done | bytes 327712 | tf_op jit(solution)/shard_map/ppermute | solution.py:48
  28.4 1.0 %collective-permute-start.5 = (f32[2,80,512]{2,1,0:T(8,128)S(1)}, f32[2,80,512]{2,1,0:T(8,128)S(1)}, u32[]{:S(2)}, u32[]{:S(2)}) collective-permute-start(f32[2,80,512]{2,1,0:T(8,128)S(1)} %add.39.refs_0_), channel_id=1, source_target_pairs={{0,1},{1,0},{2,3},{3,2},{4,5},{5,4},{6,7},{7,6},{8,9},{9,8},{10,11... | collective-permute-start | bytes 983048 | tf_op jit(solution)/shard_map/ppermute | solution.py:42
  29.5 1.6 %collective-permute-start.4 = (f32[2,80,512]{2,1,0:T(8,128)S(1)}, f32[2,80,512]{2,1,0:T(8,128)S(1)}, u32[]{:S(2)}, u32[]{:S(2)}) collective-permute-start(f32[2,80,512]{2,1,0:T(8,128)S(1)} %add.39.refs_0_), channel_id=1, source_target_pairs={{0,2},{1,5},{2,0},{3,7},{4,6},{5,1},{6,4},{7,3},{8,10},{9,13},{10,... | collective-permute-start | bytes 983048 | tf_op jit(solution)/shard_map/ppermute | solution.py:48
  31.1 0.9 %collective-permute-done.9 = f32[2,48,512]{2,1,0:T(8,128)S(1)} collective-permute-done((f32[2,48,512]{2,1,0:T(8,128)S(1)}, f32[2,48,512]{2,1,0:T(8,128)S(1)}, u32[]{:S(2)}, u32[]{:S(2)}) %collective-permute-start.9) | collective-permute-done | bytes 196640 | tf_op jit(solution)/shard_map/ppermute | solution.py:48
  32.7 2.4 %collective-permute-start.12 = (f32[2,48,512]{2,1,0:T(8,128)S(1)}, f32[2,48,512]{2,1,0:T(8,128)S(1)}, u32[]{:S(2)}, u32[]{:S(2)}) collective-permute-start(f32[2,48,512]{2,1,0:T(8,128)S(1)} %add.43.refs_2_), channel_id=1, source_target_pairs={{0,2},{1,5},{2,0},{3,7},{4,6},{5,1},{6,4},{7,3},{8,10},{9,13},{10,... | collective-permute-start | bytes 589832 | tf_op jit(solution)/shard_map/ppermute | solution.py:48
  35.1 1.4 %forward.3.refs_2_ = f32[512,1024]{1,0:T(8,128)S(1)} custom-call(s32[1]{0:T(128)} %bitcast.me.ready, bf16[1024,512]{1,0:T(8,128)(2,1)S(1)} %copy-done, bf16[512,512]{1,0:T(8,128)(2,1)S(1)} %get-tuple-element.25.left, bf16[2,512,512]{2,1,0:T(8,128)(2,1)S(1)} %bitcast.26, f32[2,80,512]{2,1,0:T(8,128)S(1)} %add.39.refs_0_, ...), custom_call_target="tpu_custom_call" | custom-call | flops 1073741824 | bytes 4194304 | tf_op jit(solution)/shard_map/forward/pallas_call | solution.py:204
  36.5 2.9 %collective-permute-done.4.refs_0_.refs_4_ = f32[2,80,512]{2,1,0:T(8,128)S(1)} collective-permute-done((f32[2,80,512]{2,1,0:T(8,128)S(1)}, f32[2,80,512]{2,1,0:T(8,128)S(1)}, u32[]{:S(2)}, u32[]{:S(2)}) %collective-permute-start.4) | collective-permute-done | bytes 327712 | tf_op jit(solution)/shard_map/ppermute | solution.py:48
  39.4 1.2 %collective-permute-start.11 = (f32[2,80,512]{2,1,0:T(8,128)S(1)}, f32[2,80,512]{2,1,0:T(8,128)S(1)}, u32[]{:S(2)}, u32[]{:S(2)}) collective-permute-start(f32[2,80,512]{2,1,0:T(8,128)S(1)} %collective-permute-done.4.refs_0_.refs_4_), channel_id=1, source_target_pairs={{0,1},{1,0},{2,3},{3,2},{4,5},{5,4},{6,7},{7,6},{8,9},{9,8},{10,11... | collective-permute-start | bytes 983048 | tf_op jit(solution)/shard_map/ppermute | solution.py:42
  40.6 3.0 %collective-permute-done.12.refs_1_.refs_5_ = f32[2,48,512]{2,1,0:T(8,128)S(1)} collective-permute-done((f32[2,48,512]{2,1,0:T(8,128)S(1)}, f32[2,48,512]{2,1,0:T(8,128)S(1)}, u32[]{:S(2)}, u32[]{:S(2)}) %collective-permute-start.12) | collective-permute-done | bytes 196640 | tf_op jit(solution)/shard_map/ppermute | solution.py:48
  43.6 1.2 %collective-permute-start.13 = (f32[2,48,512]{2,1,0:T(8,128)S(1)}, f32[2,48,512]{2,1,0:T(8,128)S(1)}, u32[]{:S(2)}, u32[]{:S(2)}) collective-permute-start(f32[2,48,512]{2,1,0:T(8,128)S(1)} %collective-permute-done.12.refs_1_.refs_5_), channel_id=1, source_target_pairs={{0,1},{1,0},{2,3},{3,2},{4,5},{5,4},{6,7},{7,6},{8,9},{9,8},{10,11... | collective-permute-start | bytes 589832 | tf_op jit(solution)/shard_map/ppermute | solution.py:42
  45.9 0.9 %forward.5 = bf16[2,512,512]{2,1,0:T(8,128)(2,1)S(1)} custom-call(s32[1]{0:T(128)} %bitcast.me.ready, bf16[1024,512]{1,0:T(8,128)(2,1)S(1)} %copy-done, bf16[512,256]{1,0:T(8,128)(2,1)S(1)} %get-tuple-element.20.left, bf16[2,512,512]{2,1,0:T(8,128)(2,1)S(1)} %bitcast.28, f32[2,80,512]{2,1,0:T(8,128)S(1)} %collective-permute-done.11.refs_0_.refs_6_, ...), custom_call_target="tpu_custom_call" | custom-call | flops 536870912 | bytes 4194304 | tf_op jit(solution)/shard_map/forward/pallas_call | solution.py:204
  50.0 1.2 %collective-permute-start.18 = (f32[2,2,64,512]{3,2,1,0:T(8,128)S(1)}, f32[2,2,64,512]{3,2,1,0:T(8,128)S(1)}, u32[]{:S(2)}, u32[]{:S(2)}) collective-permute-start(f32[2,2,64,512]{3,2,1,0:T(8,128)S(1)} %add.44.ready), channel_id=1, source_target_pairs={{0,2},{1,5},{2,0},{3,7},{4,6},{5,1},{6,4},{7,3},{8,10},{9,13},{10,... | collective-permute-start | bytes 1572872 | tf_op jit(solution)/shard_map/ppermute | solution.py:48
  52.3 2.5 %collective-permute-start.16 = (f32[2,80,512]{2,1,0:T(8,128)S(1)}, f32[2,80,512]{2,1,0:T(8,128)S(1)}, u32[]{:S(2)}, u32[]{:S(2)}) collective-permute-start(f32[2,80,512]{2,1,0:T(8,128)S(1)} %extend.1.own), channel_id=1, source_target_pairs={{8,0},{16,8},{24,16},{0,24},{9,1},{17,9},{25,17},{1,25},{10,2},{18... | collective-permute-start | bytes 983048 | tf_op jit(solution)/shard_map/ppermute | solution.py:385
  54.8 9.9 %collective-permute-done.18 = f32[2,2,64,512]{3,2,1,0:T(8,128)S(1)} collective-permute-done((f32[2,2,64,512]{3,2,1,0:T(8,128)S(1)}, f32[2,2,64,512]{3,2,1,0:T(8,128)S(1)}, u32[]{:S(2)}, u32[]{:S(2)}) %collective-permute-start.18) | collective-permute-done | bytes 524320 | tf_op jit(solution)/shard_map/ppermute | solution.py:48
  64.9 1.6 %collective-permute-start.19 = (f32[1,2,64,512]{3,2,1,0:T(8,128)S(1)}, f32[1,2,64,512]{3,2,1,0:T(8,128)S(1)}, u32[]{:S(2)}, u32[]{:S(2)}) collective-permute-start(f32[1,2,64,512]{3,2,1,0:T(8,128)S(1)} %slice.9), channel_id=1, source_target_pairs={{0,4},{1,3},{2,6},{3,1},{4,0},{5,7},{6,2},{7,5},{8,12},{9,11},{10,... | collective-permute-start | bytes 786440 | tf_op jit(solution)/shard_map/ppermute | solution.py:48
  66.5 4.2 %collective-permute-done.15.before = f32[2,80,512]{2,1,0:T(8,128)S(1)} collective-permute-done((f32[2,80,512]{2,1,0:T(8,128)S(1)}, f32[2,80,512]{2,1,0:T(8,128)S(1)}, u32[]{:S(2)}, u32[]{:S(2)}) %collective-permute-start.15) | collective-permute-done | bytes 327712 | tf_op jit(solution)/shard_map/ppermute | solution.py:384
  71.2 3.8 %collective-permute-done.19 = f32[1,2,64,512]{3,2,1,0:T(8,128)S(1)} collective-permute-done((f32[1,2,64,512]{3,2,1,0:T(8,128)S(1)}, f32[1,2,64,512]{3,2,1,0:T(8,128)S(1)}, u32[]{:S(2)}, u32[]{:S(2)}) %collective-permute-start.19) | collective-permute-done | bytes 262176 | tf_op jit(solution)/shard_map/ppermute | solution.py:48
  (48 shorter events, 13.3 us)
Async XLA Ops:
  0.0 1.5 %copy-start.2 = (bf16[1,1,2,512,512]{4,3,2,1,0:T(8,128)(2,1)S(1)}, bf16[1,1,2,512,512]{4,3,2,1,0:T(8,128)(2,1)}, u32[]{:S(2)}) copy-start(bf16[1,1,2,512,512]{4,3,2,1,0:T(8,128)(2,1)} %param.4) | copy-start | bytes 3145732
  0.0 1.9 %copy-start = (bf16[1024,512]{1,0:T(8,128)(2,1)S(1)}, bf16[1024,512]{1,0:T(8,128)(2,1)}, u32[]{:S(2)}) copy-start(bf16[1024,512]{1,0:T(8,128)(2,1)} %constant.8.clone.table) | copy-start | bytes 3145732
  0.0 2.2 %copy-start.1 = (bf16[1,1,2,512,512]{4,3,2,1,0:T(8,128)(2,1)S(1)}, bf16[1,1,2,512,512]{4,3,2,1,0:T(8,128)(2,1)}, u32[]{:S(2)}) copy-start(bf16[1,1,2,512,512]{4,3,2,1,0:T(8,128)(2,1)} %param.5) | copy-start | bytes 3145732
  3.0 2.3 %collective-permute-start.1 = (f32[1,2,80,512]{3,2,1,0:T(8,128)S(1)}, f32[1,2,80,512]{3,2,1,0:T(8,128)S(1)}, u32[]{:S(2)}, u32[]{:S(2)}) collective-permute-start(f32[1,2,80,512]{3,2,1,0:T(8,128)S(1)} %get-tuple-element.21.ready), channel_id=1, source_target_pairs={{0,1},{1,0},{2,3},{3,2},{4,5},{5,4},{6,7},{7,6},{8,9},{9,8},{10,11... | collective-permute-start | bytes 983048 | tf_op jit(solution)/shard_map/ppermute | solution.py:42
  5.2 6.8 %collective-permute-start = (f32[1,2,80,512]{3,2,1,0:T(8,128)S(1)}, f32[1,2,80,512]{3,2,1,0:T(8,128)S(1)}, u32[]{:S(2)}, u32[]{:S(2)}) collective-permute-start(f32[1,2,80,512]{3,2,1,0:T(8,128)S(1)} %get-tuple-element.23.ready), channel_id=1, source_target_pairs={{0,1},{1,0},{2,3},{3,2},{4,5},{5,4},{6,7},{7,6},{8,9},{9,8},{10,11... | collective-permute-start | bytes 983048 | tf_op jit(solution)/shard_map/ppermute | solution.py:42
  5.4 11.3 %collective-permute-start.2 = (f32[1,2,80,512]{3,2,1,0:T(8,128)S(1)}, f32[1,2,80,512]{3,2,1,0:T(8,128)S(1)}, u32[]{:S(2)}, u32[]{:S(2)}) collective-permute-start(f32[1,2,80,512]{3,2,1,0:T(8,128)S(1)} %add.37), channel_id=1, source_target_pairs={{0,2},{1,5},{2,0},{3,7},{4,6},{5,1},{6,4},{7,3},{8,10},{9,13},{10,... | collective-permute-start | bytes 983048 | tf_op jit(solution)/shard_map/ppermute | solution.py:48
  8.5 1.8 %collective-permute-start.7 = (f32[1,2,48,512]{3,2,1,0:T(8,128)S(1)}, f32[1,2,48,512]{3,2,1,0:T(8,128)S(1)}, u32[]{:S(2)}, u32[]{:S(2)}) collective-permute-start(f32[1,2,48,512]{3,2,1,0:T(8,128)S(1)} %get-tuple-element.29), channel_id=1, source_target_pairs={{0,1},{1,0},{2,3},{3,2},{4,5},{5,4},{6,7},{7,6},{8,9},{9,8},{10,11... | collective-permute-start | bytes 589832 | tf_op jit(solution)/shard_map/ppermute | solution.py:42
  9.2 11.0 %collective-permute-start.6 = (f32[1,2,48,512]{3,2,1,0:T(8,128)S(1)}, f32[1,2,48,512]{3,2,1,0:T(8,128)S(1)}, u32[]{:S(2)}, u32[]{:S(2)}) collective-permute-start(f32[1,2,48,512]{3,2,1,0:T(8,128)S(1)} %get-tuple-element.27), channel_id=1, source_target_pairs={{0,1},{1,0},{2,3},{3,2},{4,5},{5,4},{6,7},{7,6},{8,9},{9,8},{10,11... | collective-permute-start | bytes 589832 | tf_op jit(solution)/shard_map/ppermute | solution.py:42
  10.3 11.3 %collective-permute-start.8 = (f32[1,2,48,512]{3,2,1,0:T(8,128)S(1)}, f32[1,2,48,512]{3,2,1,0:T(8,128)S(1)}, u32[]{:S(2)}, u32[]{:S(2)}) collective-permute-start(f32[1,2,48,512]{3,2,1,0:T(8,128)S(1)} %add.41), channel_id=1, source_target_pairs={{0,2},{1,5},{2,0},{3,7},{4,6},{5,1},{6,4},{7,3},{8,10},{9,13},{10,... | collective-permute-start | bytes 589832 | tf_op jit(solution)/shard_map/ppermute | solution.py:48
  16.8 11.6 %collective-permute-start.3 = (f32[2,80,512]{2,1,0:T(8,128)S(1)}, f32[2,80,512]{2,1,0:T(8,128)S(1)}, u32[]{:S(2)}, u32[]{:S(2)}) collective-permute-start(f32[2,80,512]{2,1,0:T(8,128)S(1)} %add_bitcast_fusion), channel_id=1, source_target_pairs={{0,4},{1,3},{2,6},{3,1},{4,0},{5,7},{6,2},{7,5},{8,12},{9,11},{10,... | collective-permute-start | bytes 983048 | tf_op jit(solution)/shard_map/ppermute | solution.py:48
  21.7 10.3 %collective-permute-start.9 = (f32[2,48,512]{2,1,0:T(8,128)S(1)}, f32[2,48,512]{2,1,0:T(8,128)S(1)}, u32[]{:S(2)}, u32[]{:S(2)}) collective-permute-start(f32[2,48,512]{2,1,0:T(8,128)S(1)} %add_bitcast_fusion.1), channel_id=1, source_target_pairs={{0,4},{1,3},{2,6},{3,1},{4,0},{5,7},{6,2},{7,5},{8,12},{9,11},{10,... | collective-permute-start | bytes 589832 | tf_op jit(solution)/shard_map/ppermute | solution.py:48
  28.4 6.7 %collective-permute-start.5 = (f32[2,80,512]{2,1,0:T(8,128)S(1)}, f32[2,80,512]{2,1,0:T(8,128)S(1)}, u32[]{:S(2)}, u32[]{:S(2)}) collective-permute-start(f32[2,80,512]{2,1,0:T(8,128)S(1)} %add.39.refs_0_), channel_id=1, source_target_pairs={{0,1},{1,0},{2,3},{3,2},{4,5},{5,4},{6,7},{7,6},{8,9},{9,8},{10,11... | collective-permute-start | bytes 983048 | tf_op jit(solution)/shard_map/ppermute | solution.py:42
  29.5 9.9 %collective-permute-start.4 = (f32[2,80,512]{2,1,0:T(8,128)S(1)}, f32[2,80,512]{2,1,0:T(8,128)S(1)}, u32[]{:S(2)}, u32[]{:S(2)}) collective-permute-start(f32[2,80,512]{2,1,0:T(8,128)S(1)} %add.39.refs_0_), channel_id=1, source_target_pairs={{0,2},{1,5},{2,0},{3,7},{4,6},{5,1},{6,4},{7,3},{8,10},{9,13},{10,... | collective-permute-start | bytes 983048 | tf_op jit(solution)/shard_map/ppermute | solution.py:48
  32.1 3.1 %collective-permute-start.10 = (f32[2,48,512]{2,1,0:T(8,128)S(1)}, f32[2,48,512]{2,1,0:T(8,128)S(1)}, u32[]{:S(2)}, u32[]{:S(2)}) collective-permute-start(f32[2,48,512]{2,1,0:T(8,128)S(1)} %add.43.refs_2_), channel_id=1, source_target_pairs={{0,1},{1,0},{2,3},{3,2},{4,5},{5,4},{6,7},{7,6},{8,9},{9,8},{10,11... | collective-permute-start | bytes 589832 | tf_op jit(solution)/shard_map/ppermute | solution.py:42
  32.7 10.8 %collective-permute-start.12 = (f32[2,48,512]{2,1,0:T(8,128)S(1)}, f32[2,48,512]{2,1,0:T(8,128)S(1)}, u32[]{:S(2)}, u32[]{:S(2)}) collective-permute-start(f32[2,48,512]{2,1,0:T(8,128)S(1)} %add.43.refs_2_), channel_id=1, source_target_pairs={{0,2},{1,5},{2,0},{3,7},{4,6},{5,1},{6,4},{7,3},{8,10},{9,13},{10,... | collective-permute-start | bytes 589832 | tf_op jit(solution)/shard_map/ppermute | solution.py:48
  39.4 6.5 %collective-permute-start.11 = (f32[2,80,512]{2,1,0:T(8,128)S(1)}, f32[2,80,512]{2,1,0:T(8,128)S(1)}, u32[]{:S(2)}, u32[]{:S(2)}) collective-permute-start(f32[2,80,512]{2,1,0:T(8,128)S(1)} %collective-permute-done.4.refs_0_.refs_4_), channel_id=1, source_target_pairs={{0,1},{1,0},{2,3},{3,2},{4,5},{5,4},{6,7},{7,6},{8,9},{9,8},{10,11... | collective-permute-start | bytes 983048 | tf_op jit(solution)/shard_map/ppermute | solution.py:42
  43.6 2.3 %collective-permute-start.13 = (f32[2,48,512]{2,1,0:T(8,128)S(1)}, f32[2,48,512]{2,1,0:T(8,128)S(1)}, u32[]{:S(2)}, u32[]{:S(2)}) collective-permute-start(f32[2,48,512]{2,1,0:T(8,128)S(1)} %collective-permute-done.12.refs_1_.refs_5_), channel_id=1, source_target_pairs={{0,1},{1,0},{2,3},{3,2},{4,5},{5,4},{6,7},{7,6},{8,9},{9,8},{10,11... | collective-permute-start | bytes 589832 | tf_op jit(solution)/shard_map/ppermute | solution.py:42
  47.6 2.3 %collective-permute-start.14 = (f32[2,2,64,512]{3,2,1,0:T(8,128)S(1)}, f32[2,2,64,512]{3,2,1,0:T(8,128)S(1)}, u32[]{:S(2)}, u32[]{:S(2)}) collective-permute-start(f32[2,2,64,512]{3,2,1,0:T(8,128)S(1)} %adjoint.12.ready), channel_id=1, source_target_pairs={{0,1},{1,0},{2,3},{3,2},{4,5},{5,4},{6,7},{7,6},{8,9},{9,8},{10,11... | collective-permute-start | bytes 1572872 | tf_op jit(solution)/shard_map/ppermute | solution.py:42
  49.8 5.1 %collective-permute-start.17 = (f32[2,2,64,512]{3,2,1,0:T(8,128)S(1)}, f32[2,2,64,512]{3,2,1,0:T(8,128)S(1)}, u32[]{:S(2)}, u32[]{:S(2)}) collective-permute-start(f32[2,2,64,512]{3,2,1,0:T(8,128)S(1)} %adjoint.14.ready), channel_id=1, source_target_pairs={{0,1},{1,0},{2,3},{3,2},{4,5},{5,4},{6,7},{7,6},{8,9},{9,8},{10,11... | collective-permute-start | bytes 1572872 | tf_op jit(solution)/shard_map/ppermute | solution.py:42
  50.0 14.7 %collective-permute-start.18 = (f32[2,2,64,512]{3,2,1,0:T(8,128)S(1)}, f32[2,2,64,512]{3,2,1,0:T(8,128)S(1)}, u32[]{:S(2)}, u32[]{:S(2)}) collective-permute-start(f32[2,2,64,512]{3,2,1,0:T(8,128)S(1)} %add.44.ready), channel_id=1, source_target_pairs={{0,2},{1,5},{2,0},{3,7},{4,6},{5,1},{6,4},{7,3},{8,10},{9,13},{10,... | collective-permute-start | bytes 1572872 | tf_op jit(solution)/shard_map/ppermute | solution.py:48
  52.3 14.2 %collective-permute-start.16 = (f32[2,80,512]{2,1,0:T(8,128)S(1)}, f32[2,80,512]{2,1,0:T(8,128)S(1)}, u32[]{:S(2)}, u32[]{:S(2)}) collective-permute-start(f32[2,80,512]{2,1,0:T(8,128)S(1)} %extend.1.own), channel_id=1, source_target_pairs={{8,0},{16,8},{24,16},{0,24},{9,1},{17,9},{25,17},{1,25},{10,2},{18... | collective-permute-start | bytes 983048 | tf_op jit(solution)/shard_map/ppermute | solution.py:385
  54.8 15.9 %collective-permute-start.15 = (f32[2,80,512]{2,1,0:T(8,128)S(1)}, f32[2,80,512]{2,1,0:T(8,128)S(1)}, u32[]{:S(2)}, u32[]{:S(2)}) collective-permute-start(f32[2,80,512]{2,1,0:T(8,128)S(1)} %extend.1.own), channel_id=1, source_target_pairs={{0,8},{8,16},{16,24},{24,0},{1,9},{9,17},{17,25},{25,1},{2,10},{10... | collective-permute-start | bytes 983048 | tf_op jit(solution)/shard_map/ppermute | solution.py:384
  64.9 10.1 %collective-permute-start.19 = (f32[1,2,64,512]{3,2,1,0:T(8,128)S(1)}, f32[1,2,64,512]{3,2,1,0:T(8,128)S(1)}, u32[]{:S(2)}, u32[]{:S(2)}) collective-permute-start(f32[1,2,64,512]{3,2,1,0:T(8,128)S(1)} %slice.9), channel_id=1, source_target_pairs={{0,4},{1,3},{2,6},{3,1},{4,0},{5,7},{6,2},{7,5},{8,12},{9,11},{10,... | collective-permute-start | bytes 786440 | tf_op jit(solution)/shard_map/ppermute | solution.py:48

commit v4 on v3

--- a/solution.py
+++ b/solution.py
@@ -14,7 +14,6 @@
 TV_WEIGHT = 0.5
 TV_SMOOTH = 0.25
 CHUNKS = (5, 3)
-PARTS = (4,)
 
 F32 = jnp.float32
 BF16 = jnp.bfloat16
@@ -213,9 +212,8 @@
     )(me, table, left, sens, *pieces, *rest)
 
 
-def extend_kernel(blocks, me, ready, *refs):
-    del ready
-    pieces, (out, volume) = refs[:-2], refs[-2:]
+def extend_kernel(blocks, me, *refs):
+    pieces, (out, to_before, to_after, volume) = refs[:-4], refs[-4:]
     length = volume.shape[1]
     own = out.shape[1] - 16
     for (start, size), piece in zip(blocks, pieces):
@@ -226,11 +224,15 @@
         (8, first, own),
         (8 + own, (first + own) & (length - 1), 8),
     ):
-        out[:, at : at + count, :] = volume[:, pl.ds(pl.multiple_of(row, 8), count), :]
-
-
-def tv_kernel(own, before, after, *refs):
-    out = refs[-1]
+        values = volume[:, pl.ds(pl.multiple_of(row, 8), count), :]
+        out[:, at : at + count, :] = values
+        if at <= 8:
+            to_before[:, at : at + count, :] = values
+        if at >= 8:
+            to_after[:, at - 8 : at - 8 + count, :] = values
+
+
+def tv_kernel(own, before, after, kept, arrived, out):
     size = out.shape[1]
     length = out.shape[2]
 
@@ -256,9 +258,9 @@
     slices, rows, columns = fluxes(
         here, minus(parts(after, 7, count), here), minus(parts(own, 8, count), here)
     )
-    back = parts(before, 8, size)
+    back = parts(before, 0, size)
     center = parts(own, 8, size)
-    back_slices, _, _ = fluxes(back, minus(center, back), minus(parts(before, 9, size), back))
+    back_slices, _, _ = fluxes(back, minus(center, back), minus(parts(before, 1, size), back))
     for part in (0, 1):
         col = columns[part][1:]
         tv = (
@@ -266,7 +268,8 @@
             + (rows[part][:-1] - rows[part][1:])
             + (pltpu.roll(col, 1, 1) - col)
         )
-        out[part] = center[part] - (STEP_SIZE * TV_WEIGHT) * tv
+        gradient = kept[0, part] + arrived[0, part]
+        out[part] = center[part] - STEP_SIZE * (gradient + TV_WEIGHT * tv)
 
 
 def shards(kspace, sensitivity, sampling):
@@ -342,7 +345,7 @@
     resid = forward(late_blocks[1], "last", me, table, lefts[2], sens, late[1], [freq, mask])
     late = [*zip(late_blocks[0], late[0]), *zip(late_blocks[1], late[1])]
 
-    parts = [part * size // 4 for part in PARTS] if size >= 64 else [size]
+    parts = [size]
 
     def row_block(part, flip, place):
         masks = [
@@ -360,38 +363,38 @@
         for flip in (1, 0)
     ]
     summed = core_sums(groups, me, table, resid, sens)
-    gradient, halves = [], []
-    for current in summed:
-        keep, send = current
-        current = keep + swap_chips(send, 0)
-        halves.append(current)
-        for step in range(1, top):
-            middle = current.shape[0] // 2
-            current = current[:middle] + swap_chips(current[middle:], step)
-        gradient.append(current[0])
-
-    extended = pl.pallas_call(
+    keep, send = summed[0]
+    for step in range(top - 1):
+        middle = keep.shape[0] // 2
+        passed = keep[middle:] + swap_chips(send[middle:], step)
+        kept = [keep[:middle], swap_chips(send[:middle], step)]
+        if step < top - 2:
+            keep = kept[0] + kept[1]
+        send = passed
+    gradient = swap_chips(send, top - 1)
+
+    extended, to_before, to_after = pl.pallas_call(
         partial(extend_kernel, [b for b, _ in early + late]),
-        out_shape=jax.ShapeDtypeStruct((2, size + 16, length), F32),
-        in_specs=[SMEM, ANY] + [VMEM] * len(early + late),
-        out_specs=VMEM,
+        out_shape=[jax.ShapeDtypeStruct((2, size + more, length), F32) for more in (16, 8, 8)],
+        in_specs=[SMEM] + [VMEM] * len(early + late),
+        out_specs=[VMEM] * 3,
         scratch_shapes=[pltpu.VMEM((2, length, length), F32)],
         compiler_params=PARAMS,
         name="extend",
-    )(me, summed[-1][1], *[p for _, p in early + late])
+    )(me, *[p for _, p in early + late])
     ahead = [(i, (i + 1) % slabs) for i in range(slabs)]
     behind = [(target, source) for source, target in ahead]
-    before = lax.ppermute(extended, "slab", ahead)
-    after = lax.ppermute(extended, "slab", behind)
+    before = lax.ppermute(to_after, "slab", ahead)
+    after = lax.ppermute(to_before, "slab", behind)
     base = pl.pallas_call(
         tv_kernel,
         out_shape=jax.ShapeDtypeStruct((2, size, length), F32),
-        in_specs=[VMEM, VMEM, VMEM] + [ANY] * len(parts),
+        in_specs=[VMEM] * 5,
         out_specs=VMEM,
         compiler_params=PARAMS,
         name="total_variation",
-    )(extended, before, after, *halves)
-    return (base - STEP_SIZE * jnp.concatenate(gradient, axis=1))[None]
+    )(extended, before, after, *kept)
+    return (base - STEP_SIZE * gradient[0])[None]
 
 
 def solution(mesh):

time: 75.9 us -> 70.8 us (0.933)
  waiting for transfers between devices: 35.6 us -> 28.6 us
  starting transfers between devices: 25.9 us -> 27.3 us
    ppermute x8 -> x9, waiting for transfers between devices: 30.9 us -> 20.5 us  [swap_chips(): lax.ppermute(value, 'coil', [(i, i ^ 1 << orders[i & 1][step]) for i in r...]
    ppermute x2, waiting for transfers between devices: 4.18 us -> 7.68 us  [the longest x1 6.15 us: shards(): after = lax.ppermute(to_before, 'slab', behind)]
    ppermute x8 -> x9, starting transfers between devices: 17.5 us -> 18.4 us  [swap_chips(): lax.ppermute(value, 'coil', [(i, i ^ 1 << orders[i & 1][step]) for i in r...]
  transfers between devices with their start and end apart: 20 -> 21, of which waited for: 11 -> 12; matrix products, arithmetic and copies ran while one was open for 1% -> 1% of each run, Pallas kernels for 11% -> 12%
where the time goes in v4:
time: 70.8 us; the launch traced here: 70.3 us
  waiting for transfers between devices  28.6 us (40%)
  starting transfers between devices  27.3 us (39%)
  Pallas kernels  10.9 us (15%)
  other arithmetic  2.94 us (4%)
    ppermute x9, waiting for transfers between devices, swap_chips(): lax.ppermute(value, 'coil', [(i, i ^ 1 << orders[i & 1][step]) for i in r...  20.5 us
    ppermute x9, starting transfers between devices, swap_chips(): lax.ppermute(value, 'coil', [(i, i ^ 1 << orders[i & 1][step]) for i in r...  18.4 us
    pallas_call x8, Pallas kernels, adjoint(): pl.pallas_call(partial(adjoint_kernel, groups), out_shape=[jax.ShapeDtype...  6.7 us
    ppermute x1, waiting for transfers between devices, shards(): after = lax.ppermute(to_before, 'slab', behind)  6.15 us
    ppermute x10, starting transfers between devices, swap_cores(): return lax.ppermute(value, 'coil', [(i, i ^ 1) for i in range(count)])  5.87 us
    pallas_call x3, Pallas kernels, forward(): pl.pallas_call(partial(forward_kernel, blocks, stage), out_shape=resid if...  3.11 us
    mul x2, other arithmetic, shards(): measured = kspace * mask[None]  1.71 us
    ppermute x1, starting transfers between devices, shards(): before = lax.ppermute(to_after, 'slab', ahead)  1.54 us
  transfers between devices with their start and end apart: 21, of which 12 were waited for; matrix products, arithmetic and copies ran while one was open for 1% of the time, Pallas kernels for 12%

profile of v4, /device:TPU:0, one launch (start us, length us, event | category | flops | bytes accessed | tf_op | source)
XLA Modules:
  0.0 70.3 jit_solution(3157532790643734851)
XLA Ops:
  0.0 1.5 %convert_bitcast_fusion.refs_3_ = bf16[512,512]{1,0:T(8,128)(2,1)S(1)} fusion(s32[1,512,512]{2,1,0:T(8,128)} %param.6), kind=kLoop, calls=%fused_computation.1 | loop fusion | flops 262144 | bytes 1572864 | tf_op jit(solution)/shard_map/mul | solution.py:287
  5.4 3.1 %collective-permute-start.2 = (f32[1,2,80,512]{3,2,1,0:T(8,128)S(1)}, f32[1,2,80,512]{3,2,1,0:T(8,128)S(1)}, u32[]{:S(2)}, u32[]{:S(2)}) collective-permute-start(f32[1,2,80,512]{3,2,1,0:T(8,128)S(1)} %add.34), channel_id=1, source_target_pairs={{0,2},{1,5},{2,0},{3,7},{4,6},{5,1},{6,4},{7,3},{8,10},{9,13},{10,... | collective-permute-start | bytes 983048 | tf_op jit(solution)/shard_map/ppermute | solution.py:47
  10.3 1.6 %collective-permute-start.7 = (f32[1,2,48,512]{3,2,1,0:T(8,128)S(1)}, f32[1,2,48,512]{3,2,1,0:T(8,128)S(1)}, u32[]{:S(2)}, u32[]{:S(2)}) collective-permute-start(f32[1,2,48,512]{3,2,1,0:T(8,128)S(1)} %add.38), channel_id=1, source_target_pairs={{0,2},{1,5},{2,0},{3,7},{4,6},{5,1},{6,4},{7,3},{8,10},{9,13},{10,... | collective-permute-start | bytes 589832 | tf_op jit(solution)/shard_map/ppermute | solution.py:47
  12.0 4.7 %collective-permute-done.2 = f32[1,2,80,512]{3,2,1,0:T(8,128)S(1)} collective-permute-done((f32[1,2,80,512]{3,2,1,0:T(8,128)S(1)}, f32[1,2,80,512]{3,2,1,0:T(8,128)S(1)}, u32[]{:S(2)}, u32[]{:S(2)}) %collective-permute-start.2) | collective-permute-done | bytes 327712 | tf_op jit(solution)/shard_map/ppermute | solution.py:47
  16.8 3.5 %collective-permute-start.3 = (f32[2,80,512]{2,1,0:T(8,128)S(1)}, f32[2,80,512]{2,1,0:T(8,128)S(1)}, u32[]{:S(2)}, u32[]{:S(2)}) collective-permute-start(f32[2,80,512]{2,1,0:T(8,128)S(1)} %add_bitcast_fusion), channel_id=1, source_target_pairs={{0,4},{1,3},{2,6},{3,1},{4,0},{5,7},{6,2},{7,5},{8,12},{9,11},{10,... | collective-permute-start | bytes 983048 | tf_op jit(solution)/shard_map/ppermute | solution.py:47
  20.2 1.4 %collective-permute-done.7 = f32[1,2,48,512]{3,2,1,0:T(8,128)S(1)} collective-permute-done((f32[1,2,48,512]{3,2,1,0:T(8,128)S(1)}, f32[1,2,48,512]{3,2,1,0:T(8,128)S(1)}, u32[]{:S(2)}, u32[]{:S(2)}) %collective-permute-start.7) | collective-permute-done | bytes 196640 | tf_op jit(solution)/shard_map/ppermute | solution.py:47
  21.7 2.4 %collective-permute-start.8 = (f32[2,48,512]{2,1,0:T(8,128)S(1)}, f32[2,48,512]{2,1,0:T(8,128)S(1)}, u32[]{:S(2)}, u32[]{:S(2)}) collective-permute-start(f32[2,48,512]{2,1,0:T(8,128)S(1)} %add_bitcast_fusion.1), channel_id=1, source_target_pairs={{0,4},{1,3},{2,6},{3,1},{4,0},{5,7},{6,2},{7,5},{8,12},{9,11},{10,... | collective-permute-start | bytes 589832 | tf_op jit(solution)/shard_map/ppermute | solution.py:47
  24.1 4.3 %collective-permute-done.3 = f32[2,80,512]{2,1,0:T(8,128)S(1)} collective-permute-done((f32[2,80,512]{2,1,0:T(8,128)S(1)}, f32[2,80,512]{2,1,0:T(8,128)S(1)}, u32[]{:S(2)}, u32[]{:S(2)}) %collective-permute-start.3) | collective-permute-done | bytes 327712 | tf_op jit(solution)/shard_map/ppermute | solution.py:47
  28.4 1.0 %collective-permute-start.4 = (f32[2,80,512]{2,1,0:T(8,128)S(1)}, f32[2,80,512]{2,1,0:T(8,128)S(1)}, u32[]{:S(2)}, u32[]{:S(2)}) collective-permute-start(f32[2,80,512]{2,1,0:T(8,128)S(1)} %add.36.refs_0_), channel_id=1, source_target_pairs={{0,1},{1,0},{2,3},{3,2},{4,5},{5,4},{6,7},{7,6},{8,9},{9,8},{10,11... | collective-permute-start | bytes 983048 | tf_op jit(solution)/shard_map/ppermute | solution.py:41
  29.5 1.6 %collective-permute-start.10 = (f32[2,80,512]{2,1,0:T(8,128)S(1)}, f32[2,80,512]{2,1,0:T(8,128)S(1)}, u32[]{:S(2)}, u32[]{:S(2)}) collective-permute-start(f32[2,80,512]{2,1,0:T(8,128)S(1)} %add.36.refs_0_), channel_id=1, source_target_pairs={{0,2},{1,5},{2,0},{3,7},{4,6},{5,1},{6,4},{7,3},{8,10},{9,13},{10,... | collective-permute-start | bytes 983048 | tf_op jit(solution)/shard_map/ppermute | solution.py:47
  31.1 0.9 %collective-permute-done.8 = f32[2,48,512]{2,1,0:T(8,128)S(1)} collective-permute-done((f32[2,48,512]{2,1,0:T(8,128)S(1)}, f32[2,48,512]{2,1,0:T(8,128)S(1)}, u32[]{:S(2)}, u32[]{:S(2)}) %collective-permute-start.8) | collective-permute-done | bytes 196640 | tf_op jit(solution)/shard_map/ppermute | solution.py:47
  32.7 2.4 %collective-permute-start.11 = (f32[2,48,512]{2,1,0:T(8,128)S(1)}, f32[2,48,512]{2,1,0:T(8,128)S(1)}, u32[]{:S(2)}, u32[]{:S(2)}) collective-permute-start(f32[2,48,512]{2,1,0:T(8,128)S(1)} %add.40.refs_2_), channel_id=1, source_target_pairs={{0,2},{1,5},{2,0},{3,7},{4,6},{5,1},{6,4},{7,3},{8,10},{9,13},{10,... | collective-permute-start | bytes 589832 | tf_op jit(solution)/shard_map/ppermute | solution.py:47
  35.1 1.4 %forward.3.refs_2_ = f32[512,1024]{1,0:T(8,128)S(1)} custom-call(s32[1]{0:T(128)} %bitcast.me.ready, bf16[1024,512]{1,0:T(8,128)(2,1)S(1)} %copy-done, bf16[512,512]{1,0:T(8,128)(2,1)S(1)} %get-tuple-element.31.left, bf16[2,512,512]{2,1,0:T(8,128)(2,1)S(1)} %bitcast.24, f32[2,80,512]{2,1,0:T(8,128)S(1)} %add.36.refs_0_, ...), custom_call_target="tpu_custom_call" | custom-call | flops 1073741824 | bytes 4194304 | tf_op jit(solution)/shard_map/forward/pallas_call | solution.py:203
  36.5 2.9 %collective-permute-done.10.refs_4_.refs_0_ = f32[2,80,512]{2,1,0:T(8,128)S(1)} collective-permute-done((f32[2,80,512]{2,1,0:T(8,128)S(1)}, f32[2,80,512]{2,1,0:T(8,128)S(1)}, u32[]{:S(2)}, u32[]{:S(2)}) %collective-permute-start.10) | collective-permute-done | bytes 327712 | tf_op jit(solution)/shard_map/ppermute | solution.py:47
  39.4 1.2 %collective-permute-start.12 = (f32[2,80,512]{2,1,0:T(8,128)S(1)}, f32[2,80,512]{2,1,0:T(8,128)S(1)}, u32[]{:S(2)}, u32[]{:S(2)}) collective-permute-start(f32[2,80,512]{2,1,0:T(8,128)S(1)} %collective-permute-done.10.refs_4_.refs_0_), channel_id=1, source_target_pairs={{0,1},{1,0},{2,3},{3,2},{4,5},{5,4},{6,7},{7,6},{8,9},{9,8},{10,11... | collective-permute-start | bytes 983048 | tf_op jit(solution)/shard_map/ppermute | solution.py:41
  40.6 3.0 %collective-permute-done.11.refs_5_.refs_1_ = f32[2,48,512]{2,1,0:T(8,128)S(1)} collective-permute-done((f32[2,48,512]{2,1,0:T(8,128)S(1)}, f32[2,48,512]{2,1,0:T(8,128)S(1)}, u32[]{:S(2)}, u32[]{:S(2)}) %collective-permute-start.11) | collective-permute-done | bytes 196640 | tf_op jit(solution)/shard_map/ppermute | solution.py:47
  43.6 1.2 %collective-permute-start.13 = (f32[2,48,512]{2,1,0:T(8,128)S(1)}, f32[2,48,512]{2,1,0:T(8,128)S(1)}, u32[]{:S(2)}, u32[]{:S(2)}) collective-permute-start(f32[2,48,512]{2,1,0:T(8,128)S(1)} %collective-permute-done.11.refs_5_.refs_1_), channel_id=1, source_target_pairs={{0,1},{1,0},{2,3},{3,2},{4,5},{5,4},{6,7},{7,6},{8,9},{9,8},{10,11... | collective-permute-start | bytes 589832 | tf_op jit(solution)/shard_map/ppermute | solution.py:41
  50.1 1.2 %collective-permute-start.19 = (f32[1,2,64,512]{3,2,1,0:T(8,128)S(1)}, f32[1,2,64,512]{3,2,1,0:T(8,128)S(1)}, u32[]{:S(2)}, u32[]{:S(2)}) collective-permute-start(f32[1,2,64,512]{3,2,1,0:T(8,128)S(1)} %get-tuple-element.43), channel_id=1, source_target_pairs={{0,2},{1,5},{2,0},{3,7},{4,6},{5,1},{6,4},{7,3},{8,10},{9,13},{10,... | collective-permute-start | bytes 786440 | tf_op jit(solution)/shard_map/ppermute | solution.py:47
  51.5 1.5 %collective-permute-start.14 = (f32[2,72,512]{2,1,0:T(8,128)S(1)}, f32[2,72,512]{2,1,0:T(8,128)S(1)}, u32[]{:S(2)}, u32[]{:S(2)}) collective-permute-start(f32[2,72,512]{2,1,0:T(8,128)S(1)} %get-tuple-element.36), channel_id=1, source_target_pairs={{0,8},{8,16},{16,24},{24,0},{1,9},{9,17},{17,25},{25,1},{2,10},{10... | collective-permute-start | bytes 884744 | tf_op jit(solution)/shard_map/ppermute | solution.py:387
  53.1 1.4 %collective-permute-start.15 = (f32[2,72,512]{2,1,0:T(8,128)S(1)}, f32[2,72,512]{2,1,0:T(8,128)S(1)}, u32[]{:S(2)}, u32[]{:S(2)}) collective-permute-start(f32[2,72,512]{2,1,0:T(8,128)S(1)} %get-tuple-element.37), channel_id=1, source_target_pairs={{8,0},{16,8},{24,16},{0,24},{9,1},{17,9},{25,17},{1,25},{10,2},{18... | collective-permute-start | bytes 884744 | tf_op jit(solution)/shard_map/ppermute | solution.py:388
  56.4 2.8 %collective-permute-done.19 = f32[1,2,64,512]{3,2,1,0:T(8,128)S(1)} collective-permute-done((f32[1,2,64,512]{3,2,1,0:T(8,128)S(1)}, f32[1,2,64,512]{3,2,1,0:T(8,128)S(1)}, u32[]{:S(2)}, u32[]{:S(2)}) %collective-permute-start.19) | collective-permute-done | bytes 262176 | tf_op jit(solution)/shard_map/ppermute | solution.py:47
  59.2 1.6 %collective-permute-start.20 = (f32[1,2,64,512]{3,2,1,0:T(8,128)S(1)}, f32[1,2,64,512]{3,2,1,0:T(8,128)S(1)}, u32[]{:S(2)}, u32[]{:S(2)}) collective-permute-start(f32[1,2,64,512]{3,2,1,0:T(8,128)S(1)} %get-tuple-element.41), channel_id=1, source_target_pairs={{0,4},{1,3},{2,6},{3,1},{4,0},{5,7},{6,2},{7,5},{8,12},{9,11},{10,... | collective-permute-start | bytes 786440 | tf_op jit(solution)/shard_map/ppermute | solution.py:47
  60.8 1.5 %collective-permute-done.14.before = f32[2,72,512]{2,1,0:T(8,128)S(1)} collective-permute-done((f32[2,72,512]{2,1,0:T(8,128)S(1)}, f32[2,72,512]{2,1,0:T(8,128)S(1)}, u32[]{:S(2)}, u32[]{:S(2)}) %collective-permute-start.14) | collective-permute-done | bytes 294944 | tf_op jit(solution)/shard_map/ppermute | solution.py:387
  62.4 6.2 %collective-permute-done.15.after = f32[2,72,512]{2,1,0:T(8,128)S(1)} collective-permute-done((f32[2,72,512]{2,1,0:T(8,128)S(1)}, f32[2,72,512]{2,1,0:T(8,128)S(1)}, u32[]{:S(2)}, u32[]{:S(2)}) %collective-permute-start.15) | collective-permute-done | bytes 294944 | tf_op jit(solution)/shard_map/ppermute | solution.py:388
  (51 shorter events, 15.6 us)
Async XLA Ops:
  0.0 1.5 %copy-start.2 = (bf16[1,1,2,512,512]{4,3,2,1,0:T(8,128)(2,1)S(1)}, bf16[1,1,2,512,512]{4,3,2,1,0:T(8,128)(2,1)}, u32[]{:S(2)}) copy-start(bf16[1,1,2,512,512]{4,3,2,1,0:T(8,128)(2,1)} %param.4) | copy-start | bytes 3145732
  0.0 1.9 %copy-start = (bf16[1024,512]{1,0:T(8,128)(2,1)S(1)}, bf16[1024,512]{1,0:T(8,128)(2,1)}, u32[]{:S(2)}) copy-start(bf16[1024,512]{1,0:T(8,128)(2,1)} %constant.8.clone.table) | copy-start | bytes 3145732
  0.0 2.2 %copy-start.1 = (bf16[1,1,2,512,512]{4,3,2,1,0:T(8,128)(2,1)S(1)}, bf16[1,1,2,512,512]{4,3,2,1,0:T(8,128)(2,1)}, u32[]{:S(2)}) copy-start(bf16[1,1,2,512,512]{4,3,2,1,0:T(8,128)(2,1)} %param.5) | copy-start | bytes 3145732
  3.0 2.3 %collective-permute-start.1 = (f32[1,2,80,512]{3,2,1,0:T(8,128)S(1)}, f32[1,2,80,512]{3,2,1,0:T(8,128)S(1)}, u32[]{:S(2)}, u32[]{:S(2)}) collective-permute-start(f32[1,2,80,512]{3,2,1,0:T(8,128)S(1)} %get-tuple-element.23.ready), channel_id=1, source_target_pairs={{0,1},{1,0},{2,3},{3,2},{4,5},{5,4},{6,7},{7,6},{8,9},{9,8},{10,11... | collective-permute-start | bytes 983048 | tf_op jit(solution)/shard_map/ppermute | solution.py:41
  5.2 6.8 %collective-permute-start = (f32[1,2,80,512]{3,2,1,0:T(8,128)S(1)}, f32[1,2,80,512]{3,2,1,0:T(8,128)S(1)}, u32[]{:S(2)}, u32[]{:S(2)}) collective-permute-start(f32[1,2,80,512]{3,2,1,0:T(8,128)S(1)} %get-tuple-element.25.ready), channel_id=1, source_target_pairs={{0,1},{1,0},{2,3},{3,2},{4,5},{5,4},{6,7},{7,6},{8,9},{9,8},{10,11... | collective-permute-start | bytes 983048 | tf_op jit(solution)/shard_map/ppermute | solution.py:41
  5.4 11.3 %collective-permute-start.2 = (f32[1,2,80,512]{3,2,1,0:T(8,128)S(1)}, f32[1,2,80,512]{3,2,1,0:T(8,128)S(1)}, u32[]{:S(2)}, u32[]{:S(2)}) collective-permute-start(f32[1,2,80,512]{3,2,1,0:T(8,128)S(1)} %add.34), channel_id=1, source_target_pairs={{0,2},{1,5},{2,0},{3,7},{4,6},{5,1},{6,4},{7,3},{8,10},{9,13},{10,... | collective-permute-start | bytes 983048 | tf_op jit(solution)/shard_map/ppermute | solution.py:47
  8.5 1.8 %collective-permute-start.6 = (f32[1,2,48,512]{3,2,1,0:T(8,128)S(1)}, f32[1,2,48,512]{3,2,1,0:T(8,128)S(1)}, u32[]{:S(2)}, u32[]{:S(2)}) collective-permute-start(f32[1,2,48,512]{3,2,1,0:T(8,128)S(1)} %get-tuple-element.30), channel_id=1, source_target_pairs={{0,1},{1,0},{2,3},{3,2},{4,5},{5,4},{6,7},{7,6},{8,9},{9,8},{10,11... | collective-permute-start | bytes 589832 | tf_op jit(solution)/shard_map/ppermute | solution.py:41
  9.2 11.0 %collective-permute-start.5 = (f32[1,2,48,512]{3,2,1,0:T(8,128)S(1)}, f32[1,2,48,512]{3,2,1,0:T(8,128)S(1)}, u32[]{:S(2)}, u32[]{:S(2)}) collective-permute-start(f32[1,2,48,512]{3,2,1,0:T(8,128)S(1)} %get-tuple-element.28), channel_id=1, source_target_pairs={{0,1},{1,0},{2,3},{3,2},{4,5},{5,4},{6,7},{7,6},{8,9},{9,8},{10,11... | collective-permute-start | bytes 589832 | tf_op jit(solution)/shard_map/ppermute | solution.py:41
  10.3 11.3 %collective-permute-start.7 = (f32[1,2,48,512]{3,2,1,0:T(8,128)S(1)}, f32[1,2,48,512]{3,2,1,0:T(8,128)S(1)}, u32[]{:S(2)}, u32[]{:S(2)}) collective-permute-start(f32[1,2,48,512]{3,2,1,0:T(8,128)S(1)} %add.38), channel_id=1, source_target_pairs={{0,2},{1,5},{2,0},{3,7},{4,6},{5,1},{6,4},{7,3},{8,10},{9,13},{10,... | collective-permute-start | bytes 589832 | tf_op jit(solution)/shard_map/ppermute | solution.py:47
  16.8 11.6 %collective-permute-start.3 = (f32[2,80,512]{2,1,0:T(8,128)S(1)}, f32[2,80,512]{2,1,0:T(8,128)S(1)}, u32[]{:S(2)}, u32[]{:S(2)}) collective-permute-start(f32[2,80,512]{2,1,0:T(8,128)S(1)} %add_bitcast_fusion), channel_id=1, source_target_pairs={{0,4},{1,3},{2,6},{3,1},{4,0},{5,7},{6,2},{7,5},{8,12},{9,11},{10,... | collective-permute-start | bytes 983048 | tf_op jit(solution)/shard_map/ppermute | solution.py:47
  21.7 10.3 %collective-permute-start.8 = (f32[2,48,512]{2,1,0:T(8,128)S(1)}, f32[2,48,512]{2,1,0:T(8,128)S(1)}, u32[]{:S(2)}, u32[]{:S(2)}) collective-permute-start(f32[2,48,512]{2,1,0:T(8,128)S(1)} %add_bitcast_fusion.1), channel_id=1, source_target_pairs={{0,4},{1,3},{2,6},{3,1},{4,0},{5,7},{6,2},{7,5},{8,12},{9,11},{10,... | collective-permute-start | bytes 589832 | tf_op jit(solution)/shard_map/ppermute | solution.py:47
  28.4 6.7 %collective-permute-start.4 = (f32[2,80,512]{2,1,0:T(8,128)S(1)}, f32[2,80,512]{2,1,0:T(8,128)S(1)}, u32[]{:S(2)}, u32[]{:S(2)}) collective-permute-start(f32[2,80,512]{2,1,0:T(8,128)S(1)} %add.36.refs_0_), channel_id=1, source_target_pairs={{0,1},{1,0},{2,3},{3,2},{4,5},{5,4},{6,7},{7,6},{8,9},{9,8},{10,11... | collective-permute-start | bytes 983048 | tf_op jit(solution)/shard_map/ppermute | solution.py:41
  29.5 9.9 %collective-permute-start.10 = (f32[2,80,512]{2,1,0:T(8,128)S(1)}, f32[2,80,512]{2,1,0:T(8,128)S(1)}, u32[]{:S(2)}, u32[]{:S(2)}) collective-permute-start(f32[2,80,512]{2,1,0:T(8,128)S(1)} %add.36.refs_0_), channel_id=1, source_target_pairs={{0,2},{1,5},{2,0},{3,7},{4,6},{5,1},{6,4},{7,3},{8,10},{9,13},{10,... | collective-permute-start | bytes 983048 | tf_op jit(solution)/shard_map/ppermute | solution.py:47
  32.1 3.1 %collective-permute-start.9 = (f32[2,48,512]{2,1,0:T(8,128)S(1)}, f32[2,48,512]{2,1,0:T(8,128)S(1)}, u32[]{:S(2)}, u32[]{:S(2)}) collective-permute-start(f32[2,48,512]{2,1,0:T(8,128)S(1)} %add.40.refs_2_), channel_id=1, source_target_pairs={{0,1},{1,0},{2,3},{3,2},{4,5},{5,4},{6,7},{7,6},{8,9},{9,8},{10,11... | collective-permute-start | bytes 589832 | tf_op jit(solution)/shard_map/ppermute | solution.py:41
  32.7 10.8 %collective-permute-start.11 = (f32[2,48,512]{2,1,0:T(8,128)S(1)}, f32[2,48,512]{2,1,0:T(8,128)S(1)}, u32[]{:S(2)}, u32[]{:S(2)}) collective-permute-start(f32[2,48,512]{2,1,0:T(8,128)S(1)} %add.40.refs_2_), channel_id=1, source_target_pairs={{0,2},{1,5},{2,0},{3,7},{4,6},{5,1},{6,4},{7,3},{8,10},{9,13},{10,... | collective-permute-start | bytes 589832 | tf_op jit(solution)/shard_map/ppermute | solution.py:47
  39.4 6.5 %collective-permute-start.12 = (f32[2,80,512]{2,1,0:T(8,128)S(1)}, f32[2,80,512]{2,1,0:T(8,128)S(1)}, u32[]{:S(2)}, u32[]{:S(2)}) collective-permute-start(f32[2,80,512]{2,1,0:T(8,128)S(1)} %collective-permute-done.10.refs_4_.refs_0_), channel_id=1, source_target_pairs={{0,1},{1,0},{2,3},{3,2},{4,5},{5,4},{6,7},{7,6},{8,9},{9,8},{10,11... | collective-permute-start | bytes 983048 | tf_op jit(solution)/shard_map/ppermute | solution.py:41
  43.6 2.3 %collective-permute-start.13 = (f32[2,48,512]{2,1,0:T(8,128)S(1)}, f32[2,48,512]{2,1,0:T(8,128)S(1)}, u32[]{:S(2)}, u32[]{:S(2)}) collective-permute-start(f32[2,48,512]{2,1,0:T(8,128)S(1)} %collective-permute-done.11.refs_5_.refs_1_), channel_id=1, source_target_pairs={{0,1},{1,0},{2,3},{3,2},{4,5},{5,4},{6,7},{7,6},{8,9},{9,8},{10,11... | collective-permute-start | bytes 589832 | tf_op jit(solution)/shard_map/ppermute | solution.py:41
  47.6 2.3 %collective-permute-start.17 = (f32[2,2,64,512]{3,2,1,0:T(8,128)S(1)}, f32[2,2,64,512]{3,2,1,0:T(8,128)S(1)}, u32[]{:S(2)}, u32[]{:S(2)}) collective-permute-start(f32[2,2,64,512]{3,2,1,0:T(8,128)S(1)} %adjoint.12.ready), channel_id=1, source_target_pairs={{0,1},{1,0},{2,3},{3,2},{4,5},{5,4},{6,7},{7,6},{8,9},{9,8},{10,11... | collective-permute-start | bytes 1572872 | tf_op jit(solution)/shard_map/ppermute | solution.py:41
  49.8 6.5 %collective-permute-start.16 = (f32[2,2,64,512]{3,2,1,0:T(8,128)S(1)}, f32[2,2,64,512]{3,2,1,0:T(8,128)S(1)}, u32[]{:S(2)}, u32[]{:S(2)}) collective-permute-start(f32[2,2,64,512]{3,2,1,0:T(8,128)S(1)} %adjoint.14.ready), channel_id=1, source_target_pairs={{0,1},{1,0},{2,3},{3,2},{4,5},{5,4},{6,7},{7,6},{8,9},{9,8},{10,11... | collective-permute-start | bytes 1572872 | tf_op jit(solution)/shard_map/ppermute | solution.py:41
  50.1 9.1 %collective-permute-start.19 = (f32[1,2,64,512]{3,2,1,0:T(8,128)S(1)}, f32[1,2,64,512]{3,2,1,0:T(8,128)S(1)}, u32[]{:S(2)}, u32[]{:S(2)}) collective-permute-start(f32[1,2,64,512]{3,2,1,0:T(8,128)S(1)} %get-tuple-element.43), channel_id=1, source_target_pairs={{0,2},{1,5},{2,0},{3,7},{4,6},{5,1},{6,4},{7,3},{8,10},{9,13},{10,... | collective-permute-start | bytes 786440 | tf_op jit(solution)/shard_map/ppermute | solution.py:47
  51.5 10.8 %collective-permute-start.14 = (f32[2,72,512]{2,1,0:T(8,128)S(1)}, f32[2,72,512]{2,1,0:T(8,128)S(1)}, u32[]{:S(2)}, u32[]{:S(2)}) collective-permute-start(f32[2,72,512]{2,1,0:T(8,128)S(1)} %get-tuple-element.36), channel_id=1, source_target_pairs={{0,8},{8,16},{16,24},{24,0},{1,9},{9,17},{17,25},{25,1},{2,10},{10... | collective-permute-start | bytes 884744 | tf_op jit(solution)/shard_map/ppermute | solution.py:387
  53.1 15.4 %collective-permute-start.15 = (f32[2,72,512]{2,1,0:T(8,128)S(1)}, f32[2,72,512]{2,1,0:T(8,128)S(1)}, u32[]{:S(2)}, u32[]{:S(2)}) collective-permute-start(f32[2,72,512]{2,1,0:T(8,128)S(1)} %get-tuple-element.37), channel_id=1, source_target_pairs={{8,0},{16,8},{24,16},{0,24},{9,1},{17,9},{25,17},{1,25},{10,2},{18... | collective-permute-start | bytes 884744 | tf_op jit(solution)/shard_map/ppermute | solution.py:388
  55.4 13.2 %collective-permute-start.18 = (f32[1,2,64,512]{3,2,1,0:T(8,128)S(1)}, f32[1,2,64,512]{3,2,1,0:T(8,128)S(1)}, u32[]{:S(2)}, u32[]{:S(2)}) collective-permute-start(f32[1,2,64,512]{3,2,1,0:T(8,128)S(1)} %get-tuple-element.44), channel_id=1, source_target_pairs={{0,2},{1,5},{2,0},{3,7},{4,6},{5,1},{6,4},{7,3},{8,10},{9,13},{10,... | collective-permute-start | bytes 786440 | tf_op jit(solution)/shard_map/ppermute | solution.py:47
  59.2 10.3 %collective-permute-start.20 = (f32[1,2,64,512]{3,2,1,0:T(8,128)S(1)}, f32[1,2,64,512]{3,2,1,0:T(8,128)S(1)}, u32[]{:S(2)}, u32[]{:S(2)}) collective-permute-start(f32[1,2,64,512]{3,2,1,0:T(8,128)S(1)} %get-tuple-element.41), channel_id=1, source_target_pairs={{0,4},{1,3},{2,6},{3,1},{4,0},{5,7},{6,2},{7,5},{8,12},{9,11},{10,... | collective-permute-start | bytes 786440 | tf_op jit(solution)/shard_map/ppermute | solution.py:47

commit v5 on v4

--- a/solution.py
+++ b/solution.py
@@ -114,19 +114,14 @@
     )(me, table, data.reshape(2 * length, length), sens, me if ready is None else ready)
 
 
-def core_sums(groups, me, table, data, sens):
-    halves = []
-    ready = None
-    for half in (1, 0):
-        ours = [
-            [group[half * (len(group) // 2) : (half + 1) * (len(group) // 2)] for group in part]
-            for part in groups
-        ]
-        others = adjoint(ours[0], me, table, data, sens, ready)
-        owns = adjoint(ours[1], me, table, data, sens, others[0])
-        halves.append([own + swap_cores(other) for own, other in zip(owns, others)])
-        ready = owns[0]
-    return list(zip(halves[1], halves[0]))
+def core_sums(plan, me, table, data, sens):
+    terms, ready = {}, None
+    for groups in plan:
+        results = adjoint([blocks for _, _, blocks in groups], me, table, data, sens, ready)
+        terms.update(((name, flip), value) for (name, flip, _), value in zip(groups, results))
+        ready = results[0]
+    names = [name for name, flip in terms if flip]
+    return {name: terms[name, 0] + swap_cores(terms[name, 1]) for name in names}
 
 
 def columns_kernel(groups, me, table, *refs):
@@ -305,11 +300,19 @@
         return start, size
 
     places = halving_order(top - 1)
-    groups = [
-        [[chunk_block(chunk, flip, place) for place in places] for chunk in range(len(chunks))]
-        for flip in (1, 0)
+    middle = len(places) // 2
+    sent, kept = [], []
+    for chunk in range(len(chunks)):
+        blocks = [[chunk_block(chunk, flip, place) for place in places] for flip in (0, 1)]
+        sent.append([(("send", chunk), flip, blocks[flip][middle:]) for flip in (0, 1)])
+        kept.append([(("keep", chunk), flip, blocks[flip][:middle]) for flip in (0, 1)])
+    plan = [
+        [sent[0][1]],
+        [sent[0][0]] + [own_other[1] for own_other in sent[1:] + kept],
+        [own_other[0] for own_other in sent[1:] + kept],
     ]
-    currents = core_sums(groups, me, table, measured, sens)
+    sums = core_sums(plan, me, table, measured, sens)
+    currents = [(sums["keep", chunk], sums["send", chunk]) for chunk in range(len(chunks))]
     arrived = []
     for current in currents:
         keep, send = current
@@ -358,19 +361,23 @@
         )
 
     places = halving_order(top)
-    groups = [
-        [[row_block(part, flip, place) for place in places] for part in range(len(parts))]
-        for flip in (1, 0)
-    ]
-    summed = core_sums(groups, me, table, resid, sens)
-    keep, send = summed[0]
+    blocks = [[row_block(0, flip, place) for place in places] for flip in (0, 1)]
+    middle, quarter = len(places) // 2, len(places) // 4
+    passed = [("passed", flip, blocks[flip][middle + quarter :]) for flip in (0, 1)]
+    stays = [("stays", flip, blocks[flip][middle : middle + quarter]) for flip in (0, 1)]
+    kept = [("keep", flip, blocks[flip][:middle]) for flip in (0, 1)]
+    both = [("send", flip, blocks[flip][middle:]) for flip in (0, 1)]
+    plan = [[both[1]], [both[0], kept[1]], [kept[0]]]
+    sums = core_sums(plan, me, table, resid, sens)
+    keep, passed, stays = sums["keep"], sums["send"][quarter:], sums["send"][:quarter]
     for step in range(top - 1):
         middle = keep.shape[0] // 2
-        passed = keep[middle:] + swap_chips(send[middle:], step)
-        kept = [keep[:middle], swap_chips(send[:middle], step)]
+        if step:
+            passed, stays = send[middle:], send[:middle]
+        send = keep[middle:] + swap_chips(passed, step)
+        kept = [keep[:middle], swap_chips(stays, step)]
         if step < top - 2:
             keep = kept[0] + kept[1]
-        send = passed
     gradient = swap_chips(send, top - 1)
 
     extended, to_before, to_after = pl.pallas_call(

time: 70.8 us -> 70 us (0.989)
    pallas_call x8 -> x6, Pallas kernels: 6.7 us -> 6.14 us  [adjoint(): pl.pallas_call(partial(adjoint_kernel, groups), out_shape=[jax.ShapeDtype...]
  transfers between devices with their start and end apart: 21 -> 21, of which waited for: 12 -> 11; matrix products, arithmetic and copies ran while one was open for 1% -> 1% of each run, Pallas kernels for 12% -> 11%
where the time goes in v5:
time: 70 us; the launch traced here: 69.5 us
  waiting for transfers between devices  28.4 us (41%)
  starting transfers between devices  27.2 us (39%)
  Pallas kernels  10.3 us (15%)
  other arithmetic  2.92 us (4%)
    ppermute x9, waiting for transfers between devices, swap_chips(): lax.ppermute(value, 'coil', [(i, i ^ 1 << orders[i & 1][step]) for i in r...  20.5 us
    ppermute x9, starting transfers between devices, swap_chips(): lax.ppermute(value, 'coil', [(i, i ^ 1 << orders[i & 1][step]) for i in r...  18.4 us
    ppermute x1, waiting for transfers between devices, shards(): after = lax.ppermute(to_before, 'slab', behind)  6.15 us
    pallas_call x6, Pallas kernels, adjoint(): pl.pallas_call(partial(adjoint_kernel, groups), out_shape=[jax.ShapeDtype...  6.14 us
    ppermute x10, starting transfers between devices, swap_cores(): return lax.ppermute(value, 'coil', [(i, i ^ 1) for i in range(count)])  5.87 us
    pallas_call x3, Pallas kernels, forward(): pl.pallas_call(partial(forward_kernel, blocks, stage), out_shape=resid if...  3.11 us
    mul x2, other arithmetic, shards(): measured = kspace * mask[None]  1.71 us
    ppermute x1, starting transfers between devices, shards(): before = lax.ppermute(to_after, 'slab', ahead)  1.54 us
  transfers between devices with their start and end apart: 21, of which 11 were waited for; matrix products, arithmetic and copies ran while one was open for 1% of the time, Pallas kernels for 11%

profile of v5, /device:TPU:0, one launch (start us, length us, event | category | flops | bytes accessed | tf_op | source)
XLA Modules:
  0.0 69.5 jit_solution(12740260990415009474)
XLA Ops:
  0.0 1.5 %convert_bitcast_fusion.refs_3_ = bf16[512,512]{1,0:T(8,128)(2,1)S(1)} fusion(s32[1,512,512]{2,1,0:T(8,128)} %param.6), kind=kLoop, calls=%fused_computation.1 | loop fusion | flops 262144 | bytes 1572864 | tf_op jit(solution)/shard_map/mul | solution.py:282
  3.3 1.4 %adjoint.7 = (f32[1,2,80,512]{3,2,1,0:T(8,128)S(1)}, f32[1,2,48,512]{3,2,1,0:T(8,128)S(1)}, f32[1,2,80,512]{3,2,1,0:T(8,128)S(1)}, f32[1,2,48,512]{3,2,1,0:T(8,128)S(1)}) custom-call(s32[1]{0:T(128)} %bitcast.me.ready, bf16[1024,512]{1,0:T(8,128)(2,1)S(1)} %copy-done, bf16[1024,512]{1,0:T(8,128)(2,1)S(1)} %bitcast_multiply_fusion.data, ...), custom_call_target="tpu_custom_call" | custom-call | flops 1073741824 | bytes 4194304 | tf_op jit(solution)/shard_map/adjoint/pallas_call | solution.py:103
  4.9 3.1 %collective-permute-start.2 = (f32[1,2,80,512]{3,2,1,0:T(8,128)S(1)}, f32[1,2,80,512]{3,2,1,0:T(8,128)S(1)}, u32[]{:S(2)}, u32[]{:S(2)}) collective-permute-start(f32[1,2,80,512]{3,2,1,0:T(8,128)S(1)} %add.34), channel_id=1, source_target_pairs={{0,2},{1,5},{2,0},{3,7},{4,6},{5,1},{6,4},{7,3},{8,10},{9,13},{10,... | collective-permute-start | bytes 983048 | tf_op jit(solution)/shard_map/ppermute | solution.py:47
  9.9 1.6 %collective-permute-start.7 = (f32[1,2,48,512]{3,2,1,0:T(8,128)S(1)}, f32[1,2,48,512]{3,2,1,0:T(8,128)S(1)}, u32[]{:S(2)}, u32[]{:S(2)}) collective-permute-start(f32[1,2,48,512]{3,2,1,0:T(8,128)S(1)} %add.38), channel_id=1, source_target_pairs={{0,2},{1,5},{2,0},{3,7},{4,6},{5,1},{6,4},{7,3},{8,10},{9,13},{10,... | collective-permute-start | bytes 589832 | tf_op jit(solution)/shard_map/ppermute | solution.py:47
  11.5 4.7 %collective-permute-done.2 = f32[1,2,80,512]{3,2,1,0:T(8,128)S(1)} collective-permute-done((f32[1,2,80,512]{3,2,1,0:T(8,128)S(1)}, f32[1,2,80,512]{3,2,1,0:T(8,128)S(1)}, u32[]{:S(2)}, u32[]{:S(2)}) %collective-permute-start.2) | collective-permute-done | bytes 327712 | tf_op jit(solution)/shard_map/ppermute | solution.py:47
  16.3 3.5 %collective-permute-start.3 = (f32[2,80,512]{2,1,0:T(8,128)S(1)}, f32[2,80,512]{2,1,0:T(8,128)S(1)}, u32[]{:S(2)}, u32[]{:S(2)}) collective-permute-start(f32[2,80,512]{2,1,0:T(8,128)S(1)} %add_bitcast_fusion), channel_id=1, source_target_pairs={{0,4},{1,3},{2,6},{3,1},{4,0},{5,7},{6,2},{7,5},{8,12},{9,11},{10,... | collective-permute-start | bytes 983048 | tf_op jit(solution)/shard_map/ppermute | solution.py:47
  19.8 1.4 %collective-permute-done.7 = f32[1,2,48,512]{3,2,1,0:T(8,128)S(1)} collective-permute-done((f32[1,2,48,512]{3,2,1,0:T(8,128)S(1)}, f32[1,2,48,512]{3,2,1,0:T(8,128)S(1)}, u32[]{:S(2)}, u32[]{:S(2)}) %collective-permute-start.7) | collective-permute-done | bytes 196640 | tf_op jit(solution)/shard_map/ppermute | solution.py:47
  21.2 2.4 %collective-permute-start.8 = (f32[2,48,512]{2,1,0:T(8,128)S(1)}, f32[2,48,512]{2,1,0:T(8,128)S(1)}, u32[]{:S(2)}, u32[]{:S(2)}) collective-permute-start(f32[2,48,512]{2,1,0:T(8,128)S(1)} %add_bitcast_fusion.1), channel_id=1, source_target_pairs={{0,4},{1,3},{2,6},{3,1},{4,0},{5,7},{6,2},{7,5},{8,12},{9,11},{10,... | collective-permute-start | bytes 589832 | tf_op jit(solution)/shard_map/ppermute | solution.py:47
  23.7 4.3 %collective-permute-done.3 = f32[2,80,512]{2,1,0:T(8,128)S(1)} collective-permute-done((f32[2,80,512]{2,1,0:T(8,128)S(1)}, f32[2,80,512]{2,1,0:T(8,128)S(1)}, u32[]{:S(2)}, u32[]{:S(2)}) %collective-permute-start.3) | collective-permute-done | bytes 327712 | tf_op jit(solution)/shard_map/ppermute | solution.py:47
  29.0 1.6 %collective-permute-start.10 = (f32[2,80,512]{2,1,0:T(8,128)S(1)}, f32[2,80,512]{2,1,0:T(8,128)S(1)}, u32[]{:S(2)}, u32[]{:S(2)}) collective-permute-start(f32[2,80,512]{2,1,0:T(8,128)S(1)} %add.36.refs_0_), channel_id=1, source_target_pairs={{0,2},{1,5},{2,0},{3,7},{4,6},{5,1},{6,4},{7,3},{8,10},{9,13},{10,... | collective-permute-start | bytes 983048 | tf_op jit(solution)/shard_map/ppermute | solution.py:47
  32.3 2.4 %collective-permute-start.11 = (f32[2,48,512]{2,1,0:T(8,128)S(1)}, f32[2,48,512]{2,1,0:T(8,128)S(1)}, u32[]{:S(2)}, u32[]{:S(2)}) collective-permute-start(f32[2,48,512]{2,1,0:T(8,128)S(1)} %add.40.refs_2_), channel_id=1, source_target_pairs={{0,2},{1,5},{2,0},{3,7},{4,6},{5,1},{6,4},{7,3},{8,10},{9,13},{10,... | collective-permute-start | bytes 589832 | tf_op jit(solution)/shard_map/ppermute | solution.py:47
  34.7 1.4 %forward.3.refs_2_ = f32[512,1024]{1,0:T(8,128)S(1)} custom-call(s32[1]{0:T(128)} %bitcast.me.ready, bf16[1024,512]{1,0:T(8,128)(2,1)S(1)} %copy-done, bf16[512,512]{1,0:T(8,128)(2,1)S(1)} %get-tuple-element.31.left, bf16[2,512,512]{2,1,0:T(8,128)(2,1)S(1)} %bitcast.23, f32[2,80,512]{2,1,0:T(8,128)S(1)} %add.36.refs_0_, ...), custom_call_target="tpu_custom_call" | custom-call | flops 1073741824 | bytes 4194304 | tf_op jit(solution)/shard_map/forward/pallas_call | solution.py:198
  36.0 2.9 %collective-permute-done.10.refs_4_.refs_0_ = f32[2,80,512]{2,1,0:T(8,128)S(1)} collective-permute-done((f32[2,80,512]{2,1,0:T(8,128)S(1)}, f32[2,80,512]{2,1,0:T(8,128)S(1)}, u32[]{:S(2)}, u32[]{:S(2)}) %collective-permute-start.10) | collective-permute-done | bytes 327712 | tf_op jit(solution)/shard_map/ppermute | solution.py:47
  38.9 1.2 %collective-permute-start.12 = (f32[2,80,512]{2,1,0:T(8,128)S(1)}, f32[2,80,512]{2,1,0:T(8,128)S(1)}, u32[]{:S(2)}, u32[]{:S(2)}) collective-permute-start(f32[2,80,512]{2,1,0:T(8,128)S(1)} %collective-permute-done.10.refs_4_.refs_0_), channel_id=1, source_target_pairs={{0,1},{1,0},{2,3},{3,2},{4,5},{5,4},{6,7},{7,6},{8,9},{9,8},{10,11... | collective-permute-start | bytes 983048 | tf_op jit(solution)/shard_map/ppermute | solution.py:41
  40.1 3.0 %collective-permute-done.11.refs_5_.refs_1_ = f32[2,48,512]{2,1,0:T(8,128)S(1)} collective-permute-done((f32[2,48,512]{2,1,0:T(8,128)S(1)}, f32[2,48,512]{2,1,0:T(8,128)S(1)}, u32[]{:S(2)}, u32[]{:S(2)}) %collective-permute-start.11) | collective-permute-done | bytes 196640 | tf_op jit(solution)/shard_map/ppermute | solution.py:47
  43.1 1.2 %collective-permute-start.13 = (f32[2,48,512]{2,1,0:T(8,128)S(1)}, f32[2,48,512]{2,1,0:T(8,128)S(1)}, u32[]{:S(2)}, u32[]{:S(2)}) collective-permute-start(f32[2,48,512]{2,1,0:T(8,128)S(1)} %collective-permute-done.11.refs_5_.refs_1_), channel_id=1, source_target_pairs={{0,1},{1,0},{2,3},{3,2},{4,5},{5,4},{6,7},{7,6},{8,9},{9,8},{10,11... | collective-permute-start | bytes 589832 | tf_op jit(solution)/shard_map/ppermute | solution.py:41
  47.6 1.4 %adjoint.10 = (f32[2,2,64,512]{3,2,1,0:T(8,128)S(1)}, f32[2,2,64,512]{3,2,1,0:T(8,128)S(1)}) custom-call(s32[1]{0:T(128)} %bitcast.me.ready, bf16[1024,512]{1,0:T(8,128)(2,1)S(1)} %copy-done, bf16[1024,512]{1,0:T(8,128)(2,1)S(1)} %bitcast.30, bf16[2,512,512]{2,1,0:T(8,128)(2,1)S(1)} %bitcast.27, f32[2,2,64,512]{3,2,1,0:T(8,128)S(1)} %adjoint.9.ready), custom_call_target="tpu_custom_call" | custom-call | flops 1073741824 | bytes 4194304 | tf_op jit(solution)/shard_map/adjoint/pallas_call | solution.py:103
  49.3 1.3 %collective-permute-start.19 = (f32[1,2,64,512]{3,2,1,0:T(8,128)S(1)}, f32[1,2,64,512]{3,2,1,0:T(8,128)S(1)}, u32[]{:S(2)}, u32[]{:S(2)}) collective-permute-start(f32[1,2,64,512]{3,2,1,0:T(8,128)S(1)} %get-tuple-element.45), channel_id=1, source_target_pairs={{0,2},{1,5},{2,0},{3,7},{4,6},{5,1},{6,4},{7,3},{8,10},{9,13},{10,... | collective-permute-start | bytes 786440 | tf_op jit(solution)/shard_map/ppermute | solution.py:47
  50.8 1.5 %collective-permute-start.14 = (f32[2,72,512]{2,1,0:T(8,128)S(1)}, f32[2,72,512]{2,1,0:T(8,128)S(1)}, u32[]{:S(2)}, u32[]{:S(2)}) collective-permute-start(f32[2,72,512]{2,1,0:T(8,128)S(1)} %get-tuple-element.36), channel_id=1, source_target_pairs={{0,8},{8,16},{16,24},{24,0},{1,9},{9,17},{17,25},{25,1},{2,10},{10... | collective-permute-start | bytes 884744 | tf_op jit(solution)/shard_map/ppermute | solution.py:394
  52.3 1.4 %collective-permute-start.15 = (f32[2,72,512]{2,1,0:T(8,128)S(1)}, f32[2,72,512]{2,1,0:T(8,128)S(1)}, u32[]{:S(2)}, u32[]{:S(2)}) collective-permute-start(f32[2,72,512]{2,1,0:T(8,128)S(1)} %get-tuple-element.37), channel_id=1, source_target_pairs={{8,0},{16,8},{24,16},{0,24},{9,1},{17,9},{25,17},{1,25},{10,2},{18... | collective-permute-start | bytes 884744 | tf_op jit(solution)/shard_map/ppermute | solution.py:395
  55.6 2.8 %collective-permute-done.19 = f32[1,2,64,512]{3,2,1,0:T(8,128)S(1)} collective-permute-done((f32[1,2,64,512]{3,2,1,0:T(8,128)S(1)}, f32[1,2,64,512]{3,2,1,0:T(8,128)S(1)}, u32[]{:S(2)}, u32[]{:S(2)}) %collective-permute-start.19) | collective-permute-done | bytes 262176 | tf_op jit(solution)/shard_map/ppermute | solution.py:47
  58.4 1.6 %collective-permute-start.20 = (f32[1,2,64,512]{3,2,1,0:T(8,128)S(1)}, f32[1,2,64,512]{3,2,1,0:T(8,128)S(1)}, u32[]{:S(2)}, u32[]{:S(2)}) collective-permute-start(f32[1,2,64,512]{3,2,1,0:T(8,128)S(1)} %get-tuple-element.43), channel_id=1, source_target_pairs={{0,4},{1,3},{2,6},{3,1},{4,0},{5,7},{6,2},{7,5},{8,12},{9,11},{10,... | collective-permute-start | bytes 786440 | tf_op jit(solution)/shard_map/ppermute | solution.py:47
  60.1 1.5 %collective-permute-done.14.before = f32[2,72,512]{2,1,0:T(8,128)S(1)} collective-permute-done((f32[2,72,512]{2,1,0:T(8,128)S(1)}, f32[2,72,512]{2,1,0:T(8,128)S(1)}, u32[]{:S(2)}, u32[]{:S(2)}) %collective-permute-start.14) | collective-permute-done | bytes 294944 | tf_op jit(solution)/shard_map/ppermute | solution.py:394
  61.6 6.1 %collective-permute-done.15.after = f32[2,72,512]{2,1,0:T(8,128)S(1)} collective-permute-done((f32[2,72,512]{2,1,0:T(8,128)S(1)}, f32[2,72,512]{2,1,0:T(8,128)S(1)}, u32[]{:S(2)}, u32[]{:S(2)}) %collective-permute-start.15) | collective-permute-done | bytes 294944 | tf_op jit(solution)/shard_map/ppermute | solution.py:395
  (49 shorter events, 14.0 us)
Async XLA Ops:
  0.0 1.5 %copy-start.2 = (bf16[1,1,2,512,512]{4,3,2,1,0:T(8,128)(2,1)S(1)}, bf16[1,1,2,512,512]{4,3,2,1,0:T(8,128)(2,1)}, u32[]{:S(2)}) copy-start(bf16[1,1,2,512,512]{4,3,2,1,0:T(8,128)(2,1)} %param.4) | copy-start | bytes 3145732
  0.0 1.9 %copy-start = (bf16[1024,512]{1,0:T(8,128)(2,1)S(1)}, bf16[1024,512]{1,0:T(8,128)(2,1)}, u32[]{:S(2)}) copy-start(bf16[1024,512]{1,0:T(8,128)(2,1)} %constant.8.clone.table) | copy-start | bytes 3145732
  0.0 2.2 %copy-start.1 = (bf16[1,1,2,512,512]{4,3,2,1,0:T(8,128)(2,1)S(1)}, bf16[1,1,2,512,512]{4,3,2,1,0:T(8,128)(2,1)}, u32[]{:S(2)}) copy-start(bf16[1,1,2,512,512]{4,3,2,1,0:T(8,128)(2,1)} %param.5) | copy-start | bytes 3145732
  2.8 2.0 %collective-permute-start.1 = (f32[1,2,80,512]{3,2,1,0:T(8,128)S(1)}, f32[1,2,80,512]{3,2,1,0:T(8,128)S(1)}, u32[]{:S(2)}, u32[]{:S(2)}) collective-permute-start(f32[1,2,80,512]{3,2,1,0:T(8,128)S(1)} %adjoint.6.ready), channel_id=1, source_target_pairs={{0,1},{1,0},{2,3},{3,2},{4,5},{5,4},{6,7},{7,6},{8,9},{9,8},{10,11... | collective-permute-start | bytes 983048 | tf_op jit(solution)/shard_map/ppermute | solution.py:41
  4.7 6.8 %collective-permute-start = (f32[1,2,80,512]{3,2,1,0:T(8,128)S(1)}, f32[1,2,80,512]{3,2,1,0:T(8,128)S(1)}, u32[]{:S(2)}, u32[]{:S(2)}) collective-permute-start(f32[1,2,80,512]{3,2,1,0:T(8,128)S(1)} %get-tuple-element.26), channel_id=1, source_target_pairs={{0,1},{1,0},{2,3},{3,2},{4,5},{5,4},{6,7},{7,6},{8,9},{9,8},{10,11... | collective-permute-start | bytes 983048 | tf_op jit(solution)/shard_map/ppermute | solution.py:41
  4.9 11.3 %collective-permute-start.2 = (f32[1,2,80,512]{3,2,1,0:T(8,128)S(1)}, f32[1,2,80,512]{3,2,1,0:T(8,128)S(1)}, u32[]{:S(2)}, u32[]{:S(2)}) collective-permute-start(f32[1,2,80,512]{3,2,1,0:T(8,128)S(1)} %add.34), channel_id=1, source_target_pairs={{0,2},{1,5},{2,0},{3,7},{4,6},{5,1},{6,4},{7,3},{8,10},{9,13},{10,... | collective-permute-start | bytes 983048 | tf_op jit(solution)/shard_map/ppermute | solution.py:47
  8.0 1.8 %collective-permute-start.6 = (f32[1,2,48,512]{3,2,1,0:T(8,128)S(1)}, f32[1,2,48,512]{3,2,1,0:T(8,128)S(1)}, u32[]{:S(2)}, u32[]{:S(2)}) collective-permute-start(f32[1,2,48,512]{3,2,1,0:T(8,128)S(1)} %get-tuple-element.30), channel_id=1, source_target_pairs={{0,1},{1,0},{2,3},{3,2},{4,5},{5,4},{6,7},{7,6},{8,9},{9,8},{10,11... | collective-permute-start | bytes 589832 | tf_op jit(solution)/shard_map/ppermute | solution.py:41
  8.8 11.0 %collective-permute-start.5 = (f32[1,2,48,512]{3,2,1,0:T(8,128)S(1)}, f32[1,2,48,512]{3,2,1,0:T(8,128)S(1)}, u32[]{:S(2)}, u32[]{:S(2)}) collective-permute-start(f32[1,2,48,512]{3,2,1,0:T(8,128)S(1)} %get-tuple-element.28), channel_id=1, source_target_pairs={{0,1},{1,0},{2,3},{3,2},{4,5},{5,4},{6,7},{7,6},{8,9},{9,8},{10,11... | collective-permute-start | bytes 589832 | tf_op jit(solution)/shard_map/ppermute | solution.py:41
  9.9 11.3 %collective-permute-start.7 = (f32[1,2,48,512]{3,2,1,0:T(8,128)S(1)}, f32[1,2,48,512]{3,2,1,0:T(8,128)S(1)}, u32[]{:S(2)}, u32[]{:S(2)}) collective-permute-start(f32[1,2,48,512]{3,2,1,0:T(8,128)S(1)} %add.38), channel_id=1, source_target_pairs={{0,2},{1,5},{2,0},{3,7},{4,6},{5,1},{6,4},{7,3},{8,10},{9,13},{10,... | collective-permute-start | bytes 589832 | tf_op jit(solution)/shard_map/ppermute | solution.py:47
  16.3 11.6 %collective-permute-start.3 = (f32[2,80,512]{2,1,0:T(8,128)S(1)}, f32[2,80,512]{2,1,0:T(8,128)S(1)}, u32[]{:S(2)}, u32[]{:S(2)}) collective-permute-start(f32[2,80,512]{2,1,0:T(8,128)S(1)} %add_bitcast_fusion), channel_id=1, source_target_pairs={{0,4},{1,3},{2,6},{3,1},{4,0},{5,7},{6,2},{7,5},{8,12},{9,11},{10,... | collective-permute-start | bytes 983048 | tf_op jit(solution)/shard_map/ppermute | solution.py:47
  21.2 10.3 %collective-permute-start.8 = (f32[2,48,512]{2,1,0:T(8,128)S(1)}, f32[2,48,512]{2,1,0:T(8,128)S(1)}, u32[]{:S(2)}, u32[]{:S(2)}) collective-permute-start(f32[2,48,512]{2,1,0:T(8,128)S(1)} %add_bitcast_fusion.1), channel_id=1, source_target_pairs={{0,4},{1,3},{2,6},{3,1},{4,0},{5,7},{6,2},{7,5},{8,12},{9,11},{10,... | collective-permute-start | bytes 589832 | tf_op jit(solution)/shard_map/ppermute | solution.py:47
  28.0 6.7 %collective-permute-start.4 = (f32[2,80,512]{2,1,0:T(8,128)S(1)}, f32[2,80,512]{2,1,0:T(8,128)S(1)}, u32[]{:S(2)}, u32[]{:S(2)}) collective-permute-start(f32[2,80,512]{2,1,0:T(8,128)S(1)} %add.36.refs_0_), channel_id=1, source_target_pairs={{0,1},{1,0},{2,3},{3,2},{4,5},{5,4},{6,7},{7,6},{8,9},{9,8},{10,11... | collective-permute-start | bytes 983048 | tf_op jit(solution)/shard_map/ppermute | solution.py:41
  29.0 9.9 %collective-permute-start.10 = (f32[2,80,512]{2,1,0:T(8,128)S(1)}, f32[2,80,512]{2,1,0:T(8,128)S(1)}, u32[]{:S(2)}, u32[]{:S(2)}) collective-permute-start(f32[2,80,512]{2,1,0:T(8,128)S(1)} %add.36.refs_0_), channel_id=1, source_target_pairs={{0,2},{1,5},{2,0},{3,7},{4,6},{5,1},{6,4},{7,3},{8,10},{9,13},{10,... | collective-permute-start | bytes 983048 | tf_op jit(solution)/shard_map/ppermute | solution.py:47
  31.6 3.1 %collective-permute-start.9 = (f32[2,48,512]{2,1,0:T(8,128)S(1)}, f32[2,48,512]{2,1,0:T(8,128)S(1)}, u32[]{:S(2)}, u32[]{:S(2)}) collective-permute-start(f32[2,48,512]{2,1,0:T(8,128)S(1)} %add.40.refs_2_), channel_id=1, source_target_pairs={{0,1},{1,0},{2,3},{3,2},{4,5},{5,4},{6,7},{7,6},{8,9},{9,8},{10,11... | collective-permute-start | bytes 589832 | tf_op jit(solution)/shard_map/ppermute | solution.py:41
  32.3 10.8 %collective-permute-start.11 = (f32[2,48,512]{2,1,0:T(8,128)S(1)}, f32[2,48,512]{2,1,0:T(8,128)S(1)}, u32[]{:S(2)}, u32[]{:S(2)}) collective-permute-start(f32[2,48,512]{2,1,0:T(8,128)S(1)} %add.40.refs_2_), channel_id=1, source_target_pairs={{0,2},{1,5},{2,0},{3,7},{4,6},{5,1},{6,4},{7,3},{8,10},{9,13},{10,... | collective-permute-start | bytes 589832 | tf_op jit(solution)/shard_map/ppermute | solution.py:47
  38.9 6.5 %collective-permute-start.12 = (f32[2,80,512]{2,1,0:T(8,128)S(1)}, f32[2,80,512]{2,1,0:T(8,128)S(1)}, u32[]{:S(2)}, u32[]{:S(2)}) collective-permute-start(f32[2,80,512]{2,1,0:T(8,128)S(1)} %collective-permute-done.10.refs_4_.refs_0_), channel_id=1, source_target_pairs={{0,1},{1,0},{2,3},{3,2},{4,5},{5,4},{6,7},{7,6},{8,9},{9,8},{10,11... | collective-permute-start | bytes 983048 | tf_op jit(solution)/shard_map/ppermute | solution.py:41
  43.1 2.3 %collective-permute-start.13 = (f32[2,48,512]{2,1,0:T(8,128)S(1)}, f32[2,48,512]{2,1,0:T(8,128)S(1)}, u32[]{:S(2)}, u32[]{:S(2)}) collective-permute-start(f32[2,48,512]{2,1,0:T(8,128)S(1)} %collective-permute-done.11.refs_5_.refs_1_), channel_id=1, source_target_pairs={{0,1},{1,0},{2,3},{3,2},{4,5},{5,4},{6,7},{7,6},{8,9},{9,8},{10,11... | collective-permute-start | bytes 589832 | tf_op jit(solution)/shard_map/ppermute | solution.py:41
  47.1 2.0 %collective-permute-start.17 = (f32[2,2,64,512]{3,2,1,0:T(8,128)S(1)}, f32[2,2,64,512]{3,2,1,0:T(8,128)S(1)}, u32[]{:S(2)}, u32[]{:S(2)}) collective-permute-start(f32[2,2,64,512]{3,2,1,0:T(8,128)S(1)} %adjoint.9.ready), channel_id=1, source_target_pairs={{0,1},{1,0},{2,3},{3,2},{4,5},{5,4},{6,7},{7,6},{8,9},{9,8},{10,11... | collective-permute-start | bytes 1572872 | tf_op jit(solution)/shard_map/ppermute | solution.py:41
  49.0 6.5 %collective-permute-start.16 = (f32[2,2,64,512]{3,2,1,0:T(8,128)S(1)}, f32[2,2,64,512]{3,2,1,0:T(8,128)S(1)}, u32[]{:S(2)}, u32[]{:S(2)}) collective-permute-start(f32[2,2,64,512]{3,2,1,0:T(8,128)S(1)} %get-tuple-element.42), channel_id=1, source_target_pairs={{0,1},{1,0},{2,3},{3,2},{4,5},{5,4},{6,7},{7,6},{8,9},{9,8},{10,11... | collective-permute-start | bytes 1572872 | tf_op jit(solution)/shard_map/ppermute | solution.py:41
  49.3 9.1 %collective-permute-start.19 = (f32[1,2,64,512]{3,2,1,0:T(8,128)S(1)}, f32[1,2,64,512]{3,2,1,0:T(8,128)S(1)}, u32[]{:S(2)}, u32[]{:S(2)}) collective-permute-start(f32[1,2,64,512]{3,2,1,0:T(8,128)S(1)} %get-tuple-element.45), channel_id=1, source_target_pairs={{0,2},{1,5},{2,0},{3,7},{4,6},{5,1},{6,4},{7,3},{8,10},{9,13},{10,... | collective-permute-start | bytes 786440 | tf_op jit(solution)/shard_map/ppermute | solution.py:47
  50.8 10.8 %collective-permute-start.14 = (f32[2,72,512]{2,1,0:T(8,128)S(1)}, f32[2,72,512]{2,1,0:T(8,128)S(1)}, u32[]{:S(2)}, u32[]{:S(2)}) collective-permute-start(f32[2,72,512]{2,1,0:T(8,128)S(1)} %get-tuple-element.36), channel_id=1, source_target_pairs={{0,8},{8,16},{16,24},{24,0},{1,9},{9,17},{17,25},{25,1},{2,10},{10... | collective-permute-start | bytes 884744 | tf_op jit(solution)/shard_map/ppermute | solution.py:394
  52.3 15.4 %collective-permute-start.15 = (f32[2,72,512]{2,1,0:T(8,128)S(1)}, f32[2,72,512]{2,1,0:T(8,128)S(1)}, u32[]{:S(2)}, u32[]{:S(2)}) collective-permute-start(f32[2,72,512]{2,1,0:T(8,128)S(1)} %get-tuple-element.37), channel_id=1, source_target_pairs={{8,0},{16,8},{24,16},{0,24},{9,1},{17,9},{25,17},{1,25},{10,2},{18... | collective-permute-start | bytes 884744 | tf_op jit(solution)/shard_map/ppermute | solution.py:395
  54.6 13.2 %collective-permute-start.18 = (f32[1,2,64,512]{3,2,1,0:T(8,128)S(1)}, f32[1,2,64,512]{3,2,1,0:T(8,128)S(1)}, u32[]{:S(2)}, u32[]{:S(2)}) collective-permute-start(f32[1,2,64,512]{3,2,1,0:T(8,128)S(1)} %get-tuple-element.46), channel_id=1, source_target_pairs={{0,2},{1,5},{2,0},{3,7},{4,6},{5,1},{6,4},{7,3},{8,10},{9,13},{10,... | collective-permute-start | bytes 786440 | tf_op jit(solution)/shard_map/ppermute | solution.py:47
  58.4 10.3 %collective-permute-start.20 = (f32[1,2,64,512]{3,2,1,0:T(8,128)S(1)}, f32[1,2,64,512]{3,2,1,0:T(8,128)S(1)}, u32[]{:S(2)}, u32[]{:S(2)}) collective-permute-start(f32[1,2,64,512]{3,2,1,0:T(8,128)S(1)} %get-tuple-element.43), channel_id=1, source_target_pairs={{0,4},{1,3},{2,6},{3,1},{4,0},{5,7},{6,2},{7,5},{8,12},{9,11},{10,... | collective-permute-start | bytes 786440 | tf_op jit(solution)/shard_map/ppermute | solution.py:47

commit v6 on v5

--- a/solution.py
+++ b/solution.py
@@ -121,7 +121,13 @@
         terms.update(((name, flip), value) for (name, flip, _), value in zip(groups, results))
         ready = results[0]
     names = [name for name, flip in terms if flip]
-    return {name: terms[name, 0] + swap_cores(terms[name, 1]) for name in names}
+    sums = {}
+    for name in names:
+        theirs = terms[name, 1]
+        if sums and isinstance(name, tuple):
+            theirs, _ = lax.optimization_barrier((theirs, sums[names[0]]))
+        sums[name] = terms[name, 0] + swap_cores(theirs)
+    return sums
 
 
 def columns_kernel(groups, me, table, *refs):

time: 70 us -> 69.9 us (level)
  waiting for transfers between devices: 28.4 us -> 27.6 us
    ppermute x9, waiting for transfers between devices: 20.5 us -> 19.6 us  [swap_chips(): lax.ppermute(value, 'coil', [(i, i ^ 1 << orders[i & 1][step]) for i in r...]
where the time goes in v6:
time: 69.9 us; the launch traced here: 69.3 us
  starting transfers between devices  27.9 us (40%)
  waiting for transfers between devices  27.6 us (39%)
  Pallas kernels  10.3 us (15%)
  other arithmetic  2.92 us (4%)
    ppermute x9, waiting for transfers between devices, swap_chips(): lax.ppermute(value, 'coil', [(i, i ^ 1 << orders[i & 1][step]) for i in r...  19.6 us
    ppermute x9, starting transfers between devices, swap_chips(): lax.ppermute(value, 'coil', [(i, i ^ 1 << orders[i & 1][step]) for i in r...  18.8 us
    pallas_call x6, Pallas kernels, adjoint(): pl.pallas_call(partial(adjoint_kernel, groups), out_shape=[jax.ShapeDtype...  6.14 us
    ppermute x10, starting transfers between devices, swap_cores(): return lax.ppermute(value, 'coil', [(i, i ^ 1) for i in range(count)])  6.13 us
    ppermute x1, waiting for transfers between devices, shards(): after = lax.ppermute(to_before, 'slab', behind)  6.04 us
    pallas_call x3, Pallas kernels, forward(): pl.pallas_call(partial(forward_kernel, blocks, stage), out_shape=resid if...  3.11 us
    mul x2, other arithmetic, shards(): measured = kspace * mask[None]  1.71 us
    ppermute x1, waiting for transfers between devices, shards(): before = lax.ppermute(to_after, 'slab', ahead)  1.67 us
  transfers between devices with their start and end apart: 21, of which 11 were waited for; matrix products, arithmetic and copies ran while one was open for 1% of the time, Pallas kernels for 11%

profile of v6, /device:TPU:0, one launch (start us, length us, event | category | flops | bytes accessed | tf_op | source)
XLA Modules:
  0.0 69.3 jit_solution(655862836168518062)
XLA Ops:
  0.0 1.5 %convert_bitcast_fusion.refs_3_ = bf16[512,512]{1,0:T(8,128)(2,1)S(1)} fusion(s32[1,512,512]{2,1,0:T(8,128)} %param.6), kind=kLoop, calls=%fused_computation.1 | loop fusion | flops 262144 | bytes 1572864 | tf_op jit(solution)/shard_map/mul | solution.py:288
  3.3 1.4 %adjoint.7 = (f32[1,2,80,512]{3,2,1,0:T(8,128)S(1)}, f32[1,2,48,512]{3,2,1,0:T(8,128)S(1)}, f32[1,2,80,512]{3,2,1,0:T(8,128)S(1)}, f32[1,2,48,512]{3,2,1,0:T(8,128)S(1)}) custom-call(s32[1]{0:T(128)} %bitcast.me.ready, bf16[1024,512]{1,0:T(8,128)(2,1)S(1)} %copy-done, bf16[1024,512]{1,0:T(8,128)(2,1)S(1)} %bitcast_multiply_fusion.data, ...), custom_call_target="tpu_custom_call" | custom-call | flops 1073741824 | bytes 4194304 | tf_op jit(solution)/shard_map/adjoint/pallas_call | solution.py:103
  5.1 2.9 %collective-permute-start.2 = (f32[1,2,80,512]{3,2,1,0:T(8,128)S(1)}, f32[1,2,80,512]{3,2,1,0:T(8,128)S(1)}, u32[]{:S(2)}, u32[]{:S(2)}) collective-permute-start(f32[1,2,80,512]{3,2,1,0:T(8,128)S(1)} %add.33), channel_id=1, source_target_pairs={{0,2},{1,5},{2,0},{3,7},{4,6},{5,1},{6,4},{7,3},{8,10},{9,13},{10,... | collective-permute-start | bytes 983048 | tf_op jit(solution)/shard_map/ppermute | solution.py:47
  10.1 1.6 %collective-permute-start.7 = (f32[1,2,48,512]{3,2,1,0:T(8,128)S(1)}, f32[1,2,48,512]{3,2,1,0:T(8,128)S(1)}, u32[]{:S(2)}, u32[]{:S(2)}) collective-permute-start(f32[1,2,48,512]{3,2,1,0:T(8,128)S(1)} %add.38), channel_id=1, source_target_pairs={{0,2},{1,5},{2,0},{3,7},{4,6},{5,1},{6,4},{7,3},{8,10},{9,13},{10,... | collective-permute-start | bytes 589832 | tf_op jit(solution)/shard_map/ppermute | solution.py:47
  11.7 4.4 %collective-permute-done.2 = f32[1,2,80,512]{3,2,1,0:T(8,128)S(1)} collective-permute-done((f32[1,2,80,512]{3,2,1,0:T(8,128)S(1)}, f32[1,2,80,512]{3,2,1,0:T(8,128)S(1)}, u32[]{:S(2)}, u32[]{:S(2)}) %collective-permute-start.2) | collective-permute-done | bytes 327712 | tf_op jit(solution)/shard_map/ppermute | solution.py:47
  16.2 3.5 %collective-permute-start.3 = (f32[2,80,512]{2,1,0:T(8,128)S(1)}, f32[2,80,512]{2,1,0:T(8,128)S(1)}, u32[]{:S(2)}, u32[]{:S(2)}) collective-permute-start(f32[2,80,512]{2,1,0:T(8,128)S(1)} %add_bitcast_fusion), channel_id=1, source_target_pairs={{0,4},{1,3},{2,6},{3,1},{4,0},{5,7},{6,2},{7,5},{8,12},{9,11},{10,... | collective-permute-start | bytes 983048 | tf_op jit(solution)/shard_map/ppermute | solution.py:47
  19.7 1.3 %collective-permute-done.7 = f32[1,2,48,512]{3,2,1,0:T(8,128)S(1)} collective-permute-done((f32[1,2,48,512]{3,2,1,0:T(8,128)S(1)}, f32[1,2,48,512]{3,2,1,0:T(8,128)S(1)}, u32[]{:S(2)}, u32[]{:S(2)}) %collective-permute-start.7) | collective-permute-done | bytes 196640 | tf_op jit(solution)/shard_map/ppermute | solution.py:47
  21.1 2.5 %collective-permute-start.8 = (f32[2,48,512]{2,1,0:T(8,128)S(1)}, f32[2,48,512]{2,1,0:T(8,128)S(1)}, u32[]{:S(2)}, u32[]{:S(2)}) collective-permute-start(f32[2,48,512]{2,1,0:T(8,128)S(1)} %add_bitcast_fusion.1), channel_id=1, source_target_pairs={{0,4},{1,3},{2,6},{3,1},{4,0},{5,7},{6,2},{7,5},{8,12},{9,11},{10,... | collective-permute-start | bytes 589832 | tf_op jit(solution)/shard_map/ppermute | solution.py:47
  23.6 4.3 %collective-permute-done.3 = f32[2,80,512]{2,1,0:T(8,128)S(1)} collective-permute-done((f32[2,80,512]{2,1,0:T(8,128)S(1)}, f32[2,80,512]{2,1,0:T(8,128)S(1)}, u32[]{:S(2)}, u32[]{:S(2)}) %collective-permute-start.3) | collective-permute-done | bytes 327712 | tf_op jit(solution)/shard_map/ppermute | solution.py:47
  28.8 1.9 %collective-permute-start.10 = (f32[2,80,512]{2,1,0:T(8,128)S(1)}, f32[2,80,512]{2,1,0:T(8,128)S(1)}, u32[]{:S(2)}, u32[]{:S(2)}) collective-permute-start(f32[2,80,512]{2,1,0:T(8,128)S(1)} %add.36.refs_0_), channel_id=1, source_target_pairs={{0,2},{1,5},{2,0},{3,7},{4,6},{5,1},{6,4},{7,3},{8,10},{9,13},{10,... | collective-permute-start | bytes 983048 | tf_op jit(solution)/shard_map/ppermute | solution.py:47
  32.2 2.5 %collective-permute-start.11 = (f32[2,48,512]{2,1,0:T(8,128)S(1)}, f32[2,48,512]{2,1,0:T(8,128)S(1)}, u32[]{:S(2)}, u32[]{:S(2)}) collective-permute-start(f32[2,48,512]{2,1,0:T(8,128)S(1)} %add.40.refs_2_), channel_id=1, source_target_pairs={{0,2},{1,5},{2,0},{3,7},{4,6},{5,1},{6,4},{7,3},{8,10},{9,13},{10,... | collective-permute-start | bytes 589832 | tf_op jit(solution)/shard_map/ppermute | solution.py:47
  34.8 1.4 %forward.3.refs_2_ = f32[512,1024]{1,0:T(8,128)S(1)} custom-call(s32[1]{0:T(128)} %bitcast.me.ready, bf16[1024,512]{1,0:T(8,128)(2,1)S(1)} %copy-done, bf16[512,512]{1,0:T(8,128)(2,1)S(1)} %get-tuple-element.37.left, bf16[2,512,512]{2,1,0:T(8,128)(2,1)S(1)} %bitcast.23, f32[2,80,512]{2,1,0:T(8,128)S(1)} %add.36.refs_0_, ...), custom_call_target="tpu_custom_call" | custom-call | flops 1073741824 | bytes 4194304 | tf_op jit(solution)/shard_map/forward/pallas_call | solution.py:204
  36.1 2.6 %collective-permute-done.10.refs_4_.refs_0_ = f32[2,80,512]{2,1,0:T(8,128)S(1)} collective-permute-done((f32[2,80,512]{2,1,0:T(8,128)S(1)}, f32[2,80,512]{2,1,0:T(8,128)S(1)}, u32[]{:S(2)}, u32[]{:S(2)}) %collective-permute-start.10) | collective-permute-done | bytes 327712 | tf_op jit(solution)/shard_map/ppermute | solution.py:47
  38.7 1.2 %collective-permute-start.12 = (f32[2,80,512]{2,1,0:T(8,128)S(1)}, f32[2,80,512]{2,1,0:T(8,128)S(1)}, u32[]{:S(2)}, u32[]{:S(2)}) collective-permute-start(f32[2,80,512]{2,1,0:T(8,128)S(1)} %collective-permute-done.10.refs_4_.refs_0_), channel_id=1, source_target_pairs={{0,1},{1,0},{2,3},{3,2},{4,5},{5,4},{6,7},{7,6},{8,9},{9,8},{10,11... | collective-permute-start | bytes 983048 | tf_op jit(solution)/shard_map/ppermute | solution.py:41
  39.9 3.0 %collective-permute-done.11.refs_5_.refs_1_ = f32[2,48,512]{2,1,0:T(8,128)S(1)} collective-permute-done((f32[2,48,512]{2,1,0:T(8,128)S(1)}, f32[2,48,512]{2,1,0:T(8,128)S(1)}, u32[]{:S(2)}, u32[]{:S(2)}) %collective-permute-start.11) | collective-permute-done | bytes 196640 | tf_op jit(solution)/shard_map/ppermute | solution.py:47
  42.9 1.2 %collective-permute-start.13 = (f32[2,48,512]{2,1,0:T(8,128)S(1)}, f32[2,48,512]{2,1,0:T(8,128)S(1)}, u32[]{:S(2)}, u32[]{:S(2)}) collective-permute-start(f32[2,48,512]{2,1,0:T(8,128)S(1)} %collective-permute-done.11.refs_5_.refs_1_), channel_id=1, source_target_pairs={{0,1},{1,0},{2,3},{3,2},{4,5},{5,4},{6,7},{7,6},{8,9},{9,8},{10,11... | collective-permute-start | bytes 589832 | tf_op jit(solution)/shard_map/ppermute | solution.py:41
  47.4 1.4 %adjoint.10 = (f32[2,2,64,512]{3,2,1,0:T(8,128)S(1)}, f32[2,2,64,512]{3,2,1,0:T(8,128)S(1)}) custom-call(s32[1]{0:T(128)} %bitcast.me.ready, bf16[1024,512]{1,0:T(8,128)(2,1)S(1)} %copy-done, bf16[1024,512]{1,0:T(8,128)(2,1)S(1)} %bitcast.30, bf16[2,512,512]{2,1,0:T(8,128)(2,1)S(1)} %bitcast.27, f32[2,2,64,512]{3,2,1,0:T(8,128)S(1)} %adjoint.9.ready), custom_call_target="tpu_custom_call" | custom-call | flops 1073741824 | bytes 4194304 | tf_op jit(solution)/shard_map/adjoint/pallas_call | solution.py:103
  49.1 1.6 %collective-permute-start.19 = (f32[1,2,64,512]{3,2,1,0:T(8,128)S(1)}, f32[1,2,64,512]{3,2,1,0:T(8,128)S(1)}, u32[]{:S(2)}, u32[]{:S(2)}) collective-permute-start(f32[1,2,64,512]{3,2,1,0:T(8,128)S(1)} %get-tuple-element.51), channel_id=1, source_target_pairs={{0,2},{1,5},{2,0},{3,7},{4,6},{5,1},{6,4},{7,3},{8,10},{9,13},{10,... | collective-permute-start | bytes 786440 | tf_op jit(solution)/shard_map/ppermute | solution.py:47
  50.9 1.6 %collective-permute-start.14 = (f32[2,72,512]{2,1,0:T(8,128)S(1)}, f32[2,72,512]{2,1,0:T(8,128)S(1)}, u32[]{:S(2)}, u32[]{:S(2)}) collective-permute-start(f32[2,72,512]{2,1,0:T(8,128)S(1)} %get-tuple-element.42), channel_id=1, source_target_pairs={{0,8},{8,16},{16,24},{24,0},{1,9},{9,17},{17,25},{25,1},{2,10},{10... | collective-permute-start | bytes 884744 | tf_op jit(solution)/shard_map/ppermute | solution.py:400
  52.5 1.4 %collective-permute-start.15 = (f32[2,72,512]{2,1,0:T(8,128)S(1)}, f32[2,72,512]{2,1,0:T(8,128)S(1)}, u32[]{:S(2)}, u32[]{:S(2)}) collective-permute-start(f32[2,72,512]{2,1,0:T(8,128)S(1)} %get-tuple-element.43), channel_id=1, source_target_pairs={{8,0},{16,8},{24,16},{0,24},{9,1},{17,9},{25,17},{1,25},{10,2},{18... | collective-permute-start | bytes 884744 | tf_op jit(solution)/shard_map/ppermute | solution.py:401
  55.4 3.0 %collective-permute-done.19 = f32[1,2,64,512]{3,2,1,0:T(8,128)S(1)} collective-permute-done((f32[1,2,64,512]{3,2,1,0:T(8,128)S(1)}, f32[1,2,64,512]{3,2,1,0:T(8,128)S(1)}, u32[]{:S(2)}, u32[]{:S(2)}) %collective-permute-start.19) | collective-permute-done | bytes 262176 | tf_op jit(solution)/shard_map/ppermute | solution.py:47
  58.4 1.7 %collective-permute-start.20 = (f32[1,2,64,512]{3,2,1,0:T(8,128)S(1)}, f32[1,2,64,512]{3,2,1,0:T(8,128)S(1)}, u32[]{:S(2)}, u32[]{:S(2)}) collective-permute-start(f32[1,2,64,512]{3,2,1,0:T(8,128)S(1)} %get-tuple-element.49), channel_id=1, source_target_pairs={{0,4},{1,3},{2,6},{3,1},{4,0},{5,7},{6,2},{7,5},{8,12},{9,11},{10,... | collective-permute-start | bytes 786440 | tf_op jit(solution)/shard_map/ppermute | solution.py:47
  60.1 1.7 %collective-permute-done.14.before = f32[2,72,512]{2,1,0:T(8,128)S(1)} collective-permute-done((f32[2,72,512]{2,1,0:T(8,128)S(1)}, f32[2,72,512]{2,1,0:T(8,128)S(1)}, u32[]{:S(2)}, u32[]{:S(2)}) %collective-permute-start.14) | collective-permute-done | bytes 294944 | tf_op jit(solution)/shard_map/ppermute | solution.py:400
  61.8 6.0 %collective-permute-done.15.after = f32[2,72,512]{2,1,0:T(8,128)S(1)} collective-permute-done((f32[2,72,512]{2,1,0:T(8,128)S(1)}, f32[2,72,512]{2,1,0:T(8,128)S(1)}, u32[]{:S(2)}, u32[]{:S(2)}) %collective-permute-start.15) | collective-permute-done | bytes 294944 | tf_op jit(solution)/shard_map/ppermute | solution.py:401
  (49 shorter events, 13.7 us)
Async XLA Ops:
  0.0 1.5 %copy-start.2 = (bf16[1,1,2,512,512]{4,3,2,1,0:T(8,128)(2,1)S(1)}, bf16[1,1,2,512,512]{4,3,2,1,0:T(8,128)(2,1)}, u32[]{:S(2)}) copy-start(bf16[1,1,2,512,512]{4,3,2,1,0:T(8,128)(2,1)} %param.4) | copy-start | bytes 3145732
  0.0 1.9 %copy-start = (bf16[1024,512]{1,0:T(8,128)(2,1)S(1)}, bf16[1024,512]{1,0:T(8,128)(2,1)}, u32[]{:S(2)}) copy-start(bf16[1024,512]{1,0:T(8,128)(2,1)} %constant.8.clone.table) | copy-start | bytes 3145732
  0.0 2.2 %copy-start.1 = (bf16[1,1,2,512,512]{4,3,2,1,0:T(8,128)(2,1)S(1)}, bf16[1,1,2,512,512]{4,3,2,1,0:T(8,128)(2,1)}, u32[]{:S(2)}) copy-start(bf16[1,1,2,512,512]{4,3,2,1,0:T(8,128)(2,1)} %param.5) | copy-start | bytes 3145732
  2.8 1.9 %collective-permute-start = (f32[1,2,80,512]{3,2,1,0:T(8,128)S(1)}, f32[1,2,80,512]{3,2,1,0:T(8,128)S(1)}, u32[]{:S(2)}, u32[]{:S(2)}) collective-permute-start(f32[1,2,80,512]{3,2,1,0:T(8,128)S(1)} %adjoint.6.ready), channel_id=1, source_target_pairs={{0,1},{1,0},{2,3},{3,2},{4,5},{5,4},{6,7},{7,6},{8,9},{9,8},{10,11... | collective-permute-start | bytes 983048 | tf_op jit(solution)/shard_map/ppermute | solution.py:41
  4.8 6.9 %collective-permute-start.1 = (f32[1,2,80,512]{3,2,1,0:T(8,128)S(1)}, f32[1,2,80,512]{3,2,1,0:T(8,128)S(1)}, u32[]{:S(2)}, u32[]{:S(2)}) collective-permute-start(f32[1,2,80,512]{3,2,1,0:T(8,128)S(1)} %get-tuple-element.30), channel_id=1, source_target_pairs={{0,1},{1,0},{2,3},{3,2},{4,5},{5,4},{6,7},{7,6},{8,9},{9,8},{10,11... | collective-permute-start | bytes 983048 | tf_op jit(solution)/shard_map/ppermute | solution.py:41
  5.1 11.0 %collective-permute-start.2 = (f32[1,2,80,512]{3,2,1,0:T(8,128)S(1)}, f32[1,2,80,512]{3,2,1,0:T(8,128)S(1)}, u32[]{:S(2)}, u32[]{:S(2)}) collective-permute-start(f32[1,2,80,512]{3,2,1,0:T(8,128)S(1)} %add.33), channel_id=1, source_target_pairs={{0,2},{1,5},{2,0},{3,7},{4,6},{5,1},{6,4},{7,3},{8,10},{9,13},{10,... | collective-permute-start | bytes 983048 | tf_op jit(solution)/shard_map/ppermute | solution.py:47
  8.0 2.1 %collective-permute-start.6 = (f32[1,2,48,512]{3,2,1,0:T(8,128)S(1)}, f32[1,2,48,512]{3,2,1,0:T(8,128)S(1)}, u32[]{:S(2)}, u32[]{:S(2)}) collective-permute-start(f32[1,2,48,512]{3,2,1,0:T(8,128)S(1)} %get-tuple-element.36), channel_id=1, source_target_pairs={{0,1},{1,0},{2,3},{3,2},{4,5},{5,4},{6,7},{7,6},{8,9},{9,8},{10,11... | collective-permute-start | bytes 589832 | tf_op jit(solution)/shard_map/ppermute | solution.py:41
  10.0 9.7 %collective-permute-start.5 = (f32[1,2,48,512]{3,2,1,0:T(8,128)S(1)}, f32[1,2,48,512]{3,2,1,0:T(8,128)S(1)}, u32[]{:S(2)}, u32[]{:S(2)}) collective-permute-start(f32[1,2,48,512]{3,2,1,0:T(8,128)S(1)} %get-tuple-element.33), channel_id=1, source_target_pairs={{0,1},{1,0},{2,3},{3,2},{4,5},{5,4},{6,7},{7,6},{8,9},{9,8},{10,11... | collective-permute-start | bytes 589832 | tf_op jit(solution)/shard_map/ppermute | solution.py:41
  10.1 10.9 %collective-permute-start.7 = (f32[1,2,48,512]{3,2,1,0:T(8,128)S(1)}, f32[1,2,48,512]{3,2,1,0:T(8,128)S(1)}, u32[]{:S(2)}, u32[]{:S(2)}) collective-permute-start(f32[1,2,48,512]{3,2,1,0:T(8,128)S(1)} %add.38), channel_id=1, source_target_pairs={{0,2},{1,5},{2,0},{3,7},{4,6},{5,1},{6,4},{7,3},{8,10},{9,13},{10,... | collective-permute-start | bytes 589832 | tf_op jit(solution)/shard_map/ppermute | solution.py:47
  16.2 11.7 %collective-permute-start.3 = (f32[2,80,512]{2,1,0:T(8,128)S(1)}, f32[2,80,512]{2,1,0:T(8,128)S(1)}, u32[]{:S(2)}, u32[]{:S(2)}) collective-permute-start(f32[2,80,512]{2,1,0:T(8,128)S(1)} %add_bitcast_fusion), channel_id=1, source_target_pairs={{0,4},{1,3},{2,6},{3,1},{4,0},{5,7},{6,2},{7,5},{8,12},{9,11},{10,... | collective-permute-start | bytes 983048 | tf_op jit(solution)/shard_map/ppermute | solution.py:47
  21.1 10.4 %collective-permute-start.8 = (f32[2,48,512]{2,1,0:T(8,128)S(1)}, f32[2,48,512]{2,1,0:T(8,128)S(1)}, u32[]{:S(2)}, u32[]{:S(2)}) collective-permute-start(f32[2,48,512]{2,1,0:T(8,128)S(1)} %add_bitcast_fusion.1), channel_id=1, source_target_pairs={{0,4},{1,3},{2,6},{3,1},{4,0},{5,7},{6,2},{7,5},{8,12},{9,11},{10,... | collective-permute-start | bytes 589832 | tf_op jit(solution)/shard_map/ppermute | solution.py:47
  27.9 6.9 %collective-permute-start.4 = (f32[2,80,512]{2,1,0:T(8,128)S(1)}, f32[2,80,512]{2,1,0:T(8,128)S(1)}, u32[]{:S(2)}, u32[]{:S(2)}) collective-permute-start(f32[2,80,512]{2,1,0:T(8,128)S(1)} %add.36.refs_0_), channel_id=1, source_target_pairs={{0,1},{1,0},{2,3},{3,2},{4,5},{5,4},{6,7},{7,6},{8,9},{9,8},{10,11... | collective-permute-start | bytes 983048 | tf_op jit(solution)/shard_map/ppermute | solution.py:41
  28.8 9.9 %collective-permute-start.10 = (f32[2,80,512]{2,1,0:T(8,128)S(1)}, f32[2,80,512]{2,1,0:T(8,128)S(1)}, u32[]{:S(2)}, u32[]{:S(2)}) collective-permute-start(f32[2,80,512]{2,1,0:T(8,128)S(1)} %add.36.refs_0_), channel_id=1, source_target_pairs={{0,2},{1,5},{2,0},{3,7},{4,6},{5,1},{6,4},{7,3},{8,10},{9,13},{10,... | collective-permute-start | bytes 983048 | tf_op jit(solution)/shard_map/ppermute | solution.py:47
  31.5 3.2 %collective-permute-start.9 = (f32[2,48,512]{2,1,0:T(8,128)S(1)}, f32[2,48,512]{2,1,0:T(8,128)S(1)}, u32[]{:S(2)}, u32[]{:S(2)}) collective-permute-start(f32[2,48,512]{2,1,0:T(8,128)S(1)} %add.40.refs_2_), channel_id=1, source_target_pairs={{0,1},{1,0},{2,3},{3,2},{4,5},{5,4},{6,7},{7,6},{8,9},{9,8},{10,11... | collective-permute-start | bytes 589832 | tf_op jit(solution)/shard_map/ppermute | solution.py:41
  32.2 10.7 %collective-permute-start.11 = (f32[2,48,512]{2,1,0:T(8,128)S(1)}, f32[2,48,512]{2,1,0:T(8,128)S(1)}, u32[]{:S(2)}, u32[]{:S(2)}) collective-permute-start(f32[2,48,512]{2,1,0:T(8,128)S(1)} %add.40.refs_2_), channel_id=1, source_target_pairs={{0,2},{1,5},{2,0},{3,7},{4,6},{5,1},{6,4},{7,3},{8,10},{9,13},{10,... | collective-permute-start | bytes 589832 | tf_op jit(solution)/shard_map/ppermute | solution.py:47
  38.7 6.5 %collective-permute-start.12 = (f32[2,80,512]{2,1,0:T(8,128)S(1)}, f32[2,80,512]{2,1,0:T(8,128)S(1)}, u32[]{:S(2)}, u32[]{:S(2)}) collective-permute-start(f32[2,80,512]{2,1,0:T(8,128)S(1)} %collective-permute-done.10.refs_4_.refs_0_), channel_id=1, source_target_pairs={{0,1},{1,0},{2,3},{3,2},{4,5},{5,4},{6,7},{7,6},{8,9},{9,8},{10,11... | collective-permute-start | bytes 983048 | tf_op jit(solution)/shard_map/ppermute | solution.py:41
  42.9 2.3 %collective-permute-start.13 = (f32[2,48,512]{2,1,0:T(8,128)S(1)}, f32[2,48,512]{2,1,0:T(8,128)S(1)}, u32[]{:S(2)}, u32[]{:S(2)}) collective-permute-start(f32[2,48,512]{2,1,0:T(8,128)S(1)} %collective-permute-done.11.refs_5_.refs_1_), channel_id=1, source_target_pairs={{0,1},{1,0},{2,3},{3,2},{4,5},{5,4},{6,7},{7,6},{8,9},{9,8},{10,11... | collective-permute-start | bytes 589832 | tf_op jit(solution)/shard_map/ppermute | solution.py:41
  46.9 2.0 %collective-permute-start.17 = (f32[2,2,64,512]{3,2,1,0:T(8,128)S(1)}, f32[2,2,64,512]{3,2,1,0:T(8,128)S(1)}, u32[]{:S(2)}, u32[]{:S(2)}) collective-permute-start(f32[2,2,64,512]{3,2,1,0:T(8,128)S(1)} %adjoint.9.ready), channel_id=1, source_target_pairs={{0,1},{1,0},{2,3},{3,2},{4,5},{5,4},{6,7},{7,6},{8,9},{9,8},{10,11... | collective-permute-start | bytes 1572872 | tf_op jit(solution)/shard_map/ppermute | solution.py:41
  48.8 6.5 %collective-permute-start.16 = (f32[2,2,64,512]{3,2,1,0:T(8,128)S(1)}, f32[2,2,64,512]{3,2,1,0:T(8,128)S(1)}, u32[]{:S(2)}, u32[]{:S(2)}) collective-permute-start(f32[2,2,64,512]{3,2,1,0:T(8,128)S(1)} %get-tuple-element.48), channel_id=1, source_target_pairs={{0,1},{1,0},{2,3},{3,2},{4,5},{5,4},{6,7},{7,6},{8,9},{9,8},{10,11... | collective-permute-start | bytes 1572872 | tf_op jit(solution)/shard_map/ppermute | solution.py:41
  49.1 9.2 %collective-permute-start.19 = (f32[1,2,64,512]{3,2,1,0:T(8,128)S(1)}, f32[1,2,64,512]{3,2,1,0:T(8,128)S(1)}, u32[]{:S(2)}, u32[]{:S(2)}) collective-permute-start(f32[1,2,64,512]{3,2,1,0:T(8,128)S(1)} %get-tuple-element.51), channel_id=1, source_target_pairs={{0,2},{1,5},{2,0},{3,7},{4,6},{5,1},{6,4},{7,3},{8,10},{9,13},{10,... | collective-permute-start | bytes 786440 | tf_op jit(solution)/shard_map/ppermute | solution.py:47
  50.9 10.8 %collective-permute-start.14 = (f32[2,72,512]{2,1,0:T(8,128)S(1)}, f32[2,72,512]{2,1,0:T(8,128)S(1)}, u32[]{:S(2)}, u32[]{:S(2)}) collective-permute-start(f32[2,72,512]{2,1,0:T(8,128)S(1)} %get-tuple-element.42), channel_id=1, source_target_pairs={{0,8},{8,16},{16,24},{24,0},{1,9},{9,17},{17,25},{25,1},{2,10},{10... | collective-permute-start | bytes 884744 | tf_op jit(solution)/shard_map/ppermute | solution.py:400
  52.5 15.3 %collective-permute-start.15 = (f32[2,72,512]{2,1,0:T(8,128)S(1)}, f32[2,72,512]{2,1,0:T(8,128)S(1)}, u32[]{:S(2)}, u32[]{:S(2)}) collective-permute-start(f32[2,72,512]{2,1,0:T(8,128)S(1)} %get-tuple-element.43), channel_id=1, source_target_pairs={{8,0},{16,8},{24,16},{0,24},{9,1},{17,9},{25,17},{1,25},{10,2},{18... | collective-permute-start | bytes 884744 | tf_op jit(solution)/shard_map/ppermute | solution.py:401
  54.7 13.1 %collective-permute-start.18 = (f32[1,2,64,512]{3,2,1,0:T(8,128)S(1)}, f32[1,2,64,512]{3,2,1,0:T(8,128)S(1)}, u32[]{:S(2)}, u32[]{:S(2)}) collective-permute-start(f32[1,2,64,512]{3,2,1,0:T(8,128)S(1)} %get-tuple-element.52), channel_id=1, source_target_pairs={{0,2},{1,5},{2,0},{3,7},{4,6},{5,1},{6,4},{7,3},{8,10},{9,13},{10,... | collective-permute-start | bytes 786440 | tf_op jit(solution)/shard_map/ppermute | solution.py:47
  58.4 10.2 %collective-permute-start.20 = (f32[1,2,64,512]{3,2,1,0:T(8,128)S(1)}, f32[1,2,64,512]{3,2,1,0:T(8,128)S(1)}, u32[]{:S(2)}, u32[]{:S(2)}) collective-permute-start(f32[1,2,64,512]{3,2,1,0:T(8,128)S(1)} %get-tuple-element.49), channel_id=1, source_target_pairs={{0,4},{1,3},{2,6},{3,1},{4,0},{5,7},{6,2},{7,5},{8,12},{9,11},{10,... | collective-permute-start | bytes 786440 | tf_op jit(solution)/shard_map/ppermute | solution.py:47

commit v7 on v6

--- a/solution.py
+++ b/solution.py
@@ -119,7 +119,7 @@
     for groups in plan:
         results = adjoint([blocks for _, _, blocks in groups], me, table, data, sens, ready)
         terms.update(((name, flip), value) for (name, flip, _), value in zip(groups, results))
-        ready = results[0]
+        del results
     names = [name for name, flip in terms if flip]
     sums = {}
     for name in names:

time: 69.9 us -> 69.9 us (level)
  no operation moved by 1% of the time
where the time goes in v7:
time: 69.9 us; the launch traced here: 69.3 us
  starting transfers between devices  27.9 us (40%)
  waiting for transfers between devices  27.6 us (39%)
  Pallas kernels  10.3 us (15%)
  other arithmetic  2.93 us (4%)
    ppermute x9, waiting for transfers between devices, swap_chips(): lax.ppermute(value, 'coil', [(i, i ^ 1 << orders[i & 1][step]) for i in r...  19.6 us
    ppermute x9, starting transfers between devices, swap_chips(): lax.ppermute(value, 'coil', [(i, i ^ 1 << orders[i & 1][step]) for i in r...  18.8 us
    pallas_call x6, Pallas kernels, adjoint(): pl.pallas_call(partial(adjoint_kernel, groups), out_shape=[jax.ShapeDtype...  6.14 us
    ppermute x10, starting transfers between devices, swap_cores(): return lax.ppermute(value, 'coil', [(i, i ^ 1) for i in range(count)])  6.13 us
    ppermute x1, waiting for transfers between devices, shards(): after = lax.ppermute(to_before, 'slab', behind)  6.04 us
    pallas_call x3, Pallas kernels, forward(): pl.pallas_call(partial(forward_kernel, blocks, stage), out_shape=resid if...  3.11 us
    mul x2, other arithmetic, shards(): measured = kspace * mask[None]  1.71 us
    ppermute x1, waiting for transfers between devices, shards(): before = lax.ppermute(to_after, 'slab', ahead)  1.67 us
  transfers between devices with their start and end apart: 21, of which 11 were waited for; matrix products, arithmetic and copies ran while one was open for 1% of the time, Pallas kernels for 11%

profile of v7, /device:TPU:0, one launch (start us, length us, event | category | flops | bytes accessed | tf_op | source)
XLA Modules:
  0.0 69.3 jit_solution(6160011767248668384)
XLA Ops:
  0.0 1.5 %convert_bitcast_fusion.refs_3_ = bf16[512,512]{1,0:T(8,128)(2,1)S(1)} fusion(s32[1,512,512]{2,1,0:T(8,128)} %param.6), kind=kLoop, calls=%fused_computation.1 | loop fusion | flops 262144 | bytes 1572864 | tf_op jit(solution)/shard_map/mul | solution.py:288
  3.3 1.4 %adjoint.7 = (f32[1,2,80,512]{3,2,1,0:T(8,128)S(1)}, f32[1,2,48,512]{3,2,1,0:T(8,128)S(1)}, f32[1,2,80,512]{3,2,1,0:T(8,128)S(1)}, f32[1,2,48,512]{3,2,1,0:T(8,128)S(1)}) custom-call(s32[1]{0:T(128)} %bitcast.me.ready, bf16[1024,512]{1,0:T(8,128)(2,1)S(1)} %copy-done, bf16[1024,512]{1,0:T(8,128)(2,1)S(1)} %bitcast_multiply_fusion.data, ...), custom_call_target="tpu_custom_call" | custom-call | flops 1073741824 | bytes 4194304 | tf_op jit(solution)/shard_map/adjoint/pallas_call | solution.py:103
  5.1 2.9 %collective-permute-start.2 = (f32[1,2,80,512]{3,2,1,0:T(8,128)S(1)}, f32[1,2,80,512]{3,2,1,0:T(8,128)S(1)}, u32[]{:S(2)}, u32[]{:S(2)}) collective-permute-start(f32[1,2,80,512]{3,2,1,0:T(8,128)S(1)} %add.33), channel_id=1, source_target_pairs={{0,2},{1,5},{2,0},{3,7},{4,6},{5,1},{6,4},{7,3},{8,10},{9,13},{10,... | collective-permute-start | bytes 983048 | tf_op jit(solution)/shard_map/ppermute | solution.py:47
  10.1 1.6 %collective-permute-start.7 = (f32[1,2,48,512]{3,2,1,0:T(8,128)S(1)}, f32[1,2,48,512]{3,2,1,0:T(8,128)S(1)}, u32[]{:S(2)}, u32[]{:S(2)}) collective-permute-start(f32[1,2,48,512]{3,2,1,0:T(8,128)S(1)} %add.38), channel_id=1, source_target_pairs={{0,2},{1,5},{2,0},{3,7},{4,6},{5,1},{6,4},{7,3},{8,10},{9,13},{10,... | collective-permute-start | bytes 589832 | tf_op jit(solution)/shard_map/ppermute | solution.py:47
  11.7 4.4 %collective-permute-done.2 = f32[1,2,80,512]{3,2,1,0:T(8,128)S(1)} collective-permute-done((f32[1,2,80,512]{3,2,1,0:T(8,128)S(1)}, f32[1,2,80,512]{3,2,1,0:T(8,128)S(1)}, u32[]{:S(2)}, u32[]{:S(2)}) %collective-permute-start.2) | collective-permute-done | bytes 327712 | tf_op jit(solution)/shard_map/ppermute | solution.py:47
  16.2 3.5 %collective-permute-start.3 = (f32[2,80,512]{2,1,0:T(8,128)S(1)}, f32[2,80,512]{2,1,0:T(8,128)S(1)}, u32[]{:S(2)}, u32[]{:S(2)}) collective-permute-start(f32[2,80,512]{2,1,0:T(8,128)S(1)} %add_bitcast_fusion), channel_id=1, source_target_pairs={{0,4},{1,3},{2,6},{3,1},{4,0},{5,7},{6,2},{7,5},{8,12},{9,11},{10,... | collective-permute-start | bytes 983048 | tf_op jit(solution)/shard_map/ppermute | solution.py:47
  19.7 1.3 %collective-permute-done.7 = f32[1,2,48,512]{3,2,1,0:T(8,128)S(1)} collective-permute-done((f32[1,2,48,512]{3,2,1,0:T(8,128)S(1)}, f32[1,2,48,512]{3,2,1,0:T(8,128)S(1)}, u32[]{:S(2)}, u32[]{:S(2)}) %collective-permute-start.7) | collective-permute-done | bytes 196640 | tf_op jit(solution)/shard_map/ppermute | solution.py:47
  21.1 2.5 %collective-permute-start.8 = (f32[2,48,512]{2,1,0:T(8,128)S(1)}, f32[2,48,512]{2,1,0:T(8,128)S(1)}, u32[]{:S(2)}, u32[]{:S(2)}) collective-permute-start(f32[2,48,512]{2,1,0:T(8,128)S(1)} %add_bitcast_fusion.1), channel_id=1, source_target_pairs={{0,4},{1,3},{2,6},{3,1},{4,0},{5,7},{6,2},{7,5},{8,12},{9,11},{10,... | collective-permute-start | bytes 589832 | tf_op jit(solution)/shard_map/ppermute | solution.py:47
  23.6 4.3 %collective-permute-done.3 = f32[2,80,512]{2,1,0:T(8,128)S(1)} collective-permute-done((f32[2,80,512]{2,1,0:T(8,128)S(1)}, f32[2,80,512]{2,1,0:T(8,128)S(1)}, u32[]{:S(2)}, u32[]{:S(2)}) %collective-permute-start.3) | collective-permute-done | bytes 327712 | tf_op jit(solution)/shard_map/ppermute | solution.py:47
  28.8 1.9 %collective-permute-start.10 = (f32[2,80,512]{2,1,0:T(8,128)S(1)}, f32[2,80,512]{2,1,0:T(8,128)S(1)}, u32[]{:S(2)}, u32[]{:S(2)}) collective-permute-start(f32[2,80,512]{2,1,0:T(8,128)S(1)} %add.36.refs_0_), channel_id=1, source_target_pairs={{0,2},{1,5},{2,0},{3,7},{4,6},{5,1},{6,4},{7,3},{8,10},{9,13},{10,... | collective-permute-start | bytes 983048 | tf_op jit(solution)/shard_map/ppermute | solution.py:47
  32.2 2.5 %collective-permute-start.11 = (f32[2,48,512]{2,1,0:T(8,128)S(1)}, f32[2,48,512]{2,1,0:T(8,128)S(1)}, u32[]{:S(2)}, u32[]{:S(2)}) collective-permute-start(f32[2,48,512]{2,1,0:T(8,128)S(1)} %add.40.refs_2_), channel_id=1, source_target_pairs={{0,2},{1,5},{2,0},{3,7},{4,6},{5,1},{6,4},{7,3},{8,10},{9,13},{10,... | collective-permute-start | bytes 589832 | tf_op jit(solution)/shard_map/ppermute | solution.py:47
  34.8 1.4 %forward.3.refs_2_ = f32[512,1024]{1,0:T(8,128)S(1)} custom-call(s32[1]{0:T(128)} %bitcast.me.ready, bf16[1024,512]{1,0:T(8,128)(2,1)S(1)} %copy-done, bf16[512,512]{1,0:T(8,128)(2,1)S(1)} %get-tuple-element.37.left, bf16[2,512,512]{2,1,0:T(8,128)(2,1)S(1)} %bitcast.23, f32[2,80,512]{2,1,0:T(8,128)S(1)} %add.36.refs_0_, ...), custom_call_target="tpu_custom_call" | custom-call | flops 1073741824 | bytes 4194304 | tf_op jit(solution)/shard_map/forward/pallas_call | solution.py:204
  36.1 2.6 %collective-permute-done.10.refs_4_.refs_0_ = f32[2,80,512]{2,1,0:T(8,128)S(1)} collective-permute-done((f32[2,80,512]{2,1,0:T(8,128)S(1)}, f32[2,80,512]{2,1,0:T(8,128)S(1)}, u32[]{:S(2)}, u32[]{:S(2)}) %collective-permute-start.10) | collective-permute-done | bytes 327712 | tf_op jit(solution)/shard_map/ppermute | solution.py:47
  38.7 1.2 %collective-permute-start.12 = (f32[2,80,512]{2,1,0:T(8,128)S(1)}, f32[2,80,512]{2,1,0:T(8,128)S(1)}, u32[]{:S(2)}, u32[]{:S(2)}) collective-permute-start(f32[2,80,512]{2,1,0:T(8,128)S(1)} %collective-permute-done.10.refs_4_.refs_0_), channel_id=1, source_target_pairs={{0,1},{1,0},{2,3},{3,2},{4,5},{5,4},{6,7},{7,6},{8,9},{9,8},{10,11... | collective-permute-start | bytes 983048 | tf_op jit(solution)/shard_map/ppermute | solution.py:41
  39.9 3.0 %collective-permute-done.11.refs_5_.refs_1_ = f32[2,48,512]{2,1,0:T(8,128)S(1)} collective-permute-done((f32[2,48,512]{2,1,0:T(8,128)S(1)}, f32[2,48,512]{2,1,0:T(8,128)S(1)}, u32[]{:S(2)}, u32[]{:S(2)}) %collective-permute-start.11) | collective-permute-done | bytes 196640 | tf_op jit(solution)/shard_map/ppermute | solution.py:47
  42.9 1.2 %collective-permute-start.13 = (f32[2,48,512]{2,1,0:T(8,128)S(1)}, f32[2,48,512]{2,1,0:T(8,128)S(1)}, u32[]{:S(2)}, u32[]{:S(2)}) collective-permute-start(f32[2,48,512]{2,1,0:T(8,128)S(1)} %collective-permute-done.11.refs_5_.refs_1_), channel_id=1, source_target_pairs={{0,1},{1,0},{2,3},{3,2},{4,5},{5,4},{6,7},{7,6},{8,9},{9,8},{10,11... | collective-permute-start | bytes 589832 | tf_op jit(solution)/shard_map/ppermute | solution.py:41
  47.4 1.4 %adjoint.10 = (f32[2,2,64,512]{3,2,1,0:T(8,128)S(1)}, f32[2,2,64,512]{3,2,1,0:T(8,128)S(1)}) custom-call(s32[1]{0:T(128)} %bitcast.me.ready, bf16[1024,512]{1,0:T(8,128)(2,1)S(1)} %copy-done, bf16[1024,512]{1,0:T(8,128)(2,1)S(1)} %bitcast.30, bf16[2,512,512]{2,1,0:T(8,128)(2,1)S(1)} %bitcast.27, s32[1]{0:T(128)} %bitcast.me.ready), custom_call_target="tpu_custom_call" | custom-call | flops 1073741824 | bytes 4194304 | tf_op jit(solution)/shard_map/adjoint/pallas_call | solution.py:103
  49.1 1.6 %collective-permute-start.19 = (f32[1,2,64,512]{3,2,1,0:T(8,128)S(1)}, f32[1,2,64,512]{3,2,1,0:T(8,128)S(1)}, u32[]{:S(2)}, u32[]{:S(2)}) collective-permute-start(f32[1,2,64,512]{3,2,1,0:T(8,128)S(1)} %get-tuple-element.51), channel_id=1, source_target_pairs={{0,2},{1,5},{2,0},{3,7},{4,6},{5,1},{6,4},{7,3},{8,10},{9,13},{10,... | collective-permute-start | bytes 786440 | tf_op jit(solution)/shard_map/ppermute | solution.py:47
  50.9 1.6 %collective-permute-start.14 = (f32[2,72,512]{2,1,0:T(8,128)S(1)}, f32[2,72,512]{2,1,0:T(8,128)S(1)}, u32[]{:S(2)}, u32[]{:S(2)}) collective-permute-start(f32[2,72,512]{2,1,0:T(8,128)S(1)} %get-tuple-element.42), channel_id=1, source_target_pairs={{0,8},{8,16},{16,24},{24,0},{1,9},{9,17},{17,25},{25,1},{2,10},{10... | collective-permute-start | bytes 884744 | tf_op jit(solution)/shard_map/ppermute | solution.py:400
  52.5 1.4 %collective-permute-start.15 = (f32[2,72,512]{2,1,0:T(8,128)S(1)}, f32[2,72,512]{2,1,0:T(8,128)S(1)}, u32[]{:S(2)}, u32[]{:S(2)}) collective-permute-start(f32[2,72,512]{2,1,0:T(8,128)S(1)} %get-tuple-element.43), channel_id=1, source_target_pairs={{8,0},{16,8},{24,16},{0,24},{9,1},{17,9},{25,17},{1,25},{10,2},{18... | collective-permute-start | bytes 884744 | tf_op jit(solution)/shard_map/ppermute | solution.py:401
  55.4 3.0 %collective-permute-done.19 = f32[1,2,64,512]{3,2,1,0:T(8,128)S(1)} collective-permute-done((f32[1,2,64,512]{3,2,1,0:T(8,128)S(1)}, f32[1,2,64,512]{3,2,1,0:T(8,128)S(1)}, u32[]{:S(2)}, u32[]{:S(2)}) %collective-permute-start.19) | collective-permute-done | bytes 262176 | tf_op jit(solution)/shard_map/ppermute | solution.py:47
  58.4 1.7 %collective-permute-start.20 = (f32[1,2,64,512]{3,2,1,0:T(8,128)S(1)}, f32[1,2,64,512]{3,2,1,0:T(8,128)S(1)}, u32[]{:S(2)}, u32[]{:S(2)}) collective-permute-start(f32[1,2,64,512]{3,2,1,0:T(8,128)S(1)} %get-tuple-element.49), channel_id=1, source_target_pairs={{0,4},{1,3},{2,6},{3,1},{4,0},{5,7},{6,2},{7,5},{8,12},{9,11},{10,... | collective-permute-start | bytes 786440 | tf_op jit(solution)/shard_map/ppermute | solution.py:47
  60.1 1.7 %collective-permute-done.14.before = f32[2,72,512]{2,1,0:T(8,128)S(1)} collective-permute-done((f32[2,72,512]{2,1,0:T(8,128)S(1)}, f32[2,72,512]{2,1,0:T(8,128)S(1)}, u32[]{:S(2)}, u32[]{:S(2)}) %collective-permute-start.14) | collective-permute-done | bytes 294944 | tf_op jit(solution)/shard_map/ppermute | solution.py:400
  61.8 6.0 %collective-permute-done.15.after = f32[2,72,512]{2,1,0:T(8,128)S(1)} collective-permute-done((f32[2,72,512]{2,1,0:T(8,128)S(1)}, f32[2,72,512]{2,1,0:T(8,128)S(1)}, u32[]{:S(2)}, u32[]{:S(2)}) %collective-permute-start.15) | collective-permute-done | bytes 294944 | tf_op jit(solution)/shard_map/ppermute | solution.py:401
  (49 shorter events, 13.7 us)
Async XLA Ops:
  0.0 1.5 %copy-start.2 = (bf16[1,1,2,512,512]{4,3,2,1,0:T(8,128)(2,1)S(1)}, bf16[1,1,2,512,512]{4,3,2,1,0:T(8,128)(2,1)}, u32[]{:S(2)}) copy-start(bf16[1,1,2,512,512]{4,3,2,1,0:T(8,128)(2,1)} %param.4) | copy-start | bytes 3145732
  0.0 1.9 %copy-start = (bf16[1024,512]{1,0:T(8,128)(2,1)S(1)}, bf16[1024,512]{1,0:T(8,128)(2,1)}, u32[]{:S(2)}) copy-start(bf16[1024,512]{1,0:T(8,128)(2,1)} %constant.8.clone.table) | copy-start | bytes 3145732
  0.0 2.2 %copy-start.1 = (bf16[1,1,2,512,512]{4,3,2,1,0:T(8,128)(2,1)S(1)}, bf16[1,1,2,512,512]{4,3,2,1,0:T(8,128)(2,1)}, u32[]{:S(2)}) copy-start(bf16[1,1,2,512,512]{4,3,2,1,0:T(8,128)(2,1)} %param.5) | copy-start | bytes 3145732
  2.8 1.9 %collective-permute-start = (f32[1,2,80,512]{3,2,1,0:T(8,128)S(1)}, f32[1,2,80,512]{3,2,1,0:T(8,128)S(1)}, u32[]{:S(2)}, u32[]{:S(2)}) collective-permute-start(f32[1,2,80,512]{3,2,1,0:T(8,128)S(1)} %adjoint.8), channel_id=1, source_target_pairs={{0,1},{1,0},{2,3},{3,2},{4,5},{5,4},{6,7},{7,6},{8,9},{9,8},{10,11... | collective-permute-start | bytes 983048 | tf_op jit(solution)/shard_map/ppermute | solution.py:41
  4.8 6.9 %collective-permute-start.1 = (f32[1,2,80,512]{3,2,1,0:T(8,128)S(1)}, f32[1,2,80,512]{3,2,1,0:T(8,128)S(1)}, u32[]{:S(2)}, u32[]{:S(2)}) collective-permute-start(f32[1,2,80,512]{3,2,1,0:T(8,128)S(1)} %get-tuple-element.30), channel_id=1, source_target_pairs={{0,1},{1,0},{2,3},{3,2},{4,5},{5,4},{6,7},{7,6},{8,9},{9,8},{10,11... | collective-permute-start | bytes 983048 | tf_op jit(solution)/shard_map/ppermute | solution.py:41
  5.1 11.0 %collective-permute-start.2 = (f32[1,2,80,512]{3,2,1,0:T(8,128)S(1)}, f32[1,2,80,512]{3,2,1,0:T(8,128)S(1)}, u32[]{:S(2)}, u32[]{:S(2)}) collective-permute-start(f32[1,2,80,512]{3,2,1,0:T(8,128)S(1)} %add.33), channel_id=1, source_target_pairs={{0,2},{1,5},{2,0},{3,7},{4,6},{5,1},{6,4},{7,3},{8,10},{9,13},{10,... | collective-permute-start | bytes 983048 | tf_op jit(solution)/shard_map/ppermute | solution.py:47
  8.0 2.1 %collective-permute-start.6 = (f32[1,2,48,512]{3,2,1,0:T(8,128)S(1)}, f32[1,2,48,512]{3,2,1,0:T(8,128)S(1)}, u32[]{:S(2)}, u32[]{:S(2)}) collective-permute-start(f32[1,2,48,512]{3,2,1,0:T(8,128)S(1)} %get-tuple-element.36), channel_id=1, source_target_pairs={{0,1},{1,0},{2,3},{3,2},{4,5},{5,4},{6,7},{7,6},{8,9},{9,8},{10,11... | collective-permute-start | bytes 589832 | tf_op jit(solution)/shard_map/ppermute | solution.py:41
  10.0 9.7 %collective-permute-start.5 = (f32[1,2,48,512]{3,2,1,0:T(8,128)S(1)}, f32[1,2,48,512]{3,2,1,0:T(8,128)S(1)}, u32[]{:S(2)}, u32[]{:S(2)}) collective-permute-start(f32[1,2,48,512]{3,2,1,0:T(8,128)S(1)} %get-tuple-element.33), channel_id=1, source_target_pairs={{0,1},{1,0},{2,3},{3,2},{4,5},{5,4},{6,7},{7,6},{8,9},{9,8},{10,11... | collective-permute-start | bytes 589832 | tf_op jit(solution)/shard_map/ppermute | solution.py:41
  10.1 10.9 %collective-permute-start.7 = (f32[1,2,48,512]{3,2,1,0:T(8,128)S(1)}, f32[1,2,48,512]{3,2,1,0:T(8,128)S(1)}, u32[]{:S(2)}, u32[]{:S(2)}) collective-permute-start(f32[1,2,48,512]{3,2,1,0:T(8,128)S(1)} %add.38), channel_id=1, source_target_pairs={{0,2},{1,5},{2,0},{3,7},{4,6},{5,1},{6,4},{7,3},{8,10},{9,13},{10,... | collective-permute-start | bytes 589832 | tf_op jit(solution)/shard_map/ppermute | solution.py:47
  16.2 11.7 %collective-permute-start.3 = (f32[2,80,512]{2,1,0:T(8,128)S(1)}, f32[2,80,512]{2,1,0:T(8,128)S(1)}, u32[]{:S(2)}, u32[]{:S(2)}) collective-permute-start(f32[2,80,512]{2,1,0:T(8,128)S(1)} %add_bitcast_fusion), channel_id=1, source_target_pairs={{0,4},{1,3},{2,6},{3,1},{4,0},{5,7},{6,2},{7,5},{8,12},{9,11},{10,... | collective-permute-start | bytes 983048 | tf_op jit(solution)/shard_map/ppermute | solution.py:47
  21.1 10.4 %collective-permute-start.8 = (f32[2,48,512]{2,1,0:T(8,128)S(1)}, f32[2,48,512]{2,1,0:T(8,128)S(1)}, u32[]{:S(2)}, u32[]{:S(2)}) collective-permute-start(f32[2,48,512]{2,1,0:T(8,128)S(1)} %add_bitcast_fusion.1), channel_id=1, source_target_pairs={{0,4},{1,3},{2,6},{3,1},{4,0},{5,7},{6,2},{7,5},{8,12},{9,11},{10,... | collective-permute-start | bytes 589832 | tf_op jit(solution)/shard_map/ppermute | solution.py:47
  27.9 6.9 %collective-permute-start.4 = (f32[2,80,512]{2,1,0:T(8,128)S(1)}, f32[2,80,512]{2,1,0:T(8,128)S(1)}, u32[]{:S(2)}, u32[]{:S(2)}) collective-permute-start(f32[2,80,512]{2,1,0:T(8,128)S(1)} %add.36.refs_0_), channel_id=1, source_target_pairs={{0,1},{1,0},{2,3},{3,2},{4,5},{5,4},{6,7},{7,6},{8,9},{9,8},{10,11... | collective-permute-start | bytes 983048 | tf_op jit(solution)/shard_map/ppermute | solution.py:41
  28.8 9.9 %collective-permute-start.10 = (f32[2,80,512]{2,1,0:T(8,128)S(1)}, f32[2,80,512]{2,1,0:T(8,128)S(1)}, u32[]{:S(2)}, u32[]{:S(2)}) collective-permute-start(f32[2,80,512]{2,1,0:T(8,128)S(1)} %add.36.refs_0_), channel_id=1, source_target_pairs={{0,2},{1,5},{2,0},{3,7},{4,6},{5,1},{6,4},{7,3},{8,10},{9,13},{10,... | collective-permute-start | bytes 983048 | tf_op jit(solution)/shard_map/ppermute | solution.py:47
  31.5 3.2 %collective-permute-start.9 = (f32[2,48,512]{2,1,0:T(8,128)S(1)}, f32[2,48,512]{2,1,0:T(8,128)S(1)}, u32[]{:S(2)}, u32[]{:S(2)}) collective-permute-start(f32[2,48,512]{2,1,0:T(8,128)S(1)} %add.40.refs_2_), channel_id=1, source_target_pairs={{0,1},{1,0},{2,3},{3,2},{4,5},{5,4},{6,7},{7,6},{8,9},{9,8},{10,11... | collective-permute-start | bytes 589832 | tf_op jit(solution)/shard_map/ppermute | solution.py:41
  32.2 10.7 %collective-permute-start.11 = (f32[2,48,512]{2,1,0:T(8,128)S(1)}, f32[2,48,512]{2,1,0:T(8,128)S(1)}, u32[]{:S(2)}, u32[]{:S(2)}) collective-permute-start(f32[2,48,512]{2,1,0:T(8,128)S(1)} %add.40.refs_2_), channel_id=1, source_target_pairs={{0,2},{1,5},{2,0},{3,7},{4,6},{5,1},{6,4},{7,3},{8,10},{9,13},{10,... | collective-permute-start | bytes 589832 | tf_op jit(solution)/shard_map/ppermute | solution.py:47
  38.7 6.5 %collective-permute-start.12 = (f32[2,80,512]{2,1,0:T(8,128)S(1)}, f32[2,80,512]{2,1,0:T(8,128)S(1)}, u32[]{:S(2)}, u32[]{:S(2)}) collective-permute-start(f32[2,80,512]{2,1,0:T(8,128)S(1)} %collective-permute-done.10.refs_4_.refs_0_), channel_id=1, source_target_pairs={{0,1},{1,0},{2,3},{3,2},{4,5},{5,4},{6,7},{7,6},{8,9},{9,8},{10,11... | collective-permute-start | bytes 983048 | tf_op jit(solution)/shard_map/ppermute | solution.py:41
  42.9 2.3 %collective-permute-start.13 = (f32[2,48,512]{2,1,0:T(8,128)S(1)}, f32[2,48,512]{2,1,0:T(8,128)S(1)}, u32[]{:S(2)}, u32[]{:S(2)}) collective-permute-start(f32[2,48,512]{2,1,0:T(8,128)S(1)} %collective-permute-done.11.refs_5_.refs_1_), channel_id=1, source_target_pairs={{0,1},{1,0},{2,3},{3,2},{4,5},{5,4},{6,7},{7,6},{8,9},{9,8},{10,11... | collective-permute-start | bytes 589832 | tf_op jit(solution)/shard_map/ppermute | solution.py:41
  46.9 2.0 %collective-permute-start.17 = (f32[2,2,64,512]{3,2,1,0:T(8,128)S(1)}, f32[2,2,64,512]{3,2,1,0:T(8,128)S(1)}, u32[]{:S(2)}, u32[]{:S(2)}) collective-permute-start(f32[2,2,64,512]{3,2,1,0:T(8,128)S(1)} %adjoint.11), channel_id=1, source_target_pairs={{0,1},{1,0},{2,3},{3,2},{4,5},{5,4},{6,7},{7,6},{8,9},{9,8},{10,11... | collective-permute-start | bytes 1572872 | tf_op jit(solution)/shard_map/ppermute | solution.py:41
  48.8 6.5 %collective-permute-start.16 = (f32[2,2,64,512]{3,2,1,0:T(8,128)S(1)}, f32[2,2,64,512]{3,2,1,0:T(8,128)S(1)}, u32[]{:S(2)}, u32[]{:S(2)}) collective-permute-start(f32[2,2,64,512]{3,2,1,0:T(8,128)S(1)} %get-tuple-element.47), channel_id=1, source_target_pairs={{0,1},{1,0},{2,3},{3,2},{4,5},{5,4},{6,7},{7,6},{8,9},{9,8},{10,11... | collective-permute-start | bytes 1572872 | tf_op jit(solution)/shard_map/ppermute | solution.py:41
  49.1 9.2 %collective-permute-start.19 = (f32[1,2,64,512]{3,2,1,0:T(8,128)S(1)}, f32[1,2,64,512]{3,2,1,0:T(8,128)S(1)}, u32[]{:S(2)}, u32[]{:S(2)}) collective-permute-start(f32[1,2,64,512]{3,2,1,0:T(8,128)S(1)} %get-tuple-element.51), channel_id=1, source_target_pairs={{0,2},{1,5},{2,0},{3,7},{4,6},{5,1},{6,4},{7,3},{8,10},{9,13},{10,... | collective-permute-start | bytes 786440 | tf_op jit(solution)/shard_map/ppermute | solution.py:47
  50.9 10.8 %collective-permute-start.14 = (f32[2,72,512]{2,1,0:T(8,128)S(1)}, f32[2,72,512]{2,1,0:T(8,128)S(1)}, u32[]{:S(2)}, u32[]{:S(2)}) collective-permute-start(f32[2,72,512]{2,1,0:T(8,128)S(1)} %get-tuple-element.42), channel_id=1, source_target_pairs={{0,8},{8,16},{16,24},{24,0},{1,9},{9,17},{17,25},{25,1},{2,10},{10... | collective-permute-start | bytes 884744 | tf_op jit(solution)/shard_map/ppermute | solution.py:400
  52.5 15.3 %collective-permute-start.15 = (f32[2,72,512]{2,1,0:T(8,128)S(1)}, f32[2,72,512]{2,1,0:T(8,128)S(1)}, u32[]{:S(2)}, u32[]{:S(2)}) collective-permute-start(f32[2,72,512]{2,1,0:T(8,128)S(1)} %get-tuple-element.43), channel_id=1, source_target_pairs={{8,0},{16,8},{24,16},{0,24},{9,1},{17,9},{25,17},{1,25},{10,2},{18... | collective-permute-start | bytes 884744 | tf_op jit(solution)/shard_map/ppermute | solution.py:401
  54.7 13.1 %collective-permute-start.18 = (f32[1,2,64,512]{3,2,1,0:T(8,128)S(1)}, f32[1,2,64,512]{3,2,1,0:T(8,128)S(1)}, u32[]{:S(2)}, u32[]{:S(2)}) collective-permute-start(f32[1,2,64,512]{3,2,1,0:T(8,128)S(1)} %get-tuple-element.52), channel_id=1, source_target_pairs={{0,2},{1,5},{2,0},{3,7},{4,6},{5,1},{6,4},{7,3},{8,10},{9,13},{10,... | collective-permute-start | bytes 786440 | tf_op jit(solution)/shard_map/ppermute | solution.py:47
  58.4 10.2 %collective-permute-start.20 = (f32[1,2,64,512]{3,2,1,0:T(8,128)S(1)}, f32[1,2,64,512]{3,2,1,0:T(8,128)S(1)}, u32[]{:S(2)}, u32[]{:S(2)}) collective-permute-start(f32[1,2,64,512]{3,2,1,0:T(8,128)S(1)} %get-tuple-element.49), channel_id=1, source_target_pairs={{0,4},{1,3},{2,6},{3,1},{4,0},{5,7},{6,2},{7,5},{8,12},{9,11},{10,... | collective-permute-start | bytes 786440 | tf_op jit(solution)/shard_map/ppermute | solution.py:47
